TPU v7x, 128 devices: a whole 4x4x4 slice. The times are simulated.
128 devices in a mesh: pair: 32 (over z, y, x_hi), rows: 4 (over x_lo, core).
Axes of the slice: x: 4 (x_hi: 2, x_lo: 2; x = x_hi * 2 + x_lo), y: 4, z: 4, core: 2. Of those that a mesh axis runs over, the one named last changes fastest.
Arguments:
- matrix: float32 [16384, 16384], P('rows', 'pair')
Outputs:
- rotated: float32 [16384, 16384], P('rows', 'pair')
All inputs are finite; a program needn't handle non-finite values.
Results may differ from a plain program's by a relative error of at most 0.00016.
Values sent between devices are 32-bit elements; how exact they have to be, the bound alone decides.
No kernel may reach another device: no remote copies, remote signals or barrier semaphores. Data moves between devices by JAX's collectives and lax.ppermute only.
A program may use at most 128 MiB of HBM per device.

v0:
```python
import jax
import jax.numpy as jnp
from jax import lax
from jax.sharding import PartitionSpec as P

B = 64
PD = 4
ROUNDS = 3
NS_STEPS = 8


EPS = 1e-06


def passed_along(x, axis, by):
    peers = lax.axis_size(axis)
    pairs = [(i, i + by) for i in range(peers) if 0 <= i + by < peers]
    return lax.ppermute(x, axis, pairs)


def rotation_factors(gram):
    diag = jnp.diagonal(gram, axis1=-2, axis2=-1)
    norms = jnp.sqrt(diag + EPS)
    corr = gram / (norms[..., :, None] * norms[..., None, :])
    upper = jnp.triu(corr, 1)
    skew = 0.5 * (jnp.swapaxes(upper, -1, -2) - upper)
    total = jnp.sum(skew * skew, axis=(-2, -1), keepdims=True)
    eye = jnp.eye(gram.shape[-1], dtype=jnp.float32)
    current = (eye + skew) / jnp.sqrt(1.0 + total)
    for step in range(NS_STEPS):
        inner = jnp.einsum("pki,pkj->pij", current, current, precision=lax.Precision.HIGHEST)
        current = 1.5 * current - 0.5 * jnp.einsum(
            "pik,pkj->pij", current, inner, precision=lax.Precision.HIGHEST
        )
    return current


def rotate(blocks, factors):
    return jnp.einsum("rpi,pij->rpj", blocks, factors, precision=lax.Precision.HIGHEST)


def carry_ends(last_top, first_bottom):
    incoming_top = passed_along(last_top, "pair", 1)
    incoming_bottom = passed_along(first_bottom, "pair", -1)
    return (incoming_top, incoming_bottom)


def body(matrix):
    row_count = matrix.shape[0]
    width = 2 * B
    blocks = matrix.reshape(row_count, PD, width)
    index = lax.axis_index("pair")
    last_index = lax.axis_size("pair") - 1
    for step in range(ROUNDS):
        partial_gram = jnp.einsum("rpi,rpj->pij", blocks, blocks, precision=lax.Precision.HIGHEST)
        factors = rotation_factors(lax.psum(partial_gram, "rows"))
        rotated_pairs = rotate(blocks, factors)
        incoming_top, incoming_bottom = carry_ends(
            rotated_pairs[:, PD - 1, :B], rotated_pairs[:, 0, B:]
        )
        tops = rotated_pairs[:, :, :B]
        bottoms = rotated_pairs[:, :, B:]
        shifted_tops = jnp.concatenate([incoming_top[:, None, :], tops[:, : PD - 1]], axis=1)
        fixed_tops = jnp.concatenate([tops[:, :1], bottoms[:, :1], tops[:, 1 : PD - 1]], axis=1)
        new_tops = jnp.where(index == 0, fixed_tops, shifted_tops)
        shifted_bottoms = jnp.concatenate([bottoms[:, 1:], incoming_bottom[:, None, :]], axis=1)
        fixed_bottoms = jnp.concatenate([bottoms[:, 1:], tops[:, PD - 1 :]], axis=1)
        new_bottoms = jnp.where(index == last_index, fixed_bottoms, shifted_bottoms)
        blocks = jnp.concatenate([new_tops, new_bottoms], axis=2)
    return blocks.reshape(row_count, PD * width)


def solution(mesh):
    in_specs = (P("rows", "pair"),)
    out_specs = P("rows", "pair")
    return jax.shard_map(body, mesh=mesh, in_specs=in_specs, out_specs=out_specs, check_vma=False)
```

profile of v0, /device:TPU:96, one launch (start us, length us, event | category | flops | bytes accessed | tf_op | source)
XLA Modules:
  0.0 433.1 jit_solution(16303647504692332158)
XLA Ops:
  6.5 20.0 %fusion.2 = f32[4,128,128]{2,1,0:T(8,128)} fusion(f32[4096,512]{1,0:T(8,128)} %param.1), kind=kOutput, calls=%fused_computation.5 | convolution fusion | flops 3221225472 | bytes 8650752 | tf_op jit(solution)/shard_map/rpi,rpj->pij/dot_general | solution.py:55
  26.8 37.1 %all-reduce.4.cloned.1.call-done = f32[4,128,128]{2,1,0:T(8,128)} async-done(((f32[4,128,128]{2,1,0:T(8,128)}), f32[4,128,128]{2,1,0:T(8,128)}) %all-reduce.4.cloned.1.call-update) | async-done | bytes 262160 | tf_op jit(solution)/shard_map/psum | solution.py:56
  64.0 5.8 %copy.4 = f32[4,128,128]{0,2,1:T(8,128)} copy(f32[4,128,128]{2,1,0:T(8,128)} %all-reduce.4.cloned.1.call-done) | data formatting | bytes 524288 | tf_op jit(solution)/shard_map/psum | solution.py:56
  69.7 1.9 gather_fusion
  72.2 0.7 fusion.50
  80.5 10.9 %fusion.12 = f32[4096,4,128]{0,2,1:T(8,128)S(1)} fusion(f32[4,128,128]{2,1,0:T(8,128)S(1)} %fusion.34, f32[4096,512]{1,0:T(8,128)} %param.1), kind=kOutput, calls=%fused_computation.18 | convolution fusion | flops 3221225472 | bytes 17039360 | tf_op jit(solution)/shard_map/rpi,pij->rpj/dot_general | solution.py:39
  92.0 4.6 %collective-permute-start = (f32[4096,64]{0,1:T(8,128)S(1)}, f32[4096,64]{0,1:T(8,128)S(1)}, u32[]{:S(2)}, u32[]{:S(2)}) collective-permute-start(f32[4096,64]{0,1:T(8,128)S(1)} %get-tuple-element.19), channel_id=1, source_target_pairs={{0,4},{4,8},{8,12},{12,16},{16,20},{20,24},{24,28},{28,32},{32,36}... | collective-permute-start | bytes 3145736 | tf_op jit(solution)/shard_map/ppermute | solution.py:18
  96.6 5.8 %collective-permute-start.1 = (f32[4096,64]{0,1:T(8,128)S(1)}, f32[4096,64]{0,1:T(8,128)S(1)}, u32[]{:S(2)}, u32[]{:S(2)}) collective-permute-start(f32[4096,64]{0,1:T(8,128)S(1)} %get-tuple-element.20), channel_id=1, source_target_pairs={{4,0},{8,4},{12,8},{16,12},{20,16},{24,20},{28,24},{32,28},{36,32}... | collective-permute-start | bytes 3145736 | tf_op jit(solution)/shard_map/ppermute | solution.py:18
  103.3 40.9 %collective-permute-done.1 = f32[4096,64]{0,1:T(8,128)S(1)} collective-permute-done((f32[4096,64]{0,1:T(8,128)S(1)}, f32[4096,64]{0,1:T(8,128)S(1)}, u32[]{:S(2)}, u32[]{:S(2)}) %collective-permute-start.1) | collective-permute-done | bytes 1048608 | tf_op jit(solution)/shard_map/ppermute | solution.py:18
  144.2 2.3 fusion.17
  146.5 2.5 maximum_select_fusion
  149.0 14.3 %fusion.9 = f32[4,128,128]{2,1,0:T(8,128)} fusion(f32[4096,4,64]{0,2,1:T(8,128)} %fusion.17, f32[4096,4,64]{0,2,1:T(8,128)} %maximum_select_fusion), kind=kOutput, calls=%fused_computation.15 | convolution fusion | flops 3223322624 | bytes 8650752 | tf_op jit(solution)/shard_map/rpi,rpj->pij/dot_general | solution.py:55
  163.3 36.7 %all-reduce.6.cloned.1.call-done = f32[4,128,128]{2,1,0:T(8,128)} async-done(((f32[4,128,128]{2,1,0:T(8,128)}), f32[4,128,128]{2,1,0:T(8,128)}) %all-reduce.6.cloned.1.call-update) | async-done | bytes 262160 | tf_op jit(solution)/shard_map/psum | solution.py:56
  200.0 5.9 %copy.11 = f32[4,128,128]{0,2,1:T(8,128)} copy(f32[4,128,128]{2,1,0:T(8,128)} %all-reduce.6.cloned.1.call-done) | data formatting | bytes 524288 | tf_op jit(solution)/shard_map/psum | solution.py:56
  206.0 1.9 gather_fusion.1
  208.5 0.7 fusion.51
  216.8 8.8 %fusion.10 = f32[4096,4,128]{0,2,1:T(8,128)S(1)} fusion(f32[4,128,128]{2,1,0:T(8,128)S(1)} %fusion.26, f32[4096,4,64]{0,2,1:T(8,128)S(1)} %copy-done.1, f32[4096,4,64]{0,2,1:T(8,128)S(1)} %copy-done.3), kind=kOutput, calls=%fused_computation.16 | convolution fusion | flops 3223322624 | bytes 17039360 | tf_op jit(solution)/shard_map/rpi,pij->rpj/dot_general | solution.py:39
  226.2 4.6 %collective-permute-start.2 = (f32[4096,64]{0,1:T(8,128)S(1)}, f32[4096,64]{0,1:T(8,128)S(1)}, u32[]{:S(2)}, u32[]{:S(2)}) collective-permute-start(f32[4096,64]{0,1:T(8,128)S(1)} %get-tuple-element.12), channel_id=1, source_target_pairs={{0,4},{4,8},{8,12},{12,16},{16,20},{20,24},{24,28},{28,32},{32,36}... | collective-permute-start | bytes 3145736 | tf_op jit(solution)/shard_map/ppermute | solution.py:18
  230.8 5.8 %collective-permute-start.3 = (f32[4096,64]{0,1:T(8,128)S(1)}, f32[4096,64]{0,1:T(8,128)S(1)}, u32[]{:S(2)}, u32[]{:S(2)}) collective-permute-start(f32[4096,64]{0,1:T(8,128)S(1)} %get-tuple-element.13), channel_id=1, source_target_pairs={{4,0},{8,4},{12,8},{16,12},{20,16},{24,20},{28,24},{32,28},{36,32}... | collective-permute-start | bytes 3145736 | tf_op jit(solution)/shard_map/ppermute | solution.py:18
  237.4 40.9 %collective-permute-done.3 = f32[4096,64]{0,1:T(8,128)S(1)} collective-permute-done((f32[4096,64]{0,1:T(8,128)S(1)}, f32[4096,64]{0,1:T(8,128)S(1)}, u32[]{:S(2)}, u32[]{:S(2)}) %collective-permute-start.3) | collective-permute-done | bytes 1048608 | tf_op jit(solution)/shard_map/ppermute | solution.py:18
  278.3 2.4 fusion.16
  280.7 2.6 maximum_select_fusion.1
  283.3 14.3 %fusion.7 = f32[4,128,128]{2,1,0:T(8,128)} fusion(f32[4096,4,64]{0,2,1:T(8,128)} %fusion.16, f32[4096,4,64]{0,2,1:T(8,128)} %maximum_select_fusion.1), kind=kOutput, calls=%fused_computation.13 | convolution fusion | flops 3223322624 | bytes 8650752 | tf_op jit(solution)/shard_map/rpi,rpj->pij/dot_general | solution.py:55
  297.6 36.8 %all-reduce.8.cloned.1.call-done = f32[4,128,128]{2,1,0:T(8,128)} async-done(((f32[4,128,128]{2,1,0:T(8,128)}), f32[4,128,128]{2,1,0:T(8,128)}) %all-reduce.8.cloned.1.call-update) | async-done | bytes 262160 | tf_op jit(solution)/shard_map/psum | solution.py:56
  334.4 5.9 %copy.18 = f32[4,128,128]{0,2,1:T(8,128)} copy(f32[4,128,128]{2,1,0:T(8,128)} %all-reduce.8.cloned.1.call-done) | data formatting | bytes 524288 | tf_op jit(solution)/shard_map/psum | solution.py:56
  340.3 1.9 gather_fusion.2
  351.2 8.6 %fusion.11 = f32[4096,4,128]{0,2,1:T(8,128)S(1)} fusion(f32[4,128,128]{2,1,0:T(8,128)S(1)} %fusion.18, f32[4096,4,64]{0,2,1:T(8,128)S(1)} %copy-done, f32[4096,4,64]{0,2,1:T(8,128)S(1)} %copy-done.2), kind=kOutput, calls=%fused_computation.17 | convolution fusion | flops 3223322624 | bytes 17039360 | tf_op jit(solution)/shard_map/rpi,pij->rpj/dot_general | solution.py:39
  360.5 4.6 %collective-permute-start.4 = (f32[4096,64]{0,1:T(8,128)S(1)}, f32[4096,64]{0,1:T(8,128)S(1)}, u32[]{:S(2)}, u32[]{:S(2)}) collective-permute-start(f32[4096,64]{0,1:T(8,128)S(1)} %get-tuple-element.5), channel_id=1, source_target_pairs={{0,4},{4,8},{8,12},{12,16},{16,20},{20,24},{24,28},{28,32},{32,36}... | collective-permute-start | bytes 3145736 | tf_op jit(solution)/shard_map/ppermute | solution.py:18
  365.1 5.8 %collective-permute-start.5 = (f32[4096,64]{0,1:T(8,128)S(1)}, f32[4096,64]{0,1:T(8,128)S(1)}, u32[]{:S(2)}, u32[]{:S(2)}) collective-permute-start(f32[4096,64]{0,1:T(8,128)S(1)} %get-tuple-element.6), channel_id=1, source_target_pairs={{4,0},{8,4},{12,8},{16,12},{20,16},{24,20},{28,24},{32,28},{36,32}... | collective-permute-start | bytes 3145736 | tf_op jit(solution)/shard_map/ppermute | solution.py:18
  371.6 41.1 %collective-permute-done.5 = f32[4096,64]{0,1:T(8,128)S(1)} collective-permute-done((f32[4096,64]{0,1:T(8,128)S(1)}, f32[4096,64]{0,1:T(8,128)S(1)}, u32[]{:S(2)}, u32[]{:S(2)}) %collective-permute-start.5) | collective-permute-done | bytes 1048608 | tf_op jit(solution)/shard_map/ppermute | solution.py:18
  413.6 3.8 pad_maximum_fusion.2
  417.4 8.9 %copy.24 = f32[4096,512]{1,0:T(8,128)} copy(f32[4096,512]{0,1:T(8,128)} %bitcast.168) | data formatting | bytes 16777216 | tf_op jit(solution)/shard_map/reshape | solution.py:70
  (101 shorter events, 30.7 us)
Async XLA Ops:
  6.5 57.4 %all-reduce.4.cloned.1.call-start = ((), (), s32[]{:S(2)}) async-start(), calls=%async_computation | async-start | bytes 524288 | tf_op jit(solution)/shard_map/psum | solution.py:56
  26.5 173.5 %all-reduce.6.cloned.1.call-start = ((), (), s32[]{:S(2)}) async-start(), calls=%async_computation.1 | async-start | bytes 524288 | tf_op jit(solution)/shard_map/psum | solution.py:56
  64.0 7.7 %copy-start.5 = (f32[4,128,128]{2,1,0:T(8,128)S(1)}, f32[4,128,128]{2,1,0:T(8,128)}, u32[]{:S(2)}) copy-start(f32[4,128,128]{2,1,0:T(8,128)} %all-reduce.4.cloned.1.call-done) | copy-start | bytes 786436
  92.0 54.5 %collective-permute-start = (f32[4096,64]{0,1:T(8,128)S(1)}, f32[4096,64]{0,1:T(8,128)S(1)}, u32[]{:S(2)}, u32[]{:S(2)}) collective-permute-start(f32[4096,64]{0,1:T(8,128)S(1)} %get-tuple-element.19), channel_id=1, source_target_pairs={{0,4},{4,8},{8,12},{12,16},{16,20},{20,24},{24,28},{28,32},{32,36}... | collective-permute-start | bytes 3145736 | tf_op jit(solution)/shard_map/ppermute | solution.py:18
  96.6 47.6 %collective-permute-start.1 = (f32[4096,64]{0,1:T(8,128)S(1)}, f32[4096,64]{0,1:T(8,128)S(1)}, u32[]{:S(2)}, u32[]{:S(2)}) collective-permute-start(f32[4096,64]{0,1:T(8,128)S(1)} %get-tuple-element.20), channel_id=1, source_target_pairs={{4,0},{8,4},{12,8},{16,12},{20,16},{24,20},{28,24},{32,28},{36,32}... | collective-permute-start | bytes 3145736 | tf_op jit(solution)/shard_map/ppermute | solution.py:18
  163.3 171.1 %all-reduce.8.cloned.1.call-start = ((), (), s32[]{:S(2)}) async-start(), calls=%async_computation.2 | async-start | bytes 524288 | tf_op jit(solution)/shard_map/psum | solution.py:56
  200.0 7.9 %copy-start.6 = (f32[4,128,128]{2,1,0:T(8,128)S(1)}, f32[4,128,128]{2,1,0:T(8,128)}, u32[]{:S(2)}) copy-start(f32[4,128,128]{2,1,0:T(8,128)} %all-reduce.6.cloned.1.call-done) | copy-start | bytes 786436
  211.3 5.5 %copy-start.1 = (f32[4096,4,64]{0,2,1:T(8,128)S(1)}, f32[4096,4,64]{0,2,1:T(8,128)}, u32[]{:S(2)}) copy-start(f32[4096,4,64]{0,2,1:T(8,128)} %fusion.17) | copy-start | bytes 12582916
  211.3 5.5 %copy-start.3 = (f32[4096,4,64]{0,2,1:T(8,128)S(1)}, f32[4096,4,64]{0,2,1:T(8,128)}, u32[]{:S(2)}) copy-start(f32[4096,4,64]{0,2,1:T(8,128)} %maximum_select_fusion) | copy-start | bytes 12582916
  226.2 54.6 %collective-permute-start.2 = (f32[4096,64]{0,1:T(8,128)S(1)}, f32[4096,64]{0,1:T(8,128)S(1)}, u32[]{:S(2)}, u32[]{:S(2)}) collective-permute-start(f32[4096,64]{0,1:T(8,128)S(1)} %get-tuple-element.12), channel_id=1, source_target_pairs={{0,4},{4,8},{8,12},{12,16},{16,20},{20,24},{24,28},{28,32},{32,36}... | collective-permute-start | bytes 3145736 | tf_op jit(solution)/shard_map/ppermute | solution.py:18
  230.8 47.6 %collective-permute-start.3 = (f32[4096,64]{0,1:T(8,128)S(1)}, f32[4096,64]{0,1:T(8,128)S(1)}, u32[]{:S(2)}, u32[]{:S(2)}) collective-permute-start(f32[4096,64]{0,1:T(8,128)S(1)} %get-tuple-element.13), channel_id=1, source_target_pairs={{4,0},{8,4},{12,8},{16,12},{20,16},{24,20},{28,24},{32,28},{36,32}... | collective-permute-start | bytes 3145736 | tf_op jit(solution)/shard_map/ppermute | solution.py:18
  334.4 7.9 %copy-start.4 = (f32[4,128,128]{2,1,0:T(8,128)S(1)}, f32[4,128,128]{2,1,0:T(8,128)}, u32[]{:S(2)}) copy-start(f32[4,128,128]{2,1,0:T(8,128)} %all-reduce.8.cloned.1.call-done) | copy-start | bytes 786436
  345.6 5.5 %copy-start = (f32[4096,4,64]{0,2,1:T(8,128)S(1)}, f32[4096,4,64]{0,2,1:T(8,128)}, u32[]{:S(2)}) copy-start(f32[4096,4,64]{0,2,1:T(8,128)} %fusion.16) | copy-start | bytes 12582916
  345.6 5.5 %copy-start.2 = (f32[4096,4,64]{0,2,1:T(8,128)S(1)}, f32[4096,4,64]{0,2,1:T(8,128)}, u32[]{:S(2)}) copy-start(f32[4096,4,64]{0,2,1:T(8,128)} %maximum_select_fusion.1) | copy-start | bytes 12582916
  360.5 52.5 %collective-permute-start.4 = (f32[4096,64]{0,1:T(8,128)S(1)}, f32[4096,64]{0,1:T(8,128)S(1)}, u32[]{:S(2)}, u32[]{:S(2)}) collective-permute-start(f32[4096,64]{0,1:T(8,128)S(1)} %get-tuple-element.5), channel_id=1, source_target_pairs={{0,4},{4,8},{8,12},{12,16},{16,20},{20,24},{24,28},{28,32},{32,36}... | collective-permute-start | bytes 3145736 | tf_op jit(solution)/shard_map/ppermute | solution.py:18
  365.1 47.6 %collective-permute-start.5 = (f32[4096,64]{0,1:T(8,128)S(1)}, f32[4096,64]{0,1:T(8,128)S(1)}, u32[]{:S(2)}, u32[]{:S(2)}) collective-permute-start(f32[4096,64]{0,1:T(8,128)S(1)} %get-tuple-element.6), channel_id=1, source_target_pairs={{4,0},{8,4},{12,8},{16,12},{20,16},{24,20},{28,24},{32,28},{36,32}... | collective-permute-start | bytes 3145736 | tf_op jit(solution)/shard_map/ppermute | solution.py:18
Sparse Core Ops, SparseCore 0:
  26.6 37.2 all-reduce.3
  163.4 36.6 all-reduce.5
  297.7 36.6 all-reduce.7
where the time goes:
time: 441 us; the launch traced here: 433 us
  waiting for transfers between devices  234 us (53%)
  matrix products  101 us (23%)
  local copies, waits for them, and re-layouts  37 us (8%)
  starting transfers between devices  31.4 us (7%)
  other arithmetic  15.9 us (4%)
  between operations  14.1 us (3%)
    ppermute x6, waiting for transfers between devices, passed_along(): return lax.ppermute(x, axis, pairs)  123 us
    psum x3, waiting for transfers between devices, body(): factors = rotation_factors(lax.psum(partial_gram, 'rows'))  111 us
    dot_general x3, matrix products, body(): jnp.einsum('rpi,rpj->pij', blocks, blocks, precision=lax.Precision.HIGHEST)  48.5 us
    ppermute x6, starting transfers between devices, passed_along(): return lax.ppermute(x, axis, pairs)  31.1 us
    dot_general x3, matrix products, rotate(): jnp.einsum('rpi,pij->rpj', blocks, factors, precision=lax.Precision.HIGHEST)  28.2 us
    psum x3, local copies, waits for them, and re-layouts, body(): factors = rotation_factors(lax.psum(partial_gram, 'rows'))  17.6 us
    dot_general x24, matrix products, rotation_factors(): jnp.einsum('pki,pkj->pij', current, current, precision=lax.Precision.HIGH...  14.5 us
    dot_general x24, matrix products, rotation_factors(): jnp.einsum('pik,pkj->pij', current, inner, precision=lax.Precision.HIGHEST)  9.83 us
  transfers between devices with their start and end apart: 9, of which 6 were waited for; matrix products, arithmetic and copies ran while one was open for 2% of the time, Pallas kernels for 0%

commit v1 on v0

v1 whole, which is shorter than its diff:
```python
import functools

import jax
import jax.numpy as jnp
from jax import lax
from jax.experimental import pallas as pl
from jax.experimental.pallas import tpu as pltpu
from jax.sharding import PartitionSpec as P

B = 64
W = 128
PD = 4
NS_STEPS = 8
EPS = 1e-06
F32 = jnp.float32
BF16 = jnp.bfloat16

TINY = pl.CostEstimate(flops=1, bytes_accessed=1, transcendentals=0)

NN = (((1,), (0,)), ((), ()))
NT = (((1,), (1,)), ((), ()))
TN = (((0,), (0,)), ((), ()))


def params(mib=48):
    return pltpu.CompilerParams(vmem_limit_bytes=mib * 1024 * 1024)


def split(x):
    high = x.astype(BF16)
    return high, (x - high.astype(F32)).astype(BF16)


def dot(a, b, dims):
    return lax.dot_general(a, b, dims, preferred_element_type=F32)


def factor_stack(y):
    high, low = split(y)
    return jnp.concatenate(
        [jnp.concatenate([high, high], 1), jnp.concatenate([low, jnp.zeros_like(low)], 1)], 0
    )


def apply_rows(stack, values):
    high, low = split(values)
    both = dot(stack, jnp.concatenate([high, low], 0), NN)
    half = both.shape[0] // 2
    return both[:half] + both[half:]


def finish_gram(acc):
    cross = acc[:, W:]
    return acc[:, :W] + cross + cross.T


def gram_rows_kernel(m_ref, g_ref, acc):
    step = pl.program_id(0)

    @pl.when(step == 0)
    def _():
        acc[...] = jnp.zeros_like(acc)

    for k in range(PD):
        high, low = split(m_ref[:, k * W : (k + 1) * W])
        acc[k] += dot(high, jnp.concatenate([high, low], 1), TN)

    @pl.when(step == pl.num_programs(0) - 1)
    def _():
        for k in range(PD):
            g_ref[k] = finish_gram(acc[k])


def gram_rows(matrix, chunk=512):
    rows = matrix.shape[0]
    return pl.pallas_call(
        gram_rows_kernel,
        grid=(rows // chunk,),
        in_specs=[pl.BlockSpec((chunk, PD * W), lambda i: (i, 0))],
        out_specs=pl.BlockSpec((PD, W, W), lambda i: (0, 0, 0)),
        out_shape=jax.ShapeDtypeStruct((PD, W, W), F32),
        scratch_shapes=[pltpu.VMEM((PD, W, 2 * W), F32)],
        compiler_params=params(),
        cost_estimate=TINY,
        name="gram_rows",
    )(matrix)


def gram_blocks_kernel(n, *refs):
    acc = refs[-1]
    g_ref = refs[-2]
    step = pl.program_id(0)

    @pl.when(step == 0)
    def _():
        acc[...] = jnp.zeros_like(acc)

    for k in range(n):
        high, low = split(jnp.concatenate([refs[2 * k][...], refs[2 * k + 1][...]], 0))
        acc[k] += dot(high, jnp.concatenate([high, low], 0), NT)

    @pl.when(step == pl.num_programs(0) - 1)
    def _():
        for k in range(n):
            g_ref[k] = finish_gram(acc[k])


def gram_blocks(pairs, name, chunk=1024):
    blocks = [x for pair in pairs for x in pair]
    n = len(pairs)
    cols = blocks[0].shape[1]
    return pl.pallas_call(
        functools.partial(gram_blocks_kernel, n),
        grid=(cols // chunk,),
        in_specs=[pl.BlockSpec((B, chunk), lambda i: (0, i))] * (2 * n),
        out_specs=pl.BlockSpec((n, W, W), lambda i: (0, 0, 0)),
        out_shape=jax.ShapeDtypeStruct((n, W, W), F32),
        scratch_shapes=[pltpu.VMEM((n, W, 2 * W), F32)],
        compiler_params=params(),
        cost_estimate=TINY,
        name=name,
    )(*blocks)


def mm3(a, b, dims):
    ah, al = split(a)
    bh, bl = split(b)
    return dot(ah, bh, dims) + (dot(ah, bl, dims) + dot(al, bh, dims))


def factors_kernel(n, swapped, flags, a_ref, b_ref, y_ref):
    row = lax.broadcasted_iota(jnp.int32, (W, W), 0)
    col = lax.broadcasted_iota(jnp.int32, (W, W), 1)
    eye = row == col
    ys = []
    for k in range(n):
        g = a_ref[k] + b_ref[k]
        diag = jnp.where(eye, g, 0.0)
        norm_col = jnp.sqrt(jnp.sum(diag, axis=1, keepdims=True) + EPS)
        norm_row = jnp.sqrt(jnp.sum(diag, axis=0, keepdims=True) + EPS)
        corr = g / (norm_col * norm_row)
        skew = jnp.where(row < col, -0.5 * corr, jnp.where(row > col, 0.5 * corr, 0.0))
        total = jnp.sum(jnp.sum(skew * skew, axis=1, keepdims=True), axis=0, keepdims=True)
        ys.append((jnp.where(eye, 1.0, 0.0) - skew) / jnp.sqrt(1.0 + total))

    def step(_, ys):
        inner = [mm3(y, y, NT) for y in ys]
        return tuple(1.5 * y - 0.5 * mm3(a, y, NN) for a, y in zip(inner, ys))

    ys = lax.fori_loop(0, NS_STEPS, step, tuple(ys))
    for k in range(n):
        y = ys[k]
        if k == swapped:
            y = jnp.where(flags[0] != 0, jnp.concatenate([y[B:], y[:B]], 0), y)
        y_ref[k] = y


def factors(flags, a, b, name, swapped=0):
    n = a.shape[0]
    return pl.pallas_call(
        functools.partial(factors_kernel, n, swapped),
        in_specs=[
            pl.BlockSpec(memory_space=pltpu.SMEM),
            pl.BlockSpec(memory_space=pltpu.VMEM),
            pl.BlockSpec(memory_space=pltpu.VMEM),
        ],
        out_specs=pl.BlockSpec(memory_space=pltpu.VMEM),
        out_shape=jax.ShapeDtypeStruct((n, W, W), F32),
        compiler_params=params(),
        cost_estimate=TINY,
        name=name,
    )(flags, a, b)


def rotate_rows_kernel(y_ref, m_ref, *outs):
    for k in range(PD):
        stack = factor_stack(y_ref[k])
        high, low = split(m_ref[:, k * W : (k + 1) * W])
        both = dot(stack, jnp.concatenate([high, low], 1), NT)
        new = both[:W] + both[W:]
        outs[2 * k][...] = new[:B]
        outs[2 * k + 1][...] = new[B:]


def rotate_rows(y, matrix, chunk=512):
    rows = matrix.shape[0]
    outs = pl.pallas_call(
        rotate_rows_kernel,
        grid=(rows // chunk,),
        in_specs=[
            pl.BlockSpec((PD, W, W), lambda i: (0, 0, 0)),
            pl.BlockSpec((chunk, PD * W), lambda i: (i, 0)),
        ],
        out_specs=[pl.BlockSpec((B, chunk), lambda i: (0, i))] * (2 * PD),
        out_shape=[jax.ShapeDtypeStruct((B, rows), F32)] * (2 * PD),
        compiler_params=params(),
        cost_estimate=TINY,
        name="rotate_rows",
    )(y, matrix)
    return [outs[2 * k] for k in range(PD)], [outs[2 * k + 1] for k in range(PD)]


def rotate_blocks_kernel(n, *refs):
    y_ref = refs[0]
    ins, outs = refs[1 : 1 + 2 * n], refs[1 + 2 * n :]
    for k in range(n):
        new = apply_rows(
            factor_stack(y_ref[k]), jnp.concatenate([ins[2 * k][...], ins[2 * k + 1][...]], 0)
        )
        outs[2 * k][...] = new[:B]
        outs[2 * k + 1][...] = new[B:]


def rotate_blocks(y, pairs, name, chunk=1024):
    blocks = [x for pair in pairs for x in pair]
    n = len(pairs)
    cols = blocks[0].shape[1]
    spec = pl.BlockSpec((B, chunk), lambda i: (0, i))
    outs = pl.pallas_call(
        functools.partial(rotate_blocks_kernel, n),
        grid=(cols // chunk,),
        in_specs=[pl.BlockSpec((n, W, W), lambda i: (0, 0, 0))] + [spec] * (2 * n),
        out_specs=[spec] * (2 * n),
        out_shape=[jax.ShapeDtypeStruct((B, cols), F32)] * (2 * n),
        compiler_params=params(),
        cost_estimate=TINY,
        name=name,
    )(y, *blocks)
    return [outs[2 * k] for k in range(n)], [outs[2 * k + 1] for k in range(n)]


def rotate_ends_kernel(flags, yl_ref, yr_ref, lt, lb, rt, rb, l_edge, r_edge, left, right):
    new = apply_rows(factor_stack(yl_ref[...]), jnp.concatenate([lt[...], lb[...]], 0))
    left[...] = jnp.where(flags[0] != 0, l_edge[...], new)
    new = apply_rows(factor_stack(yr_ref[...]), jnp.concatenate([rt[...], rb[...]], 0))
    right[...] = jnp.where(flags[1] != 0, r_edge[...], new)


def rotate_ends(flags, y_left, y_right, left_pair, right_pair, edges, name, chunk=1024):
    cols = edges[0].shape[1]
    spec = pl.BlockSpec((B, chunk), lambda i: (0, i))
    half = pl.BlockSpec((B, W), lambda i: (0, 0))
    return pl.pallas_call(
        rotate_ends_kernel,
        grid=(cols // chunk,),
        in_specs=[pl.BlockSpec(memory_space=pltpu.SMEM), half, half] + [spec] * 6,
        out_specs=[spec] * 2,
        out_shape=[jax.ShapeDtypeStruct((B, cols), F32)] * 2,
        compiler_params=params(),
        cost_estimate=TINY,
        name=name,
    )(flags, y_left, y_right, *left_pair, *right_pair, *edges)


def final_kernel(flags, y_ref, yl_ref, yr_ref, *refs):
    out = refs[-1]
    values = [jnp.concatenate([refs[2 * k][...], refs[2 * k + 1][...]], 0) for k in range(PD + 2)]
    own = [
        apply_rows(factor_stack(y_ref[k]), values[k + 1]) for k in range(PD)
    ]
    left = apply_rows(factor_stack(yl_ref[...]), values[0])
    right = apply_rows(factor_stack(yr_ref[...]), values[PD + 1])
    left = jnp.where(flags[0] != 0, own[0][B:], left)
    right = jnp.where(flags[1] != 0, own[PD - 1][:B], right)
    tops = [left] + [x[:B] for x in own[: PD - 1]]
    bottoms = [x[B:] for x in own[1:]] + [right]
    for k in range(PD):
        out[:, k * W : (k + 1) * W] = jnp.concatenate([tops[k], bottoms[k]], 0).T


def final(flags, y, y_left, y_right, pairs, chunk=512):
    blocks = [x for pair in pairs for x in pair]
    cols = blocks[0].shape[1]
    spec = pl.BlockSpec((B, chunk), lambda i: (0, i))
    half = pl.BlockSpec((B, W), lambda i: (0, 0))
    return pl.pallas_call(
        final_kernel,
        grid=(cols // chunk,),
        in_specs=[
            pl.BlockSpec(memory_space=pltpu.SMEM),
            pl.BlockSpec((PD, W, W), lambda i: (0, 0, 0)),
            half,
            half,
        ]
        + [spec] * len(blocks),
        out_specs=pl.BlockSpec((chunk, PD * W), lambda i: (i, 0)),
        out_shape=jax.ShapeDtypeStruct((cols, PD * W), F32),
        compiler_params=params(),
        cost_estimate=TINY,
        name="final",
    )(flags, y, y_left, y_right, *blocks)


def send_on(x):
    peers = lax.axis_size("pair")
    return lax.ppermute(x, "pair", [(i, i + 1) for i in range(peers - 1)])


def send_back(x):
    peers = lax.axis_size("pair")
    return lax.ppermute(x, "pair", [(i + 1, i) for i in range(peers - 1)])


def row_terms(gram):
    near = gram + lax.ppermute(gram, "rows", [(i, i ^ 1) for i in range(4)])
    return near, lax.ppermute(near, "rows", [(i, i ^ 2) for i in range(4)])


def body(matrix):
    index = lax.axis_index("pair")
    last = lax.axis_size("pair") - 1
    first_one, last_one = index == 0, index == last
    flags = jnp.stack([first_one, last_one]).astype(jnp.int32)

    y1 = factors(flags, *row_terms(gram_rows(matrix)), name="factors_1")
    r1, l1 = rotate_rows(y1, matrix)

    in_left = send_on(r1[3])
    in_right = send_back(l1[0])
    in_left2 = send_on(r1[2])
    in_right2 = send_back(l1[1])

    in_left = jnp.where(first_one, l1[0], in_left)
    in_right = jnp.where(last_one, r1[3], in_right)
    inner2 = [(r1[0], l1[2]), (r1[1], l1[3])]
    outer2 = [(in_left, l1[1]), (r1[2], in_right)]
    g2_inner = gram_blocks(inner2, "gram_2_inner")
    y2_inner = factors(flags, *row_terms(g2_inner), name="factors_2_inner", swapped=-1)
    (r2_1, r2_2), (l2_1, l2_2) = rotate_blocks(y2_inner, inner2, "rotate_2_inner")
    in_left3 = send_on(r2_2)
    in_right3 = send_back(l2_1)

    g2_outer = gram_blocks(outer2, "gram_2_outer")
    y2_outer = factors(flags, *row_terms(g2_outer), name="factors_2_outer")
    y2_left = send_on(y2_outer[1, :B])
    y2_right = send_back(y2_outer[0, B:])
    (r2_0, r2_3), (l2_0, l2_3) = rotate_blocks(y2_outer, outer2, "rotate_2_outer")

    inner3 = [(r2_0, l2_2), (r2_1, l2_3)]
    g3_inner = gram_blocks(inner3, "gram_3_inner")
    y3_inner = factors(flags, *row_terms(g3_inner), name="factors_3_inner", swapped=-1)

    r2_left, l2_right = rotate_ends(
        flags, y2_left, y2_right, (in_left2, l1[0]), (r1[3], in_right2), (l2_0, r2_3), "ends_2"
    )
    outer3 = [(r2_left, l2_1), (r2_2, l2_right)]
    g3_outer = gram_blocks(outer3, "gram_3_outer")
    y3_outer = factors(flags, *row_terms(g3_outer), name="factors_3_outer")
    y3_left = send_on(y3_outer[1, :B])
    y3_right = send_back(y3_outer[0, B:])

    y3 = jnp.stack([y3_outer[0], y3_inner[0], y3_inner[1], y3_outer[1]])
    pairs = [(in_left3, l2_0), outer3[0], inner3[0], inner3[1], outer3[1], (r2_3, in_right3)]
    return final(flags, y3, y3_left, y3_right, pairs)


def solution(mesh):
    spec = P("rows", "pair")
    return jax.shard_map(body, mesh=mesh, in_specs=(spec,), out_specs=spec, check_vma=False)
```

time: 441 us -> 247 us (0.56); the launches traced: 433 us -> 245 us
  waiting for transfers between devices: 234 us -> 109 us
  matrix products: 101 us -> 0 us
  Pallas kernels: 0 us -> 72.2 us
  local copies, waits for them, and re-layouts: 37 us -> 11.4 us
  starting transfers between devices: 31.4 us -> 51.6 us
  other arithmetic: 15.9 us -> 0.46 us
  between operations: 14.1 us -> 0.49 us
    psum x3 -> x0, waiting for transfers between devices: 111 us -> none  [body(): factors = rotation_factors(lax.psum(partial_gram, 'rows'))]
    dot_general x54 -> x0, matrix products: 101 us -> none  [the longest x3 48.5 us: body(): jnp.einsum('rpi,rpj->pij', blocks, blocks, precision=lax.Precision.HIGHEST)]
    pallas_call x0 -> x15, Pallas kernels: none -> 72.2 us  [the longest x5 22.6 us: factors(): pl.pallas_call(functools.partial(factors_kernel, n, swapped), in_specs=[p...]
    ppermute x6 -> x20, starting transfers between devices: 31.1 us -> 51.6 us  [the longest x5 32.8 us: send_back(): return lax.ppermute(x, 'pair', [(i + 1, i) for i in range(peers - 1)])]
    psum x3 -> x0, local copies, waits for them, and re-layouts: 17.6 us -> none  [body(): factors = rotation_factors(lax.psum(partial_gram, 'rows'))]
    ppermute x6 -> x20, waiting for transfers between devices: 123 us -> 109 us  [the longest x5 51 us: row_terms(): return (near, lax.ppermute(near, 'rows', [(i, i ^ 2) for i in range(4)]))]
    unnamed x14 -> x40, local copies, waits for them, and re-layouts: 0.03 us -> 11.4 us
    select_n x8 -> x2, other arithmetic: 11 us -> 0.25 us  [the longest x1 0.14 us: body(): in_left = jnp.where(first_one, l1[0], in_left)]
  transfers between devices with their start and end apart: 9 -> 20, of which waited for: 6 -> 9; matrix products, arithmetic and copies ran while one was open for 2% -> 0% of each run, Pallas kernels for 0% -> 16%
where the time goes in v1:
time: 247 us; the launch traced here: 245 us
  waiting for transfers between devices  109 us (44%)
  Pallas kernels  72.2 us (29%)
  starting transfers between devices  51.6 us (21%)
  local copies, waits for them, and re-layouts  11.4 us (5%)
    ppermute x5, waiting for transfers between devices, row_terms(): return (near, lax.ppermute(near, 'rows', [(i, i ^ 2) for i in range(4)]))  51 us
    ppermute x5, starting transfers between devices, send_back(): return lax.ppermute(x, 'pair', [(i + 1, i) for i in range(peers - 1)])  32.8 us
    ppermute x5, waiting for transfers between devices, send_on(): return lax.ppermute(x, 'pair', [(i, i + 1) for i in range(peers - 1)])  31.2 us
    ppermute x5, waiting for transfers between devices, send_back(): return lax.ppermute(x, 'pair', [(i + 1, i) for i in range(peers - 1)])  25.5 us
    pallas_call x5, Pallas kernels, factors(): pl.pallas_call(functools.partial(factors_kernel, n, swapped), in_specs=[p...  22.6 us
    unnamed x40, local copies, waits for them, and re-layouts  11.4 us
    ppermute x5, starting transfers between devices, send_on(): return lax.ppermute(x, 'pair', [(i, i + 1) for i in range(peers - 1)])  11.1 us
    pallas_call x4, Pallas kernels, gram_blocks(): pl.pallas_call(functools.partial(gram_blocks_kernel, n), grid=(cols // ch...  10.9 us
  transfers between devices with their start and end apart: 20, of which 9 were waited for; matrix products, arithmetic and copies ran while one was open for 0% of the time, Pallas kernels for 16%

profile of v1, /device:TPU:96, one launch (start us, length us, event | category | flops | bytes accessed | tf_op | source)
XLA Modules:
  0.0 245.3 jit_solution(2311254962790009852)
XLA Ops:
  0.0 7.1 %gram_rows.1 = f32[4,128,128]{2,1,0:T(8,128)S(1)} custom-call(f32[4096,512]{1,0:T(8,128)} %m_ref.3), custom_call_target="tpu_custom_call" | custom-call | flops 1 | bytes 1 | tf_op jit(solution)/shard_map/gram_rows/pallas_call | solution.py:76
  10.4 6.8 %collective-permute-done.1.b_ref = f32[4,128,128]{2,1,0:T(8,128)S(1)} collective-permute-done((f32[4,128,128]{2,1,0:T(8,128)S(1)}, f32[4,128,128]{2,1,0:T(8,128)S(1)}, u32[]{:S(2)}, u32[]{:S(2)}) %collective-permute-start.1) | collective-permute-done | bytes 262176 | tf_op jit(solution)/shard_map/ppermute | solution.py:306
  17.2 5.5 %factors_1.1.y_ref = f32[4,128,128]{2,1,0:T(8,128)S(1)} custom-call(s32[2]{0:T(128)S(1)} %add_convert_fusion.flags, f32[4,128,128]{2,1,0:T(8,128)S(1)} %add.15.a_ref, f32[4,128,128]{2,1,0:T(8,128)S(1)} %collective-permute-done.1.b_ref), custom_call_target="tpu_custom_call" | custom-call | flops 1 | bytes 1 | tf_op jit(solution)/shard_map/factors_1/pallas_call | solution.py:160
  22.7 9.2 %rotate_rows.1 = (f32[64,4096]{1,0:T(8,128)S(1)}, f32[64,4096]{1,0:T(8,128)S(1)}, f32[64,4096]{1,0:T(8,128)S(1)}, f32[64,4096]{1,0:T(8,128)S(1)}, f32[64,4096]{1...) custom-call(f32[4,128,128]{2,1,0:T(8,128)S(1)} %factors_1.1.y_ref, f32[4096,512]{1,0:T(8,128)} %m_ref.3), custom_call_target="tpu_custom_call" | custom-call | flops 1 | bytes 1 | tf_op jit(solution)/shard_map/rotate_rows/pallas_call | solution.py:187
  32.0 7.2 %collective-permute-start.3 = (f32[64,4096]{1,0:T(8,128)S(1)}, f32[64,4096]{1,0:T(8,128)S(1)}, u32[]{:S(2)}, u32[]{:S(2)}) collective-permute-start(f32[64,4096]{1,0:T(8,128)S(1)} %get-tuple-element.23.lb), channel_id=1, source_target_pairs={{4,0},{8,4},{12,8},{16,12},{20,16},{24,20},{28,24},{32,28},{36,32}... | collective-permute-start | bytes 3145736 | tf_op jit(solution)/shard_map/ppermute | solution.py:301
  39.2 1.9 collective-permute-start.2
  43.6 2.4 gram_2_inner.1
  46.1 8.4 %collective-permute-start.9 = (f32[64,4096]{1,0:T(8,128)S(1)}, f32[64,4096]{1,0:T(8,128)S(1)}, u32[]{:S(2)}, u32[]{:S(2)}) collective-permute-start(f32[64,4096]{1,0:T(8,128)S(1)} %get-tuple-element.25.refs_1_.refs_2_), channel_id=1, source_target_pairs={{4,0},{8,4},{12,8},{16,12},{20,16},{24,20},{28,24},{32,28},{36,32}... | collective-permute-start | bytes 3145736 | tf_op jit(solution)/shard_map/ppermute | solution.py:301
  54.5 1.9 collective-permute-start.8
  56.5 6.3 %collective-permute-done.3 = f32[64,4096]{1,0:T(8,128)S(1)} collective-permute-done((f32[64,4096]{1,0:T(8,128)S(1)}, f32[64,4096]{1,0:T(8,128)S(1)}, u32[]{:S(2)}, u32[]{:S(2)}) %collective-permute-start.3) | collective-permute-done | bytes 1048608 | tf_op jit(solution)/shard_map/ppermute | solution.py:301
  62.9 23.3 %collective-permute-done.2 = f32[64,4096]{1,0:T(8,128)S(1)} collective-permute-done((f32[64,4096]{1,0:T(8,128)}, f32[64,4096]{1,0:T(8,128)S(1)}, u32[]{:S(2)}, u32[]{:S(2)}) %collective-permute-start.2) | collective-permute-done | bytes 1048608 | tf_op jit(solution)/shard_map/ppermute | solution.py:296
  86.4 3.7 %gram_2_outer.1 = f32[2,128,128]{2,1,0:T(8,128)S(1)} custom-call(f32[64,4096]{1,0:T(8,128)S(1)} %broadcast_select_fusion.1.refs_0_.refs_1_, f32[64,4096]{1,0:T(8,128)S(1)} %get-tuple-element.25.refs_1_.refs_2_, f32[64,4096]{1,0:T(8,128)} %get-tuple-element.26.refs_2_.refs_3_, f32[64,4096]{1,0:T(8,128)S(1)} %broadcast_select_fusion.refs_3_.refs_4_), custom_call_target="tpu_custom_call" | custom-call | flops 1 | bytes 1 | tf_op jit(solution)/shard_map/gram_2_outer/pallas_call | solution.py:112
  93.1 40.7 %collective-permute-done.11.b_ref = f32[2,128,128]{2,1,0:T(8,128)S(1)} collective-permute-done((f32[2,128,128]{2,1,0:T(8,128)S(1)}, f32[2,128,128]{2,1,0:T(8,128)S(1)}, u32[]{:S(2)}, u32[]{:S(2)}) %collective-permute-start.11) | collective-permute-done | bytes 131104 | tf_op jit(solution)/shard_map/ppermute | solution.py:306
  133.7 4.3 %factors_2_inner.1.refs_0_ = f32[2,128,128]{2,1,0:T(8,128)S(1)} custom-call(s32[2]{0:T(128)S(1)} %add_convert_fusion.flags, f32[2,128,128]{2,1,0:T(8,128)S(1)} %add.17.a_ref, f32[2,128,128]{2,1,0:T(8,128)S(1)} %collective-permute-done.11.b_ref), custom_call_target="tpu_custom_call" | custom-call | flops 1 | bytes 1 | tf_op jit(solution)/shard_map/factors_2_inner/pallas_call | solution.py:160
  138.0 4.0 %rotate_2_inner.1 = (f32[64,4096]{1,0:T(8,128)S(1)}, f32[64,4096]{1,0:T(8,128)S(1)}, f32[64,4096]{1,0:T(8,128)S(1)}, f32[64,4096]{1,0:T(8,128)S(1)}) custom-call(f32[2,128,128]{2,1,0:T(8,128)S(1)} %factors_2_inner.1.refs_0_, f32[64,4096]{1,0:T(8,128)S(1)} %get-tuple-element.30.refs_0_.refs_1_, f32[64,4096]{1,0:T(8,128)} %get-tuple-element.31.refs_1_.refs_2_, ...), custom_call_target="tpu_custom_call" | custom-call | flops 1 | bytes 1 | tf_op jit(solution)/shard_map/rotate_2_inner/pallas_call | solution.py:219
  142.0 3.9 %collective-permute-start.19 = (f32[64,4096]{1,0:T(8,128)S(1)}, f32[64,4096]{1,0:T(8,128)}, u32[]{:S(2)}, u32[]{:S(2)}) collective-permute-start(f32[64,4096]{1,0:T(8,128)S(1)} %get-tuple-element.34.refs_1_.refs_3_), channel_id=1, source_target_pairs={{4,0},{8,4},{12,8},{16,12},{20,16},{24,20},{28,24},{32,28},{36,32}... | collective-permute-start | bytes 3145736 | tf_op jit(solution)/shard_map/ppermute | solution.py:301
  145.9 3.5 %collective-permute-start.18 = (f32[64,4096]{1,0:T(8,128)S(1)}, f32[64,4096]{1,0:T(8,128)S(1)}, u32[]{:S(2)}, u32[]{:S(2)}) collective-permute-start(f32[64,4096]{1,0:T(8,128)S(1)} %get-tuple-element.35.refs_2_.refs_8_), channel_id=1, source_target_pairs={{0,4},{4,8},{8,12},{12,16},{16,20},{20,24},{24,28},{28,32},{32,36}... | collective-permute-start | bytes 3145736 | tf_op jit(solution)/shard_map/ppermute | solution.py:296
  149.4 4.3 %factors_2_outer.1.refs_0_ = f32[2,128,128]{2,1,0:T(8,128)S(1)} custom-call(s32[2]{0:T(128)S(1)} %add_convert_fusion.flags, f32[2,128,128]{2,1,0:T(8,128)S(1)} %add.16.a_ref, f32[2,128,128]{2,1,0:T(8,128)S(1)} %collective-permute-done.5.b_ref), custom_call_target="tpu_custom_call" | custom-call | flops 1 | bytes 1 | tf_op jit(solution)/shard_map/factors_2_outer/pallas_call | solution.py:160
  153.7 6.9 %collective-permute-start.7 = (f32[64,128]{1,0:T(8,128)S(1)}, f32[64,128]{1,0:T(8,128)S(1)}, u32[]{:S(2)}, u32[]{:S(2)}) collective-permute-start(f32[64,128]{1,0:T(8,128)S(1)} %get-tuple-element.45), channel_id=1, source_target_pairs={{4,0},{8,4},{12,8},{16,12},{20,16},{24,20},{28,24},{32,28},{36,32}... | collective-permute-start | bytes 98312 | tf_op jit(solution)/shard_map/ppermute | solution.py:301
  161.6 1.9 collective-permute-start.6
  163.5 4.0 %rotate_2_outer.1 = (f32[64,4096]{1,0:T(8,128)S(1)}, f32[64,4096]{1,0:T(8,128)S(1)}, f32[64,4096]{1,0:T(8,128)S(1)}, f32[64,4096]{1,0:T(8,128)S(1)}) custom-call(f32[2,128,128]{2,1,0:T(8,128)S(1)} %factors_2_outer.1.refs_0_, f32[64,4096]{1,0:T(8,128)S(1)} %broadcast_select_fusion.1.refs_0_.refs_1_, f32[64,4096]{1,0:T(8,128)} %copy-done.13, ...), custom_call_target="tpu_custom_call" | custom-call | flops 1 | bytes 1 | tf_op jit(solution)/shard_map/rotate_2_outer/pallas_call | solution.py:219
  169.4 2.4 gram_3_inner.1
  171.9 19.1 %collective-permute-done.7.yr_ref = f32[64,128]{1,0:T(8,128)S(1)} collective-permute-done((f32[64,128]{1,0:T(8,128)S(1)}, f32[64,128]{1,0:T(8,128)S(1)}, u32[]{:S(2)}, u32[]{:S(2)}) %collective-permute-start.7) | collective-permute-done | bytes 32800 | tf_op jit(solution)/shard_map/ppermute | solution.py:301
  191.6 3.7 %ends_2.1 = (f32[64,4096]{1,0:T(8,128)S(1)}, f32[64,4096]{1,0:T(8,128)S(1)}) custom-call(s32[2]{0:T(128)S(1)} %add_convert_fusion.flags, f32[64,128]{1,0:T(8,128)S(1)} %collective-permute-done.6.yl_ref, f32[64,128]{1,0:T(8,128)S(1)} %collective-permute-done.7.yr_ref, f32[64,4096]{1,0:T(8,128)} %collective-permute-done.8.lt, ...), custom_call_target="tpu_custom_call" | custom-call | flops 1 | bytes 1 | tf_op jit(solution)/shard_map/ends_2/pallas_call | solution.py:243
  197.9 2.4 gram_3_outer.1
  203.3 3.6 %collective-permute-done.15.b_ref = f32[2,128,128]{2,1,0:T(8,128)S(1)} collective-permute-done((f32[2,128,128]{2,1,0:T(8,128)S(1)}, f32[2,128,128]{2,1,0:T(8,128)S(1)}, u32[]{:S(2)}, u32[]{:S(2)}) %collective-permute-start.15) | collective-permute-done | bytes 131104 | tf_op jit(solution)/shard_map/ppermute | solution.py:306
  206.8 4.3 %factors_3_inner.1 = f32[2,128,128]{2,1,0:T(8,128)S(1)} custom-call(s32[2]{0:T(128)S(1)} %add_convert_fusion.flags, f32[2,128,128]{2,1,0:T(8,128)S(1)} %add.19.a_ref, f32[2,128,128]{2,1,0:T(8,128)S(1)} %collective-permute-done.15.b_ref), custom_call_target="tpu_custom_call" | custom-call | flops 1 | bytes 1 | tf_op jit(solution)/shard_map/factors_3_inner/pallas_call | solution.py:160
  211.1 4.3 %factors_3_outer.1 = f32[2,128,128]{2,1,0:T(8,128)S(1)} custom-call(s32[2]{0:T(128)S(1)} %add_convert_fusion.flags, f32[2,128,128]{2,1,0:T(8,128)S(1)} %add.18.a_ref, f32[2,128,128]{2,1,0:T(8,128)S(1)} %collective-permute-done.13.b_ref), custom_call_target="tpu_custom_call" | custom-call | flops 1 | bytes 1 | tf_op jit(solution)/shard_map/factors_3_outer/pallas_call | solution.py:160
  215.4 6.4 %collective-permute-start.17 = (f32[64,128]{1,0:T(8,128)S(1)}, f32[64,128]{1,0:T(8,128)S(1)}, u32[]{:S(2)}, u32[]{:S(2)}) collective-permute-start(f32[64,128]{1,0:T(8,128)S(1)} %get-tuple-element.41), channel_id=1, source_target_pairs={{4,0},{8,4},{12,8},{16,12},{20,16},{24,20},{28,24},{32,28},{36,32}... | collective-permute-start | bytes 98312 | tf_op jit(solution)/shard_map/ppermute | solution.py:301
  221.8 1.9 collective-permute-start.16
  224.8 7.3 %collective-permute-done.16.yl_ref = f32[64,128]{1,0:T(8,128)S(1)} collective-permute-done((f32[64,128]{1,0:T(8,128)S(1)}, f32[64,128]{1,0:T(8,128)S(1)}, u32[]{:S(2)}, u32[]{:S(2)}) %collective-permute-start.16) | collective-permute-done | bytes 32800 | tf_op jit(solution)/shard_map/ppermute | solution.py:296
  234.6 10.8 %final.1 = f32[4096,512]{1,0:T(8,128)} custom-call(s32[2]{0:T(128)S(1)} %add_convert_fusion.flags, f32[4,128,128]{2,1,0:T(8,128)S(1)} %pad_maximum_fusion.y_ref, f32[64,128]{1,0:T(8,128)S(1)} %collective-permute-done.16.yl_ref, f32[64,128]{1,0:T(8,128)S(1)} %collective-permute-done.17.yr_ref, f32[64,4096]{1,0:T(8,128)S(1)} %copy-done.18, ...), custom_call_target="tpu_custom_call" | custom-call | flops 1 | bytes 1 | tf_op jit(solution)/shard_map/final/pallas_call | solution.py:276
  (75 shorter events, 21.6 us)
Async XLA Ops:
  7.1 1.6 collective-permute-start
  8.8 8.4 %collective-permute-start.1 = (f32[4,128,128]{2,1,0:T(8,128)S(1)}, f32[4,128,128]{2,1,0:T(8,128)S(1)}, u32[]{:S(2)}, u32[]{:S(2)}) collective-permute-start(f32[4,128,128]{2,1,0:T(8,128)S(1)} %add.15.a_ref), channel_id=1, source_target_pairs={{0,2},{1,3},{2,0},{3,1},{4,6},{5,7},{6,4},{7,5},{8,10},{9,11},{10,... | collective-permute-start | bytes 786440 | tf_op jit(solution)/shard_map/ppermute | solution.py:306
  32.0 30.9 %copy-start.14 = (f32[64,4096]{1,0:T(8,128)}, f32[64,4096]{1,0:T(8,128)S(1)}, u32[]{:S(2)}) copy-start(f32[64,4096]{1,0:T(8,128)S(1)} %get-tuple-element.32.refs_2_.refs_3_) | copy-start | bytes 3145732
  32.0 110.0 %copy-start.13 = (f32[64,4096]{1,0:T(8,128)}, f32[64,4096]{1,0:T(8,128)S(1)}, u32[]{:S(2)}) copy-start(f32[64,4096]{1,0:T(8,128)S(1)} %get-tuple-element.25.refs_1_.refs_2_) | copy-start | bytes 3145732
  32.0 30.8 %collective-permute-start.3 = (f32[64,4096]{1,0:T(8,128)S(1)}, f32[64,4096]{1,0:T(8,128)S(1)}, u32[]{:S(2)}, u32[]{:S(2)}) collective-permute-start(f32[64,4096]{1,0:T(8,128)S(1)} %get-tuple-element.23.lb), channel_id=1, source_target_pairs={{4,0},{8,4},{12,8},{16,12},{20,16},{24,20},{28,24},{32,28},{36,32}... | collective-permute-start | bytes 3145736 | tf_op jit(solution)/shard_map/ppermute | solution.py:301
  39.2 47.0 %collective-permute-start.2 = (f32[64,4096]{1,0:T(8,128)}, f32[64,4096]{1,0:T(8,128)S(1)}, u32[]{:S(2)}, u32[]{:S(2)}) collective-permute-start(f32[64,4096]{1,0:T(8,128)} %get-tuple-element.24.rt), channel_id=1, source_target_pairs={{0,4},{4,8},{8,12},{12,16},{16,20},{20,24},{24,28},{28,32},{32,36}... | collective-permute-start | bytes 3145736 | tf_op jit(solution)/shard_map/ppermute | solution.py:296
  46.0 44.1 %collective-permute-start.10 = (f32[2,128,128]{2,1,0:T(8,128)S(1)}, f32[2,128,128]{2,1,0:T(8,128)S(1)}, u32[]{:S(2)}, u32[]{:S(2)}) collective-permute-start(f32[2,128,128]{2,1,0:T(8,128)S(1)} %gram_2_inner.1), channel_id=1, source_target_pairs={{0,1},{1,0},{2,3},{3,2},{4,5},{5,4},{6,7},{7,6},{8,9},{9,8},{10,11... | collective-permute-start | bytes 393224 | tf_op jit(solution)/shard_map/ppermute | solution.py:305
  46.1 114.5 %collective-permute-start.9 = (f32[64,4096]{1,0:T(8,128)S(1)}, f32[64,4096]{1,0:T(8,128)S(1)}, u32[]{:S(2)}, u32[]{:S(2)}) collective-permute-start(f32[64,4096]{1,0:T(8,128)S(1)} %get-tuple-element.25.refs_1_.refs_2_), channel_id=1, source_target_pairs={{4,0},{8,4},{12,8},{16,12},{20,16},{24,20},{28,24},{32,28},{36,32}... | collective-permute-start | bytes 3145736 | tf_op jit(solution)/shard_map/ppermute | solution.py:301
  54.5 117.3 %collective-permute-start.8 = (f32[64,4096]{1,0:T(8,128)}, f32[64,4096]{1,0:T(8,128)}, u32[]{:S(2)}, u32[]{:S(2)}) collective-permute-start(f32[64,4096]{1,0:T(8,128)} %get-tuple-element.26.refs_2_.refs_3_), channel_id=1, source_target_pairs={{0,4},{4,8},{8,12},{12,16},{16,20},{20,24},{24,28},{28,32},{32,36}... | collective-permute-start | bytes 3145736 | tf_op jit(solution)/shard_map/ppermute | solution.py:296
  62.9 100.6 %copy-start = (f32[64,4096]{1,0:T(8,128)}, f32[64,4096]{1,0:T(8,128)S(1)}, u32[]{:S(2)}) copy-start(f32[64,4096]{1,0:T(8,128)S(1)} %broadcast_select_fusion.refs_3_.refs_4_) | copy-start | bytes 3145732
  90.0 101.6 %copy-start.4 = (f32[64,4096]{1,0:T(8,128)S(1)}, f32[64,4096]{1,0:T(8,128)}, u32[]{:S(2)}) copy-start(f32[64,4096]{1,0:T(8,128)} %get-tuple-element.24.rt) | copy-start | bytes 3145732
  90.0 1.7 collective-permute-start.4
  90.2 43.6 %collective-permute-start.11 = (f32[2,128,128]{2,1,0:T(8,128)S(1)}, f32[2,128,128]{2,1,0:T(8,128)S(1)}, u32[]{:S(2)}, u32[]{:S(2)}) collective-permute-start(f32[2,128,128]{2,1,0:T(8,128)S(1)} %add.17.a_ref), channel_id=1, source_target_pairs={{0,2},{1,3},{2,0},{3,1},{4,6},{5,7},{6,4},{7,5},{8,10},{9,11},{10,... | collective-permute-start | bytes 393224 | tf_op jit(solution)/shard_map/ppermute | solution.py:306
  91.8 57.6 %collective-permute-start.5 = (f32[2,128,128]{2,1,0:T(8,128)S(1)}, f32[2,128,128]{2,1,0:T(8,128)S(1)}, u32[]{:S(2)}, u32[]{:S(2)}) collective-permute-start(f32[2,128,128]{2,1,0:T(8,128)S(1)} %add.16.a_ref), channel_id=1, source_target_pairs={{0,2},{1,3},{2,0},{3,1},{4,6},{5,7},{6,4},{7,5},{8,10},{9,11},{10,... | collective-permute-start | bytes 393224 | tf_op jit(solution)/shard_map/ppermute | solution.py:306
  142.0 58.3 %copy-start.5 = (f32[64,4096]{1,0:T(8,128)}, f32[64,4096]{1,0:T(8,128)S(1)}, u32[]{:S(2)}) copy-start(f32[64,4096]{1,0:T(8,128)S(1)} %get-tuple-element.39.refs_2_.refs_6_) | copy-start | bytes 3145732
  142.0 58.3 %copy-start.6 = (f32[64,4096]{1,0:T(8,128)}, f32[64,4096]{1,0:T(8,128)S(1)}, u32[]{:S(2)}) copy-start(f32[64,4096]{1,0:T(8,128)S(1)} %get-tuple-element.35.refs_2_.refs_8_) | copy-start | bytes 3145732
  142.0 58.3 %copy-start.7 = (f32[64,4096]{1,0:T(8,128)}, f32[64,4096]{1,0:T(8,128)S(1)}, u32[]{:S(2)}) copy-start(f32[64,4096]{1,0:T(8,128)S(1)} %get-tuple-element.38.refs_1_.refs_5_) | copy-start | bytes 3145732
  142.0 81.8 %collective-permute-start.19 = (f32[64,4096]{1,0:T(8,128)S(1)}, f32[64,4096]{1,0:T(8,128)}, u32[]{:S(2)}, u32[]{:S(2)}) collective-permute-start(f32[64,4096]{1,0:T(8,128)S(1)} %get-tuple-element.34.refs_1_.refs_3_), channel_id=1, source_target_pairs={{4,0},{8,4},{12,8},{16,12},{20,16},{24,20},{28,24},{32,28},{36,32}... | collective-permute-start | bytes 3145736 | tf_op jit(solution)/shard_map/ppermute | solution.py:301
  145.9 77.9 %collective-permute-start.18 = (f32[64,4096]{1,0:T(8,128)S(1)}, f32[64,4096]{1,0:T(8,128)S(1)}, u32[]{:S(2)}, u32[]{:S(2)}) collective-permute-start(f32[64,4096]{1,0:T(8,128)S(1)} %get-tuple-element.35.refs_2_.refs_8_), channel_id=1, source_target_pairs={{0,4},{4,8},{8,12},{12,16},{16,20},{20,24},{24,28},{28,32},{32,36}... | collective-permute-start | bytes 3145736 | tf_op jit(solution)/shard_map/ppermute | solution.py:296
  153.7 37.4 %collective-permute-start.7 = (f32[64,128]{1,0:T(8,128)S(1)}, f32[64,128]{1,0:T(8,128)S(1)}, u32[]{:S(2)}, u32[]{:S(2)}) collective-permute-start(f32[64,128]{1,0:T(8,128)S(1)} %get-tuple-element.45), channel_id=1, source_target_pairs={{4,0},{8,4},{12,8},{16,12},{20,16},{24,20},{28,24},{32,28},{36,32}... | collective-permute-start | bytes 98312 | tf_op jit(solution)/shard_map/ppermute | solution.py:301
  161.6 30.0 %collective-permute-start.6 = (f32[64,128]{1,0:T(8,128)S(1)}, f32[64,128]{1,0:T(8,128)S(1)}, u32[]{:S(2)}, u32[]{:S(2)}) collective-permute-start(f32[64,128]{1,0:T(8,128)S(1)} %get-tuple-element.46), channel_id=1, source_target_pairs={{0,4},{4,8},{8,12},{12,16},{16,20},{20,24},{24,28},{28,32},{32,36}... | collective-permute-start | bytes 98312 | tf_op jit(solution)/shard_map/ppermute | solution.py:296
  169.4 54.3 %copy-start.8 = (f32[64,4096]{1,0:T(8,128)}, f32[64,4096]{1,0:T(8,128)S(1)}, u32[]{:S(2)}) copy-start(f32[64,4096]{1,0:T(8,128)S(1)} %get-tuple-element.40.refs_3_.refs_7_) | copy-start | bytes 3145732
  169.4 62.7 %copy-start.2 = (f32[64,4096]{1,0:T(8,128)S(1)}, f32[64,4096]{1,0:T(8,128)}, u32[]{:S(2)}) copy-start(f32[64,4096]{1,0:T(8,128)} %copy-done.1) | copy-start | bytes 3145732
  171.9 28.6 %collective-permute-start.14 = (f32[2,128,128]{2,1,0:T(8,128)S(1)}, f32[2,128,128]{2,1,0:T(8,128)S(1)}, u32[]{:S(2)}, u32[]{:S(2)}) collective-permute-start(f32[2,128,128]{2,1,0:T(8,128)S(1)} %gram_3_inner.1), channel_id=1, source_target_pairs={{0,1},{1,0},{2,3},{3,2},{4,5},{5,4},{6,7},{7,6},{8,9},{9,8},{10,11... | collective-permute-start | bytes 393224 | tf_op jit(solution)/shard_map/ppermute | solution.py:305
  196.3 35.9 %copy-start.12 = (f32[64,4096]{1,0:T(8,128)}, f32[64,4096]{1,0:T(8,128)S(1)}, u32[]{:S(2)}) copy-start(f32[64,4096]{1,0:T(8,128)S(1)} %get-tuple-element.36.refs_3_.refs_9_) | copy-start | bytes 3145732
  196.3 1.6 copy-start.10
  200.3 1.6 collective-permute-start.12
  200.5 6.4 %collective-permute-start.15 = (f32[2,128,128]{2,1,0:T(8,128)S(1)}, f32[2,128,128]{2,1,0:T(8,128)S(1)}, u32[]{:S(2)}, u32[]{:S(2)}) collective-permute-start(f32[2,128,128]{2,1,0:T(8,128)S(1)} %add.19.a_ref), channel_id=1, source_target_pairs={{0,2},{1,3},{2,0},{3,1},{4,6},{5,7},{6,4},{7,5},{8,10},{9,11},{10,... | collective-permute-start | bytes 393224 | tf_op jit(solution)/shard_map/ppermute | solution.py:306
  202.0 9.1 %collective-permute-start.13 = (f32[2,128,128]{2,1,0:T(8,128)S(1)}, f32[2,128,128]{2,1,0:T(8,128)S(1)}, u32[]{:S(2)}, u32[]{:S(2)}) collective-permute-start(f32[2,128,128]{2,1,0:T(8,128)S(1)} %add.18.a_ref), channel_id=1, source_target_pairs={{0,2},{1,3},{2,0},{3,1},{4,6},{5,7},{6,4},{7,5},{8,10},{9,11},{10,... | collective-permute-start | bytes 393224 | tf_op jit(solution)/shard_map/ppermute | solution.py:306
  215.4 9.4 %collective-permute-start.17 = (f32[64,128]{1,0:T(8,128)S(1)}, f32[64,128]{1,0:T(8,128)S(1)}, u32[]{:S(2)}, u32[]{:S(2)}) collective-permute-start(f32[64,128]{1,0:T(8,128)S(1)} %get-tuple-element.41), channel_id=1, source_target_pairs={{4,0},{8,4},{12,8},{16,12},{20,16},{24,20},{28,24},{32,28},{36,32}... | collective-permute-start | bytes 98312 | tf_op jit(solution)/shard_map/ppermute | solution.py:301
  221.8 10.3 %collective-permute-start.16 = (f32[64,128]{1,0:T(8,128)S(1)}, f32[64,128]{1,0:T(8,128)S(1)}, u32[]{:S(2)}, u32[]{:S(2)}) collective-permute-start(f32[64,128]{1,0:T(8,128)S(1)} %get-tuple-element.42), channel_id=1, source_target_pairs={{0,4},{4,8},{8,12},{12,16},{16,20},{20,24},{24,28},{28,32},{32,36}... | collective-permute-start | bytes 98312 | tf_op jit(solution)/shard_map/ppermute | solution.py:296
  232.1 1.2 copy-start.11
  (8 other events, 8.5 us)

commit v2 on v0

v2 whole, which is shorter than its diff:
```python
import functools

import jax
import jax.numpy as jnp
from jax import lax
from jax.experimental import pallas as pl
from jax.experimental.pallas import tpu as pltpu
from jax.sharding import PartitionSpec as P

B = 64
W = 128
PD = 4
NS_STEPS = 8
EPS = 1e-06
F32 = jnp.float32
BF16 = jnp.bfloat16

LONG = pl.CostEstimate(flops=10**10, bytes_accessed=4 * 10**8, transcendentals=0)

NN = (((1,), (0,)), ((), ()))
NT = (((1,), (1,)), ((), ()))
TN = (((0,), (0,)), ((), ()))


def params(mib=60):
    return pltpu.CompilerParams(vmem_limit_bytes=mib * 1024 * 1024)


def split(x):
    high = x.astype(BF16)
    return high, (x - high.astype(F32)).astype(BF16)


def dot(a, b, dims):
    return lax.dot_general(a, b, dims, preferred_element_type=F32)


def factor_stack(y):
    high, low = split(y)
    return jnp.concatenate(
        [jnp.concatenate([high, high], 1), jnp.concatenate([low, jnp.zeros_like(low)], 1)], 0
    )


def apply_rows(stack, values):
    high, low = split(values)
    both = dot(stack, jnp.concatenate([high, low], 0), NN)
    half = both.shape[0] // 2
    return both[:half] + both[half:]


def finish_gram(acc):
    cross = acc[:, W:]
    return acc[:, :W] + cross + cross.T


def store_gram(flags, acc, mine, theirs):
    half = PD // 2
    core = flags[2]
    for j in range(half):
        mine[j] = finish_gram(acc[core * half + j])
        theirs[j] = finish_gram(acc[(1 - core) * half + j])


def gram_rows_kernel(flags, *refs):
    cols, (mine, theirs, acc) = refs[:PD], refs[PD:]
    step = pl.program_id(0)

    @pl.when(step == 0)
    def _():
        acc[...] = jnp.zeros_like(acc)

    for k in range(PD):
        high, low = split(cols[k][...])
        acc[k] += dot(high, jnp.concatenate([high, low], 1), TN)

    @pl.when(step == pl.num_programs(0) - 1)
    def _():
        store_gram(flags, acc, mine, theirs)


def gram_blocks_kernel(flags, *refs):
    blocks, (grams, acc) = refs[: 2 * PD], refs[2 * PD :]
    step = pl.program_id(0)

    @pl.when(step == 0)
    def _():
        acc[...] = jnp.zeros_like(acc)

    for k in range(PD):
        high, low = split(jnp.concatenate([blocks[2 * k][...], blocks[2 * k + 1][...]], 0))
        acc[k] += dot(high, jnp.concatenate([high, low], 0), NT)

    @pl.when(step == pl.num_programs(0) - 1)
    def _():
        for k in range(PD):
            grams[k] = finish_gram(acc[k])


SMEM_SPEC = pl.BlockSpec(memory_space=pltpu.SMEM)
ANY_SPEC = pl.BlockSpec(memory_space=pl.ANY)


def gram_call(kernel, flags, operands, specs, steps, counts, name):
    return pl.pallas_call(
        kernel,
        grid=(steps,),
        in_specs=[SMEM_SPEC] + specs,
        out_specs=[pl.BlockSpec((n, W, W), lambda i: (0, 0, 0)) for n in counts],
        out_shape=[jax.ShapeDtypeStruct((n, W, W), F32) for n in counts],
        scratch_shapes=[pltpu.VMEM((PD, W, 2 * W), F32)],
        compiler_params=params(),
        cost_estimate=LONG,
        name=name,
    )(flags, *operands)


def column_spec(k, chunk):
    return pl.BlockSpec((chunk, W), lambda i: (i, k))


def gram_rows(flags, matrix, name, chunk=1024):
    specs = [column_spec(k, chunk) for k in range(PD)]
    steps, counts = matrix.shape[0] // chunk, (PD // 2, PD // 2)
    return gram_call(gram_rows_kernel, flags, [matrix] * PD, specs, steps, counts, name)


def gram_blocks(flags, pairs, name, chunk=1024):
    blocks = [x for pair in pairs for x in pair]
    specs = [pl.BlockSpec((B, chunk), lambda i: (0, i))] * len(blocks)
    steps = blocks[0].shape[1] // chunk
    return gram_call(gram_blocks_kernel, flags, blocks, specs, steps, (PD,), name)[0]


def mm3(a, b, dims):
    ah, al = split(a)
    bh, bl = split(b)
    zero = jnp.zeros_like(bl)
    if dims == NT:
        right = jnp.concatenate([jnp.concatenate([bh, bh], 1), jnp.concatenate([bl, zero], 1)], 0)
    else:
        right = jnp.concatenate([jnp.concatenate([bh, bl], 1), jnp.concatenate([bh, zero], 1)], 0)
    out = dot(jnp.concatenate([ah, al], 1), right, dims)
    return out[:, :W] + out[:, W:]


def factors_kernel(flags, a_ref, b_ref, y_ref, *edges):
    row = lax.broadcasted_iota(jnp.int32, (W, W), 0)
    col = lax.broadcasted_iota(jnp.int32, (W, W), 1)
    eye = row == col
    n = y_ref.shape[0]
    ys = []
    for k in range(n):
        g = a_ref[k] + b_ref[k]
        diag = jnp.where(eye, g, 0.0)
        norm_col = jnp.sqrt(jnp.sum(diag, axis=1, keepdims=True) + EPS)
        norm_row = jnp.sqrt(jnp.sum(diag, axis=0, keepdims=True) + EPS)
        corr = g / (norm_col * norm_row)
        skew = jnp.where(row < col, -0.5 * corr, jnp.where(row > col, 0.5 * corr, 0.0))
        total = jnp.sum(jnp.sum(skew * skew, axis=1, keepdims=True), axis=0, keepdims=True)
        ys.append((jnp.where(eye, 1.0, 0.0) - skew) / jnp.sqrt(1.0 + total))

    def step(_, ys):
        inner = [mm3(y, y, NT) for y in ys]
        return tuple(1.5 * y - 0.5 * mm3(a, y, NN) for a, y in zip(inner, ys))

    ys = list(lax.fori_loop(0, NS_STEPS, step, tuple(ys)))
    swap = flags[0] != 0
    if n < PD:
        swap = jnp.logical_and(swap, flags[2] == 0)
    ys[0] = jnp.where(swap, jnp.concatenate([ys[0][B:], ys[0][:B]], 0), ys[0])
    for k in range(n):
        y_ref[k] = ys[k]
    if edges:
        edges[0][...] = ys[0][B:]
        edges[1][...] = ys[n - 1][:B]


def factors(flags, a, b, name):
    vmem = pl.BlockSpec(memory_space=pltpu.VMEM)
    edges = 2 if a.shape[0] == PD else 0
    return pl.pallas_call(
        factors_kernel,
        in_specs=[SMEM_SPEC, vmem, vmem],
        out_specs=[vmem] * (1 + edges),
        out_shape=[jax.ShapeDtypeStruct(a.shape, F32)] + [jax.ShapeDtypeStruct((B, W), F32)] * edges,
        compiler_params=params(),
        cost_estimate=LONG,
        name=name,
    )(flags, a, b)


def factor_of(flags, ys, k, half=None):
    if len(ys) == 1:
        y = ys[0][k]
    else:
        core, slot = divmod(k, PD // 2)
        y = jnp.where(flags[2] == core, ys[0][slot], ys[1][slot])
    return y if half is None else y[half * B : (half + 1) * B]


def rotate_kernel(parts, by_rows, sources, deps, flags, *refs):
    per = 1 if by_rows else 2
    ys, refs = refs[:sources], refs[sources:]
    ins, outs = refs[: per * len(parts)], list(refs[per * len(parts) + deps :])
    for at, (k, half) in enumerate(parts):
        y = factor_of(flags, ys, k, half)
        count = y.shape[0]
        if by_rows:
            high, low = split(ins[at][...])
            both = dot(factor_stack(y), jnp.concatenate([high, low], 1), NT)
            new = both[:count] + both[count:]
        else:
            new = apply_rows(
                factor_stack(y), jnp.concatenate([ins[2 * at][...], ins[2 * at + 1][...]], 0)
            )
        for start in range(0, count, B):
            outs.pop(0)[...] = new[start : start + B]


def rotate_call(flags, ys, parts, by_rows, operands, specs, cols, chunk, name, deps=()):
    count = sum(2 if half is None else 1 for _, half in parts)
    whole = pl.BlockSpec(ys[0].shape, lambda i: (0, 0, 0))
    return pl.pallas_call(
        functools.partial(rotate_kernel, parts, by_rows, len(ys), len(deps)),
        grid=(cols // chunk,),
        in_specs=[SMEM_SPEC] + [whole] * len(ys) + specs + [ANY_SPEC] * len(deps),
        out_specs=[pl.BlockSpec((B, chunk), lambda i: (0, i))] * count,
        out_shape=[jax.ShapeDtypeStruct((B, cols), F32)] * count,
        compiler_params=params(),
        cost_estimate=LONG,
        name=name,
    )(flags, *ys, *operands, *deps)


def rotate_rows(flags, ys, parts, matrix, name, chunk=1024):
    specs = [column_spec(k, chunk) for k, _ in parts]
    operands = [matrix] * len(parts)
    return rotate_call(flags, ys, parts, True, operands, specs, matrix.shape[0], chunk, name)


def rotate_blocks(flags, ys, parts, pairs, name, deps=(), chunk=1024):
    blocks = [x for k, _ in parts for x in pairs[k]]
    specs = [pl.BlockSpec((B, chunk), lambda i: (0, i))] * len(blocks)
    cols = blocks[0].shape[1]
    return rotate_call(flags, ys, parts, False, blocks, specs, cols, chunk, name, deps)


def rotate_ends_kernel(flags, y_left, y_right, lt, lb, rt, rb, l_edge, r_edge, left, right):
    new = apply_rows(factor_stack(y_left[...]), jnp.concatenate([lt[...], lb[...]], 0))
    left[...] = jnp.where(flags[0] != 0, l_edge[...], new)
    new = apply_rows(factor_stack(y_right[...]), jnp.concatenate([rt[...], rb[...]], 0))
    right[...] = jnp.where(flags[1] != 0, r_edge[...], new)


def rotate_ends(flags, edges, left_pair, right_pair, instead, name, chunk=1024):
    cols = instead[0].shape[1]
    spec = pl.BlockSpec((B, chunk), lambda i: (0, i))
    half = pl.BlockSpec((B, W), lambda i: (0, 0))
    return pl.pallas_call(
        rotate_ends_kernel,
        grid=(cols // chunk,),
        in_specs=[SMEM_SPEC, half, half] + [spec] * 6,
        out_specs=[spec] * 2,
        out_shape=[jax.ShapeDtypeStruct((B, cols), F32)] * 2,
        compiler_params=params(),
        cost_estimate=LONG,
        name=name,
    )(flags, *edges, *left_pair, *right_pair, *instead)


def final_inner_kernel(flags, y_ref, *refs):
    ins = refs[: 2 * PD]
    out, l_1, r_2, l_0, r_3 = refs[2 * PD :]

    def rotated(k, half):
        values = jnp.concatenate([ins[2 * k][...], ins[2 * k + 1][...]], 0)
        return apply_rows(factor_stack(factor_of(flags, (y_ref,), k, half)), values)

    own1, own2 = rotated(1, None), rotated(2, None)
    l_1[...] = own1[B:]
    r_2[...] = own2[:B]
    out[:, :W] = jnp.concatenate([rotated(0, 0), own2[B:]], 0).T
    out[:, W:] = jnp.concatenate([own1[:B], rotated(3, 1)], 0).T

    @pl.when(flags[0] != 0)
    def _():
        l_0[...] = rotated(0, 1)

    @pl.when(flags[1] != 0)
    def _():
        r_3[...] = rotated(3, 0)


def edge_specs(chunk):
    return [
        pl.BlockSpec((B, chunk), lambda i, flags: (0, i * flags[0])),
        pl.BlockSpec((B, chunk), lambda i, flags: (0, i * flags[1])),
    ]


def final_inner(flags, y, pairs, chunk=1024):
    blocks = [x for pair in pairs for x in pair]
    cols = blocks[0].shape[1]
    spec = pl.BlockSpec((B, chunk), lambda i, flags: (0, i))
    block = jax.ShapeDtypeStruct((B, cols), F32)
    whole = pl.BlockSpec((PD, W, W), lambda i, flags: (0, 0, 0))
    return pl.pallas_call(
        final_inner_kernel,
        grid_spec=pltpu.PrefetchScalarGridSpec(
            num_scalar_prefetch=1,
            grid=(cols // chunk,),
            in_specs=[whole] + [spec] * len(blocks),
            out_specs=[pl.BlockSpec((chunk, 2 * W), lambda i, flags: (i, 0)), spec, spec]
            + edge_specs(chunk),
        ),
        out_shape=[jax.ShapeDtypeStruct((cols, 2 * W), F32)] + [block] * 4,
        compiler_params=params(),
        cost_estimate=LONG,
        name="final_inner",
    )(flags, y, *blocks)


def final_kernel(flags, y_left, y_right, lt, lb, rt, rb, l_1, r_2, l_0, r_3, inner, out):
    left = apply_rows(factor_stack(y_left[...]), jnp.concatenate([lt[...], lb[...]], 0))
    right = apply_rows(factor_stack(y_right[...]), jnp.concatenate([rt[...], rb[...]], 0))
    left = jnp.where(flags[0] != 0, l_0[...], left)
    right = jnp.where(flags[1] != 0, r_3[...], right)
    out[:, :W] = jnp.concatenate([left, l_1[...]], 0).T
    out[:, W : 3 * W] = inner[...]
    out[:, 3 * W :] = jnp.concatenate([r_2[...], right], 0).T


def final(flags, edges, left_pair, right_pair, done, inner, chunk=1024):
    cols = inner.shape[0]
    spec = pl.BlockSpec((B, chunk), lambda i, flags: (0, i))
    half = pl.BlockSpec((B, W), lambda i, flags: (0, 0))
    return pl.pallas_call(
        final_kernel,
        grid_spec=pltpu.PrefetchScalarGridSpec(
            num_scalar_prefetch=1,
            grid=(cols // chunk,),
            in_specs=[half, half]
            + [spec] * 6
            + edge_specs(chunk)
            + [pl.BlockSpec((chunk, 2 * W), lambda i, flags: (i, 0))],
            out_specs=pl.BlockSpec((chunk, PD * W), lambda i, flags: (i, 0)),
        ),
        out_shape=jax.ShapeDtypeStruct((cols, PD * W), F32),
        compiler_params=params(),
        cost_estimate=LONG,
        name="final",
    )(flags, *edges, *left_pair, *right_pair, *done, inner)


def send_on(x):
    peers = lax.axis_size("pair")
    return lax.ppermute(x, "pair", [(i, i + 1) for i in range(peers - 1)])


def send_back(x):
    peers = lax.axis_size("pair")
    return lax.ppermute(x, "pair", [(i + 1, i) for i in range(peers - 1)])


def after(x, *deps):
    return pl.pallas_call(
        lambda *refs: None,
        in_specs=[pl.BlockSpec(memory_space=pl.ANY)] * (1 + len(deps)),
        out_specs=pl.BlockSpec(memory_space=pl.ANY),
        out_shape=jax.ShapeDtypeStruct(x.shape, x.dtype),
        input_output_aliases={0: 0},
        cost_estimate=LONG,
        name="after",
    )(x, *deps)


def other_core(x):
    return lax.ppermute(x, "rows", [(i, i ^ 1) for i in range(4)])


def row_terms(mine, theirs, *deps):
    near = mine + other_core(theirs)
    if deps:
        near = after(near, *deps)
    return near, lax.ppermute(near, "rows", [(i, i ^ 2) for i in range(4)])


def body(matrix):
    index = lax.axis_index("pair")
    last = lax.axis_size("pair") - 1
    first_one, last_one = index == 0, index == last
    core = lax.axis_index("rows") % 2
    flags = jnp.stack([first_one, last_one, core]).astype(jnp.int32)

    near, far = row_terms(*gram_rows(flags, matrix, "gram_1"))
    (y1,) = factors(flags, near, far, "factors_1")
    y1 = (y1, other_core(y1))
    r1_3, l1_0 = rotate_rows(flags, y1, [(3, 0), (0, 1)], matrix, "rotate_1_ends")
    in_left = send_on(r1_3)
    in_right = send_back(l1_0)
    r1_0, l1_3, r1_1, l1_1, r1_2, l1_2 = rotate_rows(
        flags, y1, [(0, 0), (3, 1), (1, None), (2, None)], matrix, "rotate_1_inner"
    )
    in_left2 = send_on(r1_2)

    in_left = jnp.where(first_one, l1_0, in_left)
    in_right = jnp.where(last_one, r1_3, in_right)
    pairs2 = [(in_left, l1_1), (r1_0, l1_2), (r1_1, l1_3), (r1_2, in_right)]
    near, far = row_terms(*[gram_blocks(flags, pairs2, "gram_2")] * 2, in_left2)
    l1_1 = after(l1_1, near)
    pairs2[0] = (in_left, l1_1)
    in_right2 = send_back(l1_1)
    y2, to_left, to_right = factors(flags, near, far, "factors_2")
    edges2 = (send_on(to_right), send_back(to_left))
    r2_2, l2_1 = rotate_blocks(flags, (y2,), [(2, 0), (1, 1)], pairs2, "rotate_2_ends")
    in_left3 = send_on(r2_2)
    r2_0, l2_0, r2_3, l2_3, r2_1, l2_2 = rotate_blocks(
        flags, (y2,), [(0, None), (3, None), (1, 0), (2, 1)], pairs2, "rotate_2_inner", edges2
    )

    r2_left, l2_right = rotate_ends(
        flags, edges2, (in_left2, l1_0), (r1_3, in_right2), (l2_0, r2_3), "ends_2"
    )
    pairs3 = [(r2_left, l2_1), (r2_0, l2_2), (r2_1, l2_3), (r2_2, l2_right)]
    near, far = row_terms(*[gram_blocks(flags, pairs3, "gram_3")] * 2, in_left3)
    l2_1 = after(l2_1, near)
    pairs3[0] = (r2_left, l2_1)
    in_right3 = send_back(l2_1)
    y3, to_left, to_right = factors(flags, near, far, "factors_3")
    edges3 = (send_on(to_right), send_back(to_left))
    inner, *done = final_inner(flags, y3, pairs3)
    return final(flags, edges3, (in_left3, l2_0), (r2_3, in_right3), done, inner)


def solution(mesh):
    spec = P("rows", "pair")
    return jax.shard_map(body, mesh=mesh, in_specs=(spec,), out_specs=spec, check_vma=False)
```

time: 441 us -> 211 us (0.48); the launches traced: 433 us -> 210 us
  waiting for transfers between devices: 234 us -> 59.8 us
  matrix products: 101 us -> 0 us
  Pallas kernels: 0 us -> 83.2 us
  local copies, waits for them, and re-layouts: 37 us -> 6.32 us
  starting transfers between devices: 31.4 us -> 52 us
  between operations: 14.1 us -> 0.18 us
  other arithmetic: 15.9 us -> 8.33 us
    psum x3 -> x0, waiting for transfers between devices: 111 us -> none  [body(): factors = rotation_factors(lax.psum(partial_gram, 'rows'))]
    dot_general x54 -> x0, matrix products: 101 us -> none  [the longest x3 48.5 us: body(): jnp.einsum('rpi,rpj->pij', blocks, blocks, precision=lax.Precision.HIGHEST)]
    pallas_call x0 -> x17, Pallas kernels: none -> 83.2 us  [the longest x4 24.8 us: rotate_call(): pl.pallas_call(functools.partial(rotate_kernel, parts, by_rows, len(ys),...]
    ppermute x6 -> x17, waiting for transfers between devices: 123 us -> 59.8 us  [the longest x5 33.8 us: send_on(): return lax.ppermute(x, 'pair', [(i, i + 1) for i in range(peers - 1)])]
    ppermute x6 -> x17, starting transfers between devices: 31.1 us -> 52 us  [the longest x5 31.5 us: send_back(): return lax.ppermute(x, 'pair', [(i + 1, i) for i in range(peers - 1)])]
    psum x3 -> x0, local copies, waits for them, and re-layouts: 17.6 us -> none  [body(): factors = rotation_factors(lax.psum(partial_gram, 'rows'))]
    reshape x1 -> x0, local copies, waits for them, and re-layouts: 8.94 us -> none  [body(): return blocks.reshape(row_count, PD * width)]
    select_n x8 -> x2, other arithmetic: 11 us -> 3.39 us  [the longest x1 2.31 us: body(): in_right = jnp.where(last_one, r1_3, in_right)]
  transfers between devices with their start and end apart: 9 -> 17, of which waited for: 6 -> 13; matrix products, arithmetic and copies ran while one was open for 2% -> 3% of each run, Pallas kernels for 0% -> 28%
where the time goes in v2:
time: 211 us; the launch traced here: 210 us
  Pallas kernels  83.2 us (39%)
  waiting for transfers between devices  59.8 us (28%)
  starting transfers between devices  52 us (25%)
  other arithmetic  8.33 us (4%)
  local copies, waits for them, and re-layouts  6.32 us (3%)
    ppermute x5, waiting for transfers between devices, send_on(): return lax.ppermute(x, 'pair', [(i, i + 1) for i in range(peers - 1)])  33.8 us
    ppermute x5, starting transfers between devices, send_back(): return lax.ppermute(x, 'pair', [(i + 1, i) for i in range(peers - 1)])  31.5 us
    pallas_call x4, Pallas kernels, rotate_call(): pl.pallas_call(functools.partial(rotate_kernel, parts, by_rows, len(ys),...  24.8 us
    pallas_call x3, Pallas kernels, gram_call(): pl.pallas_call(kernel, grid=(steps,), in_specs=[SMEM_SPEC] + specs, out_s...  18.9 us
    ppermute x5, starting transfers between devices, send_on(): return lax.ppermute(x, 'pair', [(i, i + 1) for i in range(peers - 1)])  16.4 us
    pallas_call x3, Pallas kernels, factors(): pl.pallas_call(factors_kernel, in_specs=[SMEM_SPEC, vmem, vmem], out_spec...  16.3 us
    ppermute x5, waiting for transfers between devices, send_back(): return lax.ppermute(x, 'pair', [(i + 1, i) for i in range(peers - 1)])  11.6 us
    pallas_call x1, Pallas kernels, final(): pl.pallas_call(final_kernel, grid_spec=pltpu.PrefetchScalarGridSpec(num_s...  9.21 us
  transfers between devices with their start and end apart: 17, of which 13 were waited for; matrix products, arithmetic and copies ran while one was open for 3% of the time, Pallas kernels for 28%

profile of v2, /device:TPU:96, one launch (start us, length us, event | category | flops | bytes accessed | tf_op | source)
XLA Modules:
  0.0 209.9 jit_solution(477841217023265595)
XLA Ops:
  0.6 5.7 %gram_1.1 = (f32[2,128,128]{2,1,0:T(8,128)}, f32[2,128,128]{2,1,0:T(8,128)}) custom-call(s32[3]{0:T(128)} %pad_add_fusion.flags, f32[4096,512]{1,0:T(8,128)} %refs_5_.1, f32[4096,512]{1,0:T(8,128)} %refs_5_.1, f32[4096,512]{1,0:T(8,128)} %refs_5_.1, f32[4096,512]{1,0:T(8,128)} %refs_5_.1), custom_call_target="tpu_custom_call" | custom-call | flops 10000000000 | bytes 400000000 | tf_op jit(solution)/shard_map/gram_1/pallas_call | solution.py:105
  10.5 4.1 %collective-permute-done.1.b_ref = f32[2,128,128]{2,1,0:T(8,128)S(1)} collective-permute-done((f32[2,128,128]{2,1,0:T(8,128)S(1)}, f32[2,128,128]{2,1,0:T(8,128)S(1)}, u32[]{:S(2)}, u32[]{:S(2)}) %collective-permute-start.1) | collective-permute-done | bytes 131104 | tf_op jit(solution)/shard_map/ppermute | solution.py:386
  15.2 4.8 %factors_1.1.refs_0_ = f32[2,128,128]{2,1,0:T(8,128)} custom-call(s32[3]{0:T(128)} %pad_add_fusion.flags, f32[2,128,128]{2,1,0:T(8,128)} %copy-done.2, f32[2,128,128]{2,1,0:T(8,128)} %copy-done.9), custom_call_target="tpu_custom_call" | custom-call | flops 10000000000 | bytes 400000000 | tf_op jit(solution)/shard_map/factors_1/pallas_call | solution.py:182
  22.2 5.0 %rotate_1_ends.1 = (f32[64,4096]{1,0:T(8,128)}, f32[64,4096]{1,0:T(8,128)}) custom-call(s32[3]{0:T(128)} %pad_add_fusion.flags, f32[2,128,128]{2,1,0:T(8,128)} %factors_1.1.refs_0_, f32[2,128,128]{2,1,0:T(8,128)} %copy-done.8, f32[4096,512]{1,0:T(8,128)} %refs_5_.1, f32[4096,512]{1,0:T(8,128)} %refs_5_.1), custom_call_target="tpu_custom_call" | custom-call | flops 10000000000 | bytes 400000000 | tf_op jit(solution)/shard_map/rotate_1_ends/pallas_call | solution.py:224
  27.1 7.2 %collective-permute-start.4 = (f32[64,4096]{1,0:T(8,128)}, f32[64,4096]{1,0:T(8,128)}, u32[]{:S(2)}, u32[]{:S(2)}) collective-permute-start(f32[64,4096]{1,0:T(8,128)} %get-tuple-element.38.lb), channel_id=1, source_target_pairs={{4,0},{8,4},{12,8},{16,12},{20,16},{24,20},{28,24},{32,28},{36,32}... | collective-permute-start | bytes 3145736 | tf_op jit(solution)/shard_map/ppermute | solution.py:363
  34.4 2.1 collective-permute-start.3
  36.4 8.0 %rotate_1_inner.1 = (f32[64,4096]{1,0:T(8,128)}, f32[64,4096]{1,0:T(8,128)}, f32[64,4096]{1,0:T(8,128)}, f32[64,4096]{1,0:T(8,128)}, f32[64,4096]{1,0:T(8,128)}, /*index=5*/f32[64,4096]{1,0:T(8,128)}) custom-call(s32[3]{0:T(128)} %pad_add_fusion.flags, f32[2,128,128]{2,1,0:T(8,128)} %factors_1.1.refs_0_, f32[2,128,128]{2,1,0:T(8,128)} %copy-done.8, ...), custom_call_target="tpu_custom_call" | custom-call | flops 10000000000 | bytes 400000000 | tf_op jit(solution)/shard_map/rotate_1_inner/pallas_call | solution.py:224
  44.4 4.0 %collective-permute-start.6 = (f32[64,4096]{1,0:T(8,128)}, f32[64,4096]{1,0:T(8,128)}, u32[]{:S(2)}, u32[]{:S(2)}) collective-permute-start(f32[64,4096]{1,0:T(8,128)} %get-tuple-element.45.refs_6_.refs_3_), channel_id=1, source_target_pairs={{0,4},{4,8},{8,12},{12,16},{16,20},{20,24},{24,28},{28,32},{32,36}... | collective-permute-start | bytes 3145736 | tf_op jit(solution)/shard_map/ppermute | solution.py:358
  48.4 9.7 %collective-permute-done.4 = f32[64,4096]{1,0:T(8,128)} collective-permute-done((f32[64,4096]{1,0:T(8,128)}, f32[64,4096]{1,0:T(8,128)}, u32[]{:S(2)}, u32[]{:S(2)}) %collective-permute-start.4) | collective-permute-done | bytes 1048608 | tf_op jit(solution)/shard_map/ppermute | solution.py:363
  58.2 2.3 %broadcast_select_fusion.refs_7_.refs_4_ = f32[64,4096]{1,0:T(8,128)} fusion(f32[64,4096]{1,0:T(8,128)S(1)} %copy-done, f32[64,4096]{1,0:T(8,128)} %collective-permute-done.4, pred[]{:T(512)S(6)} %eq.9), kind=kLoop, calls=%fused_computation | loop fusion | flops 262144 | bytes 3145729 | tf_op jit(solution)/shard_map/jit(_where)/select_n | solution.py:408
  60.5 21.0 %collective-permute-done.3 = f32[64,4096]{1,0:T(8,128)S(1)} collective-permute-done((f32[64,4096]{1,0:T(8,128)}, f32[64,4096]{1,0:T(8,128)S(1)}, u32[]{:S(2)}, u32[]{:S(2)}) %collective-permute-start.3) | collective-permute-done | bytes 1048608 | tf_op jit(solution)/shard_map/ppermute | solution.py:358
  82.6 6.6 %gram_2.1 = f32[4,128,128]{2,1,0:T(8,128)} custom-call(s32[3]{0:T(128)} %pad_add_fusion.flags, f32[64,4096]{1,0:T(8,128)} %broadcast_select_fusion.1.refs_0_.refs_1_, f32[64,4096]{1,0:T(8,128)} %get-tuple-element.40.refs_1_.refs_0_, f32[64,4096]{1,0:T(8,128)} %get-tuple-element.41.refs_2_.refs_5_.refs_3_, ...), custom_call_target="tpu_custom_call" | custom-call | flops 10000000000 | bytes 400000000 | tf_op jit(solution)/shard_map/gram_2/pallas_call | solution.py:105
  89.1 1.7 collective-permute-done.5
  92.6 10.7 %collective-permute-done.6.refs_1_.lt = f32[64,4096]{1,0:T(8,128)} collective-permute-done((f32[64,4096]{1,0:T(8,128)}, f32[64,4096]{1,0:T(8,128)}, u32[]{:S(2)}, u32[]{:S(2)}) %collective-permute-start.6) | collective-permute-done | bytes 1048608 | tf_op jit(solution)/shard_map/ppermute | solution.py:358
  104.8 4.8 %collective-permute-start.10 = (f32[64,4096]{1,0:T(8,128)}, f32[64,4096]{1,0:T(8,128)S(1)}, u32[]{:S(2)}, u32[]{:S(2)}) collective-permute-start(f32[64,4096]{1,0:T(8,128)} %after.5.refs_2_), channel_id=1, source_target_pairs={{4,0},{8,4},{12,8},{16,12},{20,16},{24,20},{28,24},{32,28},{36,32}... | collective-permute-start | bytes 3145736 | tf_op jit(solution)/shard_map/ppermute | solution.py:363
  109.6 2.8 %collective-permute-done.7.b_ref = f32[4,128,128]{2,1,0:T(8,128)S(1)} collective-permute-done((f32[4,128,128]{2,1,0:T(8,128)}, f32[4,128,128]{2,1,0:T(8,128)S(1)}, u32[]{:S(2)}, u32[]{:S(2)}) %collective-permute-start.7) | collective-permute-done | bytes 262176 | tf_op jit(solution)/shard_map/ppermute | solution.py:386
  113.0 5.7 %factors_2.1 = (f32[4,128,128]{2,1,0:T(8,128)}, f32[64,128]{1,0:T(8,128)}, f32[64,128]{1,0:T(8,128)}) custom-call(s32[3]{0:T(128)} %pad_add_fusion.flags, f32[4,128,128]{2,1,0:T(8,128)} %after.4.a_ref.refs_1_, f32[4,128,128]{2,1,0:T(8,128)} %copy-done.6), custom_call_target="tpu_custom_call" | custom-call | flops 10000000000 | bytes 400000000 | tf_op jit(solution)/shard_map/factors_2/pallas_call | solution.py:182
  118.8 5.3 %collective-permute-start.8 = (f32[64,128]{1,0:T(8,128)}, f32[64,128]{1,0:T(8,128)S(1)}, u32[]{:S(2)}, u32[]{:S(2)}) collective-permute-start(f32[64,128]{1,0:T(8,128)} %get-tuple-element.46), channel_id=1, source_target_pairs={{0,4},{4,8},{8,12},{12,16},{16,20},{20,24},{24,28},{28,32},{32,36}... | collective-permute-start | bytes 98312 | tf_op jit(solution)/shard_map/ppermute | solution.py:358
  124.1 5.0 %collective-permute-start.9 = (f32[64,128]{1,0:T(8,128)}, f32[64,128]{1,0:T(8,128)S(1)}, u32[]{:S(2)}, u32[]{:S(2)}) collective-permute-start(f32[64,128]{1,0:T(8,128)} %get-tuple-element.47), channel_id=1, source_target_pairs={{4,0},{8,4},{12,8},{16,12},{20,16},{24,20},{28,24},{32,28},{36,32}... | collective-permute-start | bytes 98312 | tf_op jit(solution)/shard_map/ppermute | solution.py:363
  129.1 4.8 %rotate_2_ends.1 = (f32[64,4096]{1,0:T(8,128)}, f32[64,4096]{1,0:T(8,128)}) custom-call(s32[3]{0:T(128)} %pad_add_fusion.flags, f32[4,128,128]{2,1,0:T(8,128)} %get-tuple-element.48.refs_0_, f32[64,4096]{1,0:T(8,128)} %get-tuple-element.43.refs_4_.refs_7_.refs_1_, f32[64,4096]{1,0:T(8,128)} %get-tuple-element.44.refs_5_.refs_8_.refs_2_, ...), custom_call_target="tpu_custom_call" | custom-call | flops 10000000000 | bytes 400000000 | tf_op jit(solution)/shard_map/rotate_2_ends/pallas_call | solution.py:224
  133.9 2.3 %collective-permute-start.12 = (f32[64,4096]{1,0:T(8,128)}, f32[64,4096]{1,0:T(8,128)S(1)}, u32[]{:S(2)}, u32[]{:S(2)}) collective-permute-start(f32[64,4096]{1,0:T(8,128)} %get-tuple-element.57.refs_6_), channel_id=1, source_target_pairs={{0,4},{4,8},{8,12},{12,16},{16,20},{20,24},{24,28},{28,32},{32,36}... | collective-permute-start | bytes 3145736 | tf_op jit(solution)/shard_map/ppermute | solution.py:358
  136.9 1.9 collective-permute-done.9.refs_10_.y_right
  139.4 7.1 %rotate_2_inner.1 = (f32[64,4096]{1,0:T(8,128)}, f32[64,4096]{1,0:T(8,128)}, f32[64,4096]{1,0:T(8,128)}, f32[64,4096]{1,0:T(8,128)}, f32[64,4096]{1,0:T(8,128)}, /*index=5*/f32[64,4096]{1,0:T(8,128)}) custom-call(s32[3]{0:T(128)} %pad_add_fusion.flags, f32[4,128,128]{2,1,0:T(8,128)} %get-tuple-element.48.refs_0_, ...), custom_call_target="tpu_custom_call" | custom-call | flops 10000000000 | bytes 400000000 | tf_op jit(solution)/shard_map/rotate_2_inner/pallas_call | solution.py:224
  147.5 5.1 %ends_2.1 = (f32[64,4096]{1,0:T(8,128)}, f32[64,4096]{1,0:T(8,128)}) custom-call(s32[3]{0:T(128)} %pad_add_fusion.flags, f32[64,128]{1,0:T(8,128)} %copy-done.10, f32[64,128]{1,0:T(8,128)} %copy-done.11, f32[64,4096]{1,0:T(8,128)} %collective-permute-done.6.refs_1_.lt, f32[64,4096]{1,0:T(8,128)} %get-tuple-element.38.lb, f32[64,4096]{1,0:T(8,128)} %get-tuple-element.39.rt, ...), custom_call_target="tpu_custom_call" | custom-call | flops 10000000000 | bytes 400000000 | tf_op jit(solution)/shard_map/ends_2/pallas_call | solution.py:260
  152.6 6.6 %gram_3.1 = f32[4,128,128]{2,1,0:T(8,128)} custom-call(s32[3]{0:T(128)} %pad_add_fusion.flags, f32[64,4096]{1,0:T(8,128)} %get-tuple-element.51.refs_0_, f32[64,4096]{1,0:T(8,128)} %get-tuple-element.52.refs_1_.refs_0_, f32[64,4096]{1,0:T(8,128)} %get-tuple-element.53.refs_2_, f32[64,4096]{1,0:T(8,128)} %get-tuple-element.54.refs_3_, ...), custom_call_target="tpu_custom_call" | custom-call | flops 10000000000 | bytes 400000000 | tf_op jit(solution)/shard_map/gram_3/pallas_call | solution.py:105
  159.2 1.7 collective-permute-done.11
  164.6 6.9 %collective-permute-start.16 = (f32[64,4096]{1,0:T(8,128)}, f32[64,4096]{1,0:T(8,128)S(1)}, u32[]{:S(2)}, u32[]{:S(2)}) collective-permute-start(f32[64,4096]{1,0:T(8,128)} %after.7.refs_1_), channel_id=1, source_target_pairs={{4,0},{8,4},{12,8},{16,12},{20,16},{24,20},{28,24},{32,28},{36,32}... | collective-permute-start | bytes 3145736 | tf_op jit(solution)/shard_map/ppermute | solution.py:363
  173.2 5.7 %factors_3.1 = (f32[4,128,128]{2,1,0:T(8,128)}, f32[64,128]{1,0:T(8,128)}, f32[64,128]{1,0:T(8,128)}) custom-call(s32[3]{0:T(128)} %pad_add_fusion.flags, f32[4,128,128]{2,1,0:T(8,128)} %after.6.a_ref.refs_1_, f32[4,128,128]{2,1,0:T(8,128)} %copy-done.7), custom_call_target="tpu_custom_call" | custom-call | flops 10000000000 | bytes 400000000 | tf_op jit(solution)/shard_map/factors_3/pallas_call | solution.py:182
  179.0 2.8 %collective-permute-start.14 = (f32[64,128]{1,0:T(8,128)}, f32[64,128]{1,0:T(8,128)S(1)}, u32[]{:S(2)}, u32[]{:S(2)}) collective-permute-start(f32[64,128]{1,0:T(8,128)} %get-tuple-element.59), channel_id=1, source_target_pairs={{0,4},{4,8},{8,12},{12,16},{16,20},{20,24},{24,28},{28,32},{32,36}... | collective-permute-start | bytes 98312 | tf_op jit(solution)/shard_map/ppermute | solution.py:358
  181.7 7.6 %collective-permute-start.15 = (f32[64,128]{1,0:T(8,128)}, f32[64,128]{1,0:T(8,128)S(1)}, u32[]{:S(2)}, u32[]{:S(2)}) collective-permute-start(f32[64,128]{1,0:T(8,128)} %get-tuple-element.60), channel_id=1, source_target_pairs={{4,0},{8,4},{12,8},{16,12},{20,16},{24,20},{28,24},{32,28},{36,32}... | collective-permute-start | bytes 98312 | tf_op jit(solution)/shard_map/ppermute | solution.py:363
  189.3 9.0 %final_inner.1 = (f32[4096,256]{1,0:T(8,128)}, f32[64,4096]{1,0:T(8,128)}, f32[64,4096]{1,0:T(8,128)}, f32[64,4096]{1,0:T(8,128)}, f32[64,4096]{1,0:T(8,128)}) custom-call(s32[3]{0:T(128)} %pad_add_fusion.flags, f32[4,128,128]{2,1,0:T(8,128)} %get-tuple-element.61.y_ref, f32[64,4096]{1,0:T(8,128)} %get-tuple-element.51.refs_0_, f32[64,4096]{1,0:T(8,128)} %after.7.refs_1_, ...), custom_call_target="tpu_custom_call" | custom-call | flops 10000000000 | bytes 400000000 | tf_op jit(solution)/shard_map/final_inner/pallas_call | solution.py:308
  200.6 9.2 %final.1 = f32[4096,512]{1,0:T(8,128)} custom-call(s32[3]{0:T(128)} %pad_add_fusion.flags, f32[64,128]{1,0:T(8,128)} %copy-done.12, f32[64,128]{1,0:T(8,128)} %copy-done.13, f32[64,4096]{1,0:T(8,128)} %copy-done.3, f32[64,4096]{1,0:T(8,128)} %get-tuple-element.49.l_edge.lb, f32[64,4096]{1,0:T(8,128)} %get-tuple-element.50.r_edge.rt, f32[64,4096]{1,0:T(8,128)} %copy-done.5, ...), custom_call_target="tpu_custom_call" | custom-call | flops 10000000000 | bytes 400000000 | tf_op jit(solution)/shard_map/final/pallas_call | solution.py:338
  (53 shorter events, 22.6 us)
Async XLA Ops:
  6.4 1.6 collective-permute-start
  8.9 5.6 %copy-start.2 = (f32[2,128,128]{2,1,0:T(8,128)}, f32[2,128,128]{2,1,0:T(8,128)S(1)}, u32[]{:S(2)}) copy-start(f32[2,128,128]{2,1,0:T(8,128)S(1)} %add.14.a_ref) | copy-start | bytes 393220
  8.9 5.6 %collective-permute-start.1 = (f32[2,128,128]{2,1,0:T(8,128)S(1)}, f32[2,128,128]{2,1,0:T(8,128)S(1)}, u32[]{:S(2)}, u32[]{:S(2)}) collective-permute-start(f32[2,128,128]{2,1,0:T(8,128)S(1)} %add.14.a_ref), channel_id=1, source_target_pairs={{0,2},{1,3},{2,0},{3,1},{4,6},{5,7},{6,4},{7,5},{8,10},{9,11},{10,... | collective-permute-start | bytes 393224 | tf_op jit(solution)/shard_map/ppermute | solution.py:386
  14.5 0.6 copy-start.9
  19.9 1.6 collective-permute-start.2
  21.5 0.6 copy-start.8
  27.1 31.0 %collective-permute-start.4 = (f32[64,4096]{1,0:T(8,128)}, f32[64,4096]{1,0:T(8,128)}, u32[]{:S(2)}, u32[]{:S(2)}) collective-permute-start(f32[64,4096]{1,0:T(8,128)} %get-tuple-element.38.lb), channel_id=1, source_target_pairs={{4,0},{8,4},{12,8},{16,12},{20,16},{24,20},{28,24},{32,28},{36,32}... | collective-permute-start | bytes 3145736 | tf_op jit(solution)/shard_map/ppermute | solution.py:363
  34.3 23.8 %copy-start = (f32[64,4096]{1,0:T(8,128)S(1)}, f32[64,4096]{1,0:T(8,128)}, u32[]{:S(2)}) copy-start(f32[64,4096]{1,0:T(8,128)} %get-tuple-element.39.rt) | copy-start | bytes 3145732
  34.4 47.1 %copy-start.1 = (f32[64,4096]{1,0:T(8,128)S(1)}, f32[64,4096]{1,0:T(8,128)}, u32[]{:S(2)}) copy-start(f32[64,4096]{1,0:T(8,128)} %get-tuple-element.38.lb) | copy-start | bytes 3145732
  34.4 47.1 %collective-permute-start.3 = (f32[64,4096]{1,0:T(8,128)}, f32[64,4096]{1,0:T(8,128)S(1)}, u32[]{:S(2)}, u32[]{:S(2)}) collective-permute-start(f32[64,4096]{1,0:T(8,128)} %get-tuple-element.39.rt), channel_id=1, source_target_pairs={{0,4},{4,8},{8,12},{12,16},{16,20},{20,24},{24,28},{28,32},{32,36}... | collective-permute-start | bytes 3145736 | tf_op jit(solution)/shard_map/ppermute | solution.py:358
  44.4 58.9 %collective-permute-start.6 = (f32[64,4096]{1,0:T(8,128)}, f32[64,4096]{1,0:T(8,128)}, u32[]{:S(2)}, u32[]{:S(2)}) collective-permute-start(f32[64,4096]{1,0:T(8,128)} %get-tuple-element.45.refs_6_.refs_3_), channel_id=1, source_target_pairs={{0,4},{4,8},{8,12},{12,16},{16,20},{20,24},{24,28},{28,32},{32,36}... | collective-permute-start | bytes 3145736 | tf_op jit(solution)/shard_map/ppermute | solution.py:358
  89.1 1.7 collective-permute-start.5
  103.3 9.1 %collective-permute-start.7 = (f32[4,128,128]{2,1,0:T(8,128)}, f32[4,128,128]{2,1,0:T(8,128)S(1)}, u32[]{:S(2)}, u32[]{:S(2)}) collective-permute-start(f32[4,128,128]{2,1,0:T(8,128)} %after.4.a_ref.refs_1_), channel_id=1, source_target_pairs={{0,2},{1,3},{2,0},{3,1},{4,6},{5,7},{6,4},{7,5},{8,10},{9,11},{10,... | collective-permute-start | bytes 786440 | tf_op jit(solution)/shard_map/ppermute | solution.py:386
  104.8 41.7 %collective-permute-start.10 = (f32[64,4096]{1,0:T(8,128)}, f32[64,4096]{1,0:T(8,128)S(1)}, u32[]{:S(2)}, u32[]{:S(2)}) collective-permute-start(f32[64,4096]{1,0:T(8,128)} %after.5.refs_2_), channel_id=1, source_target_pairs={{4,0},{8,4},{12,8},{16,12},{20,16},{24,20},{28,24},{32,28},{36,32}... | collective-permute-start | bytes 3145736 | tf_op jit(solution)/shard_map/ppermute | solution.py:363
  112.4 0.7 copy-start.6
  118.8 18.1 %collective-permute-start.8 = (f32[64,128]{1,0:T(8,128)}, f32[64,128]{1,0:T(8,128)S(1)}, u32[]{:S(2)}, u32[]{:S(2)}) collective-permute-start(f32[64,128]{1,0:T(8,128)} %get-tuple-element.46), channel_id=1, source_target_pairs={{0,4},{4,8},{8,12},{12,16},{16,20},{20,24},{24,28},{28,32},{32,36}... | collective-permute-start | bytes 98312 | tf_op jit(solution)/shard_map/ppermute | solution.py:358
  124.1 14.7 %collective-permute-start.9 = (f32[64,128]{1,0:T(8,128)}, f32[64,128]{1,0:T(8,128)S(1)}, u32[]{:S(2)}, u32[]{:S(2)}) collective-permute-start(f32[64,128]{1,0:T(8,128)} %get-tuple-element.47), channel_id=1, source_target_pairs={{4,0},{8,4},{12,8},{16,12},{20,16},{24,20},{28,24},{32,28},{36,32}... | collective-permute-start | bytes 98312 | tf_op jit(solution)/shard_map/ppermute | solution.py:363
  133.9 28.7 %collective-permute-start.12 = (f32[64,4096]{1,0:T(8,128)}, f32[64,4096]{1,0:T(8,128)S(1)}, u32[]{:S(2)}, u32[]{:S(2)}) collective-permute-start(f32[64,4096]{1,0:T(8,128)} %get-tuple-element.57.refs_6_), channel_id=1, source_target_pairs={{0,4},{4,8},{8,12},{12,16},{16,20},{20,24},{24,28},{28,32},{32,36}... | collective-permute-start | bytes 3145736 | tf_op jit(solution)/shard_map/ppermute | solution.py:358
  136.9 1.9 copy-start.10
  138.8 0.6 copy-start.11
  146.5 1.0 copy-start.4
  159.2 1.7 collective-permute-start.11
  162.6 1.0 copy-start.3
  163.6 8.9 %collective-permute-start.13 = (f32[4,128,128]{2,1,0:T(8,128)}, f32[4,128,128]{2,1,0:T(8,128)S(1)}, u32[]{:S(2)}, u32[]{:S(2)}) collective-permute-start(f32[4,128,128]{2,1,0:T(8,128)} %after.6.a_ref.refs_1_), channel_id=1, source_target_pairs={{0,2},{1,3},{2,0},{3,1},{4,6},{5,7},{6,4},{7,5},{8,10},{9,11},{10,... | collective-permute-start | bytes 786440 | tf_op jit(solution)/shard_map/ppermute | solution.py:386
  164.6 35.1 %collective-permute-start.16 = (f32[64,4096]{1,0:T(8,128)}, f32[64,4096]{1,0:T(8,128)S(1)}, u32[]{:S(2)}, u32[]{:S(2)}) collective-permute-start(f32[64,4096]{1,0:T(8,128)} %after.7.refs_1_), channel_id=1, source_target_pairs={{4,0},{8,4},{12,8},{16,12},{20,16},{24,20},{28,24},{32,28},{36,32}... | collective-permute-start | bytes 3145736 | tf_op jit(solution)/shard_map/ppermute | solution.py:363
  172.5 0.7 copy-start.7
  179.0 20.7 %collective-permute-start.14 = (f32[64,128]{1,0:T(8,128)}, f32[64,128]{1,0:T(8,128)S(1)}, u32[]{:S(2)}, u32[]{:S(2)}) collective-permute-start(f32[64,128]{1,0:T(8,128)} %get-tuple-element.59), channel_id=1, source_target_pairs={{0,4},{4,8},{8,12},{12,16},{16,20},{20,24},{24,28},{28,32},{32,36}... | collective-permute-start | bytes 98312 | tf_op jit(solution)/shard_map/ppermute | solution.py:358
  181.7 17.9 %collective-permute-start.15 = (f32[64,128]{1,0:T(8,128)}, f32[64,128]{1,0:T(8,128)S(1)}, u32[]{:S(2)}, u32[]{:S(2)}) collective-permute-start(f32[64,128]{1,0:T(8,128)} %get-tuple-element.60), channel_id=1, source_target_pairs={{4,0},{8,4},{12,8},{16,12},{20,16},{24,20},{28,24},{32,28},{36,32}... | collective-permute-start | bytes 98312 | tf_op jit(solution)/shard_map/ppermute | solution.py:363
  199.6 0.6 copy-start.12
  199.7 0.6 copy-start.13
  199.7 1.0 copy-start.5

commit v3 on v2

--- a/solution.py
+++ b/solution.py
@@ -54,15 +54,15 @@
     return acc[:, :W] + cross + cross.T
 
 
-def store_gram(flags, acc, mine, theirs):
+def store_gram(acc, mine, theirs):
     half = PD // 2
-    core = flags[2]
+    core = lax.axis_index("rows") % 2
     for j in range(half):
         mine[j] = finish_gram(acc[core * half + j])
         theirs[j] = finish_gram(acc[(1 - core) * half + j])
 
 
-def gram_rows_kernel(flags, *refs):
+def gram_rows_kernel(*refs):
     cols, (mine, theirs, acc) = refs[:PD], refs[PD:]
     step = pl.program_id(0)
 
@@ -76,10 +76,10 @@
 
     @pl.when(step == pl.num_programs(0) - 1)
     def _():
-        store_gram(flags, acc, mine, theirs)
-
-
-def gram_blocks_kernel(flags, *refs):
+        store_gram(acc, mine, theirs)
+
+
+def gram_blocks_kernel(*refs):
     blocks, (grams, acc) = refs[: 2 * PD], refs[2 * PD :]
     step = pl.program_id(0)
 
@@ -101,35 +101,35 @@
 ANY_SPEC = pl.BlockSpec(memory_space=pl.ANY)
 
 
-def gram_call(kernel, flags, operands, specs, steps, counts, name):
+def gram_call(kernel, operands, specs, steps, counts, name):
     return pl.pallas_call(
         kernel,
         grid=(steps,),
-        in_specs=[SMEM_SPEC] + specs,
+        in_specs=specs,
         out_specs=[pl.BlockSpec((n, W, W), lambda i: (0, 0, 0)) for n in counts],
         out_shape=[jax.ShapeDtypeStruct((n, W, W), F32) for n in counts],
         scratch_shapes=[pltpu.VMEM((PD, W, 2 * W), F32)],
         compiler_params=params(),
         cost_estimate=LONG,
         name=name,
-    )(flags, *operands)
+    )(*operands)
 
 
 def column_spec(k, chunk):
     return pl.BlockSpec((chunk, W), lambda i: (i, k))
 
 
-def gram_rows(flags, matrix, name, chunk=1024):
+def gram_rows(matrix, name, chunk=2048):
     specs = [column_spec(k, chunk) for k in range(PD)]
     steps, counts = matrix.shape[0] // chunk, (PD // 2, PD // 2)
-    return gram_call(gram_rows_kernel, flags, [matrix] * PD, specs, steps, counts, name)
-
-
-def gram_blocks(flags, pairs, name, chunk=1024):
+    return gram_call(gram_rows_kernel, [matrix] * PD, specs, steps, counts, name)
+
+
+def gram_blocks(pairs, name, chunk=2048):
     blocks = [x for pair in pairs for x in pair]
     specs = [pl.BlockSpec((B, chunk), lambda i: (0, i))] * len(blocks)
     steps = blocks[0].shape[1] // chunk
-    return gram_call(gram_blocks_kernel, flags, blocks, specs, steps, (PD,), name)[0]
+    return gram_call(gram_blocks_kernel, blocks, specs, steps, (PD,), name)[0]
 
 
 def mm3(a, b, dims):
@@ -233,40 +233,72 @@
     )(flags, *ys, *operands, *deps)
 
 
-def rotate_rows(flags, ys, parts, matrix, name, chunk=1024):
+def rotate_rows(flags, ys, parts, matrix, name, chunk=2048):
     specs = [column_spec(k, chunk) for k, _ in parts]
     operands = [matrix] * len(parts)
     return rotate_call(flags, ys, parts, True, operands, specs, matrix.shape[0], chunk, name)
 
 
-def rotate_blocks(flags, ys, parts, pairs, name, deps=(), chunk=1024):
+def rotate_blocks(flags, ys, parts, pairs, name, deps=(), chunk=2048):
     blocks = [x for k, _ in parts for x in pairs[k]]
     specs = [pl.BlockSpec((B, chunk), lambda i: (0, i))] * len(blocks)
     cols = blocks[0].shape[1]
     return rotate_call(flags, ys, parts, False, blocks, specs, cols, chunk, name, deps)
 
 
-def rotate_ends_kernel(flags, y_left, y_right, lt, lb, rt, rb, l_edge, r_edge, left, right):
-    new = apply_rows(factor_stack(y_left[...]), jnp.concatenate([lt[...], lb[...]], 0))
-    left[...] = jnp.where(flags[0] != 0, l_edge[...], new)
-    new = apply_rows(factor_stack(y_right[...]), jnp.concatenate([rt[...], rb[...]], 0))
-    right[...] = jnp.where(flags[1] != 0, r_edge[...], new)
-
-
-def rotate_ends(flags, edges, left_pair, right_pair, instead, name, chunk=1024):
-    cols = instead[0].shape[1]
+def round_2_rest_kernel(flags, y_ref, y_left, y_right, *refs):
+    step = pl.program_id(0)
+    left, p0, p1, p2, p3, right = [
+        jnp.concatenate([refs[2 * k][...], refs[2 * k + 1][...]], 0) for k in range(PD + 2)
+    ]
+    r2, l1 = refs[2 * PD + 4][...], refs[2 * PD + 5][...]
+    r_left, r_0, l_0, r_1, l_2, r_3, l_3, l_right, grams, acc = refs[2 * PD + 6 :]
+
+    def rotated(y, values):
+        return apply_rows(factor_stack(y), values)
+
+    new0, new3 = rotated(y_ref[0], p0), rotated(y_ref[3], p3)
+    r0, l0, r3, l3 = new0[:B], new0[B:], new3[:B], new3[B:]
+    r1, l2 = rotated(y_ref[1][:B], p1), rotated(y_ref[2][B:], p2)
+    rl = jnp.where(flags[0] != 0, l0, rotated(y_left[...], left))
+    lr = jnp.where(flags[1] != 0, r3, rotated(y_right[...], right))
+    for ref, value in zip(
+        (r_left, r_0, l_0, r_1, l_2, r_3, l_3, l_right), (rl, r0, l0, r1, l2, r3, l3, lr)
+    ):
+        ref[...] = value
+
+    @pl.when(step == 0)
+    def _():
+        acc[...] = jnp.zeros_like(acc)
+
+    for k, (top, bottom) in enumerate([(rl, l1), (r0, l2), (r1, l3), (r2, lr)]):
+        high, low = split(jnp.concatenate([top, bottom], 0))
+        acc[k] += dot(high, jnp.concatenate([high, low], 0), NT)
+
+    @pl.when(step == pl.num_programs(0) - 1)
+    def _():
+        for k in range(PD):
+            grams[k] = finish_gram(acc[k])
+
+
+def round_2_rest(flags, y, edges, pairs, left_pair, right_pair, done, chunk=1024):
+    blocks = [*left_pair, *[x for pair in pairs for x in pair], *right_pair, *done]
+    cols = done[0].shape[1]
     spec = pl.BlockSpec((B, chunk), lambda i: (0, i))
     half = pl.BlockSpec((B, W), lambda i: (0, 0))
-    return pl.pallas_call(
-        rotate_ends_kernel,
+    whole = pl.BlockSpec((PD, W, W), lambda i: (0, 0, 0))
+    return pl.pallas_call(
+        round_2_rest_kernel,
         grid=(cols // chunk,),
-        in_specs=[SMEM_SPEC, half, half] + [spec] * 6,
-        out_specs=[spec] * 2,
-        out_shape=[jax.ShapeDtypeStruct((B, cols), F32)] * 2,
-        compiler_params=params(),
-        cost_estimate=LONG,
-        name=name,
-    )(flags, *edges, *left_pair, *right_pair, *instead)
+        in_specs=[SMEM_SPEC, whole, half, half] + [spec] * len(blocks),
+        out_specs=[spec] * 8 + [whole],
+        out_shape=[jax.ShapeDtypeStruct((B, cols), F32)] * 8
+        + [jax.ShapeDtypeStruct((PD, W, W), F32)],
+        scratch_shapes=[pltpu.VMEM((PD, W, 2 * W), F32)],
+        compiler_params=params(),
+        cost_estimate=LONG,
+        name="round_2_rest",
+    )(flags, y, *edges, *blocks)
 
 
 def final_inner_kernel(flags, y_ref, *refs):
@@ -299,7 +331,7 @@
     ]
 
 
-def final_inner(flags, y, pairs, chunk=1024):
+def final_inner(flags, y, pairs, chunk=2048):
     blocks = [x for pair in pairs for x in pair]
     cols = blocks[0].shape[1]
     spec = pl.BlockSpec((B, chunk), lambda i, flags: (0, i))
@@ -331,7 +363,7 @@
     out[:, 3 * W :] = jnp.concatenate([r_2[...], right], 0).T
 
 
-def final(flags, edges, left_pair, right_pair, done, inner, chunk=1024):
+def final(flags, edges, left_pair, right_pair, done, inner, chunk=2048):
     cols = inner.shape[0]
     spec = pl.BlockSpec((B, chunk), lambda i, flags: (0, i))
     half = pl.BlockSpec((B, W), lambda i, flags: (0, 0))
@@ -379,10 +411,8 @@
     return lax.ppermute(x, "rows", [(i, i ^ 1) for i in range(4)])
 
 
-def row_terms(mine, theirs, *deps):
+def row_terms(mine, theirs):
     near = mine + other_core(theirs)
-    if deps:
-        near = after(near, *deps)
     return near, lax.ppermute(near, "rows", [(i, i ^ 2) for i in range(4)])
 
 
@@ -393,7 +423,7 @@
     core = lax.axis_index("rows") % 2
     flags = jnp.stack([first_one, last_one, core]).astype(jnp.int32)
 
-    near, far = row_terms(*gram_rows(flags, matrix, "gram_1"))
+    near, far = row_terms(*gram_rows(matrix, "gram_1"))
     (y1,) = factors(flags, near, far, "factors_1")
     y1 = (y1, other_core(y1))
     r1_3, l1_0 = rotate_rows(flags, y1, [(3, 0), (0, 1)], matrix, "rotate_1_ends")
@@ -407,24 +437,21 @@
     in_left = jnp.where(first_one, l1_0, in_left)
     in_right = jnp.where(last_one, r1_3, in_right)
     pairs2 = [(in_left, l1_1), (r1_0, l1_2), (r1_1, l1_3), (r1_2, in_right)]
-    near, far = row_terms(*[gram_blocks(flags, pairs2, "gram_2")] * 2, in_left2)
-    l1_1 = after(l1_1, near)
+    near, far = row_terms(*[gram_blocks(pairs2, "gram_2")] * 2)
+    l1_1 = after(l1_1, near, in_left2)
     pairs2[0] = (in_left, l1_1)
     in_right2 = send_back(l1_1)
     y2, to_left, to_right = factors(flags, near, far, "factors_2")
     edges2 = (send_on(to_right), send_back(to_left))
     r2_2, l2_1 = rotate_blocks(flags, (y2,), [(2, 0), (1, 1)], pairs2, "rotate_2_ends")
     in_left3 = send_on(r2_2)
-    r2_0, l2_0, r2_3, l2_3, r2_1, l2_2 = rotate_blocks(
-        flags, (y2,), [(0, None), (3, None), (1, 0), (2, 1)], pairs2, "rotate_2_inner", edges2
+    r2_left, r2_0, l2_0, r2_1, l2_2, r2_3, l2_3, l2_right, gram = round_2_rest(
+        flags, y2, edges2, pairs2, (in_left2, l1_0), (r1_3, in_right2), (r2_2, l2_1)
     )
 
-    r2_left, l2_right = rotate_ends(
-        flags, edges2, (in_left2, l1_0), (r1_3, in_right2), (l2_0, r2_3), "ends_2"
-    )
     pairs3 = [(r2_left, l2_1), (r2_0, l2_2), (r2_1, l2_3), (r2_2, l2_right)]
-    near, far = row_terms(*[gram_blocks(flags, pairs3, "gram_3")] * 2, in_left3)
-    l2_1 = after(l2_1, near)
+    near, far = row_terms(gram, gram)
+    l2_1 = after(l2_1, near, in_left3)
     pairs3[0] = (r2_left, l2_1)
     in_right3 = send_back(l2_1)
     y3, to_left, to_right = factors(flags, near, far, "factors_3")

time: 211 us -> 198 us (0.938)
  Pallas kernels: 83.2 us -> 71.1 us
  waiting for transfers between devices: 59.8 us -> 65.1 us
  starting transfers between devices: 52 us -> 48.7 us
    ppermute x5, waiting for transfers between devices: 33.8 us -> 44.2 us  [send_on(): return lax.ppermute(x, 'pair', [(i, i + 1) for i in range(peers - 1)])]
    pallas_call x4 -> x3, Pallas kernels: 24.8 us -> 15.3 us  [rotate_call(): pl.pallas_call(functools.partial(rotate_kernel, parts, by_rows, len(ys),...]
    ppermute x3, waiting for transfers between devices: 7.86 us -> 3.45 us  [row_terms(): return (near, lax.ppermute(near, 'rows', [(i, i ^ 2) for i in range(4)]))]
    ppermute x5, starting transfers between devices: 31.5 us -> 27.5 us  [send_back(): return lax.ppermute(x, 'pair', [(i + 1, i) for i in range(peers - 1)])]
    pallas_call x4 -> x3, Pallas kernels: 24 us -> 23.1 us  [the longest x1 11.9 us: round_2_rest(): pl.pallas_call(round_2_rest_kernel, grid=(cols // chunk,), in_specs=[SMEM...]
    unnamed x28 -> x32, local copies, waits for them, and re-layouts: 6.32 us -> 5.69 us
  transfers between devices with their start and end apart: 17 -> 17, of which waited for: 13 -> 11; matrix products, arithmetic and copies ran while one was open for 3% -> 3% of each run, Pallas kernels for 28% -> 25%
where the time goes in v3:
time: 198 us
  Pallas kernels  71.1 us (36%)
  waiting for transfers between devices  65.1 us (33%)
  starting transfers between devices  48.7 us (25%)
  other arithmetic  6.93 us (4%)
  local copies, waits for them, and re-layouts  5.69 us (3%)
    ppermute x5, waiting for transfers between devices, send_on(): return lax.ppermute(x, 'pair', [(i, i + 1) for i in range(peers - 1)])  44.2 us
    ppermute x5, starting transfers between devices, send_back(): return lax.ppermute(x, 'pair', [(i + 1, i) for i in range(peers - 1)])  27.5 us
    pallas_call x3, Pallas kernels, factors(): pl.pallas_call(factors_kernel, in_specs=[SMEM_SPEC, vmem, vmem], out_spec...  16.3 us
    ppermute x5, starting transfers between devices, send_on(): return lax.ppermute(x, 'pair', [(i, i + 1) for i in range(peers - 1)])  15.6 us
    pallas_call x3, Pallas kernels, rotate_call(): pl.pallas_call(functools.partial(rotate_kernel, parts, by_rows, len(ys),...  15.3 us
    pallas_call x1, Pallas kernels, round_2_rest(): pl.pallas_call(round_2_rest_kernel, grid=(cols // chunk,), in_specs=[SMEM...  11.9 us
    pallas_call x2, Pallas kernels, gram_call(): pl.pallas_call(kernel, grid=(steps,), in_specs=specs, out_specs=[pl.Block...  11.2 us
    ppermute x5, waiting for transfers between devices, send_back(): return lax.ppermute(x, 'pair', [(i + 1, i) for i in range(peers - 1)])  10.9 us
  transfers between devices with their start and end apart: 17, of which 11 were waited for; matrix products, arithmetic and copies ran while one was open for 3% of the time, Pallas kernels for 25%

profile of v3, /device:TPU:96, one launch (start us, length us, event | category | flops | bytes accessed | tf_op | source)
XLA Modules:
  0.0 197.8 jit_solution(564983723705839207)
XLA Ops:
  0.0 5.1 %gram_1.1 = (f32[2,128,128]{2,1,0:T(8,128)}, f32[2,128,128]{2,1,0:T(8,128)}) custom-call(f32[4096,512]{1,0:T(8,128)} %refs_5_.1, f32[4096,512]{1,0:T(8,128)} %refs_5_.1, f32[4096,512]{1,0:T(8,128)} %refs_5_.1, f32[4096,512]{1,0:T(8,128)} %refs_5_.1), custom_call_target="tpu_custom_call" | custom-call | flops 10000000000 | bytes 400000000 | tf_op jit(solution)/shard_map/gram_1/pallas_call | solution.py:105
  7.6 1.6 collective-permute-start.1
  9.8 3.4 %collective-permute-done.1.b_ref = f32[2,128,128]{2,1,0:T(8,128)S(1)} collective-permute-done((f32[2,128,128]{2,1,0:T(8,128)S(1)}, f32[2,128,128]{2,1,0:T(8,128)S(1)}, u32[]{:S(2)}, u32[]{:S(2)}) %collective-permute-start.1) | collective-permute-done | bytes 131104 | tf_op jit(solution)/shard_map/ppermute | solution.py:416
  13.9 4.8 %factors_1.1.refs_0_ = f32[2,128,128]{2,1,0:T(8,128)} custom-call(s32[3]{0:T(128)} %pad_add_fusion.flags, f32[2,128,128]{2,1,0:T(8,128)} %copy-done.4, f32[2,128,128]{2,1,0:T(8,128)} %copy-done.10), custom_call_target="tpu_custom_call" | custom-call | flops 10000000000 | bytes 400000000 | tf_op jit(solution)/shard_map/factors_1/pallas_call | solution.py:182
  20.9 4.1 %rotate_1_ends.1 = (f32[64,4096]{1,0:T(8,128)}, f32[64,4096]{1,0:T(8,128)}) custom-call(s32[3]{0:T(128)} %pad_add_fusion.flags, f32[2,128,128]{2,1,0:T(8,128)} %factors_1.1.refs_0_, f32[2,128,128]{2,1,0:T(8,128)} %copy-done.11, f32[4096,512]{1,0:T(8,128)} %refs_5_.1, f32[4096,512]{1,0:T(8,128)} %refs_5_.1), custom_call_target="tpu_custom_call" | custom-call | flops 10000000000 | bytes 400000000 | tf_op jit(solution)/shard_map/rotate_1_ends/pallas_call | solution.py:224
  25.1 7.2 %collective-permute-start.4 = (f32[64,4096]{1,0:T(8,128)}, f32[64,4096]{1,0:T(8,128)}, u32[]{:S(2)}, u32[]{:S(2)}) collective-permute-start(f32[64,4096]{1,0:T(8,128)} %get-tuple-element.39.refs_1_), channel_id=1, source_target_pairs={{4,0},{8,4},{12,8},{16,12},{20,16},{24,20},{28,24},{32,28},{36,32}... | collective-permute-start | bytes 3145736 | tf_op jit(solution)/shard_map/ppermute | solution.py:395
  32.3 2.1 %collective-permute-start.3 = (f32[64,4096]{1,0:T(8,128)}, f32[64,4096]{1,0:T(8,128)S(1)}, u32[]{:S(2)}, u32[]{:S(2)}) collective-permute-start(f32[64,4096]{1,0:T(8,128)} %get-tuple-element.40.refs_10_), channel_id=1, source_target_pairs={{0,4},{4,8},{8,12},{12,16},{16,20},{20,24},{24,28},{28,32},{32,36}... | collective-permute-start | bytes 3145736 | tf_op jit(solution)/shard_map/ppermute | solution.py:390
  34.4 7.4 %rotate_1_inner.1 = (f32[64,4096]{1,0:T(8,128)}, f32[64,4096]{1,0:T(8,128)}, f32[64,4096]{1,0:T(8,128)}, f32[64,4096]{1,0:T(8,128)}, f32[64,4096]{1,0:T(8,128)}, /*index=5*/f32[64,4096]{1,0:T(8,128)}) custom-call(s32[3]{0:T(128)} %pad_add_fusion.flags, f32[2,128,128]{2,1,0:T(8,128)} %factors_1.1.refs_0_, f32[2,128,128]{2,1,0:T(8,128)} %copy-done.11, ...), custom_call_target="tpu_custom_call" | custom-call | flops 10000000000 | bytes 400000000 | tf_op jit(solution)/shard_map/rotate_1_inner/pallas_call | solution.py:224
  41.8 4.0 %collective-permute-start.9 = (f32[64,4096]{1,0:T(8,128)}, f32[64,4096]{1,0:T(8,128)}, u32[]{:S(2)}, u32[]{:S(2)}) collective-permute-start(f32[64,4096]{1,0:T(8,128)} %get-tuple-element.46.refs_6_.refs_8_), channel_id=1, source_target_pairs={{0,4},{4,8},{8,12},{12,16},{16,20},{20,24},{24,28},{28,32},{32,36}... | collective-permute-start | bytes 3145736 | tf_op jit(solution)/shard_map/ppermute | solution.py:390
  45.8 10.3 %collective-permute-done.4 = f32[64,4096]{1,0:T(8,128)} collective-permute-done((f32[64,4096]{1,0:T(8,128)}, f32[64,4096]{1,0:T(8,128)}, u32[]{:S(2)}, u32[]{:S(2)}) %collective-permute-start.4) | collective-permute-done | bytes 1048608 | tf_op jit(solution)/shard_map/ppermute | solution.py:395
  56.1 2.3 %broadcast_select_fusion.refs_7_.refs_9_ = f32[64,4096]{1,0:T(8,128)} fusion(f32[64,4096]{1,0:T(8,128)S(1)} %copy-done, f32[64,4096]{1,0:T(8,128)} %collective-permute-done.4, pred[]{:T(512)S(6)} %eq.9), kind=kLoop, calls=%fused_computation | loop fusion | flops 262144 | bytes 3145729 | tf_op jit(solution)/shard_map/jit(_where)/select_n | solution.py:438
  58.4 21.0 %collective-permute-done.3 = f32[64,4096]{1,0:T(8,128)S(1)} collective-permute-done((f32[64,4096]{1,0:T(8,128)}, f32[64,4096]{1,0:T(8,128)S(1)}, u32[]{:S(2)}, u32[]{:S(2)}) %collective-permute-start.3) | collective-permute-done | bytes 1048608 | tf_op jit(solution)/shard_map/ppermute | solution.py:390
  80.5 6.1 %gram_2.1 = f32[4,128,128]{2,1,0:T(8,128)} custom-call(f32[64,4096]{1,0:T(8,128)} %broadcast_select_fusion.1.refs_0_.refs_2_, f32[64,4096]{1,0:T(8,128)} %get-tuple-element.41.refs_1_.refs_0_, f32[64,4096]{1,0:T(8,128)} %get-tuple-element.42.refs_2_.refs_3_.refs_4_, f32[64,4096]{1,0:T(8,128)} %get-tuple-element.43.refs_3_.refs_4_.refs_5_, ...), custom_call_target="tpu_custom_call" | custom-call | flops 10000000000 | bytes 400000000 | tf_op jit(solution)/shard_map/gram_2/pallas_call | solution.py:105
  86.6 1.7 collective-permute-done.5
  89.3 1.6 collective-permute-start.6
  90.9 11.1 %collective-permute-done.9.refs_2_.refs_0_ = f32[64,4096]{1,0:T(8,128)} collective-permute-done((f32[64,4096]{1,0:T(8,128)}, f32[64,4096]{1,0:T(8,128)}, u32[]{:S(2)}, u32[]{:S(2)}) %collective-permute-start.9) | collective-permute-done | bytes 1048608 | tf_op jit(solution)/shard_map/ppermute | solution.py:390
  102.0 5.1 %collective-permute-start.10 = (f32[64,4096]{1,0:T(8,128)}, f32[64,4096]{1,0:T(8,128)S(1)}, u32[]{:S(2)}, u32[]{:S(2)}) collective-permute-start(f32[64,4096]{1,0:T(8,128)} %after.2.refs_3_), channel_id=1, source_target_pairs={{4,0},{8,4},{12,8},{16,12},{20,16},{24,20},{28,24},{32,28},{36,32}... | collective-permute-start | bytes 3145736 | tf_op jit(solution)/shard_map/ppermute | solution.py:395
  107.8 5.7 %factors_2.1 = (f32[4,128,128]{2,1,0:T(8,128)}, f32[64,128]{1,0:T(8,128)}, f32[64,128]{1,0:T(8,128)}) custom-call(s32[3]{0:T(128)} %pad_add_fusion.flags, f32[4,128,128]{2,1,0:T(8,128)} %copy-done.2, f32[4,128,128]{2,1,0:T(8,128)} %copy-done.8), custom_call_target="tpu_custom_call" | custom-call | flops 10000000000 | bytes 400000000 | tf_op jit(solution)/shard_map/factors_2/pallas_call | solution.py:182
  113.6 2.2 %collective-permute-start.7 = (f32[64,128]{1,0:T(8,128)}, f32[64,128]{1,0:T(8,128)S(1)}, u32[]{:S(2)}, u32[]{:S(2)}) collective-permute-start(f32[64,128]{1,0:T(8,128)} %get-tuple-element.48), channel_id=1, source_target_pairs={{0,4},{4,8},{8,12},{12,16},{16,20},{20,24},{24,28},{28,32},{32,36}... | collective-permute-start | bytes 98312 | tf_op jit(solution)/shard_map/ppermute | solution.py:390
  115.8 8.1 %collective-permute-start.8 = (f32[64,128]{1,0:T(8,128)}, f32[64,128]{1,0:T(8,128)S(1)}, u32[]{:S(2)}, u32[]{:S(2)}) collective-permute-start(f32[64,128]{1,0:T(8,128)} %get-tuple-element.49), channel_id=1, source_target_pairs={{4,0},{8,4},{12,8},{16,12},{20,16},{24,20},{28,24},{32,28},{36,32}... | collective-permute-start | bytes 98312 | tf_op jit(solution)/shard_map/ppermute | solution.py:395
  123.9 3.7 %rotate_2_ends.1 = (f32[64,4096]{1,0:T(8,128)}, f32[64,4096]{1,0:T(8,128)}) custom-call(s32[3]{0:T(128)} %pad_add_fusion.flags, f32[4,128,128]{2,1,0:T(8,128)} %get-tuple-element.47.refs_0_.y_ref, f32[64,4096]{1,0:T(8,128)} %get-tuple-element.44.refs_4_.refs_1_.refs_6_, f32[64,4096]{1,0:T(8,128)} %get-tuple-element.45.refs_5_.refs_2_.refs_7_, ...), custom_call_target="tpu_custom_call" | custom-call | flops 10000000000 | bytes 400000000 | tf_op jit(solution)/shard_map/rotate_2_ends/pallas_call | solution.py:224
  127.7 1.9 collective-permute-start.15
  132.1 11.9 %round_2_rest.1 = (f32[64,4096]{1,0:T(8,128)}, f32[64,4096]{1,0:T(8,128)}, f32[64,4096]{1,0:T(8,128)}, f32[64,4096]{1,0:T(8,128)}, f32[64,4096]{1,0:T(8,128)}, /...) custom-call(s32[3]{0:T(128)} %pad_add_fusion.flags, ...), custom_call_target="tpu_custom_call" | custom-call | flops 10000000000 | bytes 400000000 | tf_op jit(solution)/shard_map/round_2_rest/pallas_call | solution.py:290
  144.0 1.7 collective-permute-done.11
  146.8 2.4 %collective-permute-start.12 = (f32[4,128,128]{2,1,0:T(8,128)S(1)}, f32[4,128,128]{2,1,0:T(8,128)S(1)}, u32[]{:S(2)}, u32[]{:S(2)}) collective-permute-start(f32[4,128,128]{2,1,0:T(8,128)S(1)} %add.16.a_ref.refs_1_), channel_id=1, source_target_pairs={{0,2},{1,3},{2,0},{3,1},{4,6},{5,7},{6,4},{7,5},{8,10},{9,11},{10,... | collective-permute-start | bytes 786440 | tf_op jit(solution)/shard_map/ppermute | solution.py:416
  149.1 11.2 %collective-permute-done.15.refs_2_.lt = f32[64,4096]{1,0:T(8,128)S(1)} collective-permute-done((f32[64,4096]{1,0:T(8,128)}, f32[64,4096]{1,0:T(8,128)S(1)}, u32[]{:S(2)}, u32[]{:S(2)}) %collective-permute-start.15) | collective-permute-done | bytes 1048608 | tf_op jit(solution)/shard_map/ppermute | solution.py:390
  161.4 1.9 collective-permute-start.16
  164.0 5.8 %factors_3.1 = (f32[4,128,128]{2,1,0:T(8,128)}, f32[64,128]{1,0:T(8,128)}, f32[64,128]{1,0:T(8,128)}) custom-call(s32[3]{0:T(128)} %pad_add_fusion.flags, f32[4,128,128]{2,1,0:T(8,128)} %copy-done.3, f32[4,128,128]{2,1,0:T(8,128)} %copy-done.9), custom_call_target="tpu_custom_call" | custom-call | flops 10000000000 | bytes 400000000 | tf_op jit(solution)/shard_map/factors_3/pallas_call | solution.py:182
  169.7 5.4 %collective-permute-start.13 = (f32[64,128]{1,0:T(8,128)}, f32[64,128]{1,0:T(8,128)S(1)}, u32[]{:S(2)}, u32[]{:S(2)}) collective-permute-start(f32[64,128]{1,0:T(8,128)} %get-tuple-element.53), channel_id=1, source_target_pairs={{0,4},{4,8},{8,12},{12,16},{16,20},{20,24},{24,28},{28,32},{32,36}... | collective-permute-start | bytes 98312 | tf_op jit(solution)/shard_map/ppermute | solution.py:390
  175.2 5.1 %collective-permute-start.14 = (f32[64,128]{1,0:T(8,128)}, f32[64,128]{1,0:T(8,128)S(1)}, u32[]{:S(2)}, u32[]{:S(2)}) collective-permute-start(f32[64,128]{1,0:T(8,128)} %get-tuple-element.54), channel_id=1, source_target_pairs={{4,0},{8,4},{12,8},{16,12},{20,16},{24,20},{28,24},{32,28},{36,32}... | collective-permute-start | bytes 98312 | tf_op jit(solution)/shard_map/ppermute | solution.py:395
  180.3 8.2 %final_inner.1 = (f32[4096,256]{1,0:T(8,128)}, f32[64,4096]{1,0:T(8,128)}, f32[64,4096]{1,0:T(8,128)}, f32[64,4096]{1,0:T(8,128)}, f32[64,4096]{1,0:T(8,128)}) custom-call(s32[3]{0:T(128)} %pad_add_fusion.flags, f32[4,128,128]{2,1,0:T(8,128)} %get-tuple-element.57.y_ref, f32[64,4096]{1,0:T(8,128)} %get-tuple-element.58.refs_0_, f32[64,4096]{1,0:T(8,128)} %after.3.refs_1_, ...), custom_call_target="tpu_custom_call" | custom-call | flops 10000000000 | bytes 400000000 | tf_op jit(solution)/shard_map/final_inner/pallas_call | solution.py:340
  189.5 8.3 %final.1 = f32[4096,512]{1,0:T(8,128)} custom-call(s32[3]{0:T(128)} %pad_add_fusion.flags, f32[64,128]{1,0:T(8,128)} %copy-done.14, f32[64,128]{1,0:T(8,128)} %copy-done.15, f32[64,4096]{1,0:T(8,128)} %copy-done.5, f32[64,4096]{1,0:T(8,128)} %get-tuple-element.55.lb, f32[64,4096]{1,0:T(8,128)} %get-tuple-element.56.rt, f32[64,4096]{1,0:T(8,128)} %copy-done.7, ...), custom_call_target="tpu_custom_call" | custom-call | flops 10000000000 | bytes 400000000 | tf_op jit(solution)/shard_map/final/pallas_call | solution.py:370
  (53 shorter events, 15.0 us)
Async XLA Ops:
  5.1 1.6 collective-permute-start
  7.6 5.6 %copy-start.4 = (f32[2,128,128]{2,1,0:T(8,128)}, f32[2,128,128]{2,1,0:T(8,128)S(1)}, u32[]{:S(2)}) copy-start(f32[2,128,128]{2,1,0:T(8,128)S(1)} %add.14.a_ref) | copy-start | bytes 393220
  7.6 5.6 %collective-permute-start.1 = (f32[2,128,128]{2,1,0:T(8,128)S(1)}, f32[2,128,128]{2,1,0:T(8,128)S(1)}, u32[]{:S(2)}, u32[]{:S(2)}) collective-permute-start(f32[2,128,128]{2,1,0:T(8,128)S(1)} %add.14.a_ref), channel_id=1, source_target_pairs={{0,2},{1,3},{2,0},{3,1},{4,6},{5,7},{6,4},{7,5},{8,10},{9,11},{10,... | collective-permute-start | bytes 393224 | tf_op jit(solution)/shard_map/ppermute | solution.py:416
  13.3 0.7 copy-start.10
  18.7 1.6 collective-permute-start.2
  20.3 0.7 copy-start.11
  25.1 31.0 %collective-permute-start.4 = (f32[64,4096]{1,0:T(8,128)}, f32[64,4096]{1,0:T(8,128)}, u32[]{:S(2)}, u32[]{:S(2)}) collective-permute-start(f32[64,4096]{1,0:T(8,128)} %get-tuple-element.39.refs_1_), channel_id=1, source_target_pairs={{4,0},{8,4},{12,8},{16,12},{20,16},{24,20},{28,24},{32,28},{36,32}... | collective-permute-start | bytes 3145736 | tf_op jit(solution)/shard_map/ppermute | solution.py:395
  32.3 23.8 %copy-start = (f32[64,4096]{1,0:T(8,128)S(1)}, f32[64,4096]{1,0:T(8,128)}, u32[]{:S(2)}) copy-start(f32[64,4096]{1,0:T(8,128)} %get-tuple-element.40.refs_10_) | copy-start | bytes 3145732
  32.3 47.1 %copy-start.1 = (f32[64,4096]{1,0:T(8,128)S(1)}, f32[64,4096]{1,0:T(8,128)}, u32[]{:S(2)}) copy-start(f32[64,4096]{1,0:T(8,128)} %get-tuple-element.39.refs_1_) | copy-start | bytes 3145732
  32.3 47.1 %collective-permute-start.3 = (f32[64,4096]{1,0:T(8,128)}, f32[64,4096]{1,0:T(8,128)S(1)}, u32[]{:S(2)}, u32[]{:S(2)}) collective-permute-start(f32[64,4096]{1,0:T(8,128)} %get-tuple-element.40.refs_10_), channel_id=1, source_target_pairs={{0,4},{4,8},{8,12},{12,16},{16,20},{20,24},{24,28},{28,32},{32,36}... | collective-permute-start | bytes 3145736 | tf_op jit(solution)/shard_map/ppermute | solution.py:390
  41.8 60.2 %collective-permute-start.9 = (f32[64,4096]{1,0:T(8,128)}, f32[64,4096]{1,0:T(8,128)}, u32[]{:S(2)}, u32[]{:S(2)}) collective-permute-start(f32[64,4096]{1,0:T(8,128)} %get-tuple-element.46.refs_6_.refs_8_), channel_id=1, source_target_pairs={{0,4},{4,8},{8,12},{12,16},{16,20},{20,24},{24,28},{28,32},{32,36}... | collective-permute-start | bytes 3145736 | tf_op jit(solution)/shard_map/ppermute | solution.py:390
  86.6 1.7 collective-permute-start.5
  89.3 12.7 %copy-start.2 = (f32[4,128,128]{2,1,0:T(8,128)}, f32[4,128,128]{2,1,0:T(8,128)S(1)}, u32[]{:S(2)}) copy-start(f32[4,128,128]{2,1,0:T(8,128)S(1)} %add.15.a_ref.refs_1_) | copy-start | bytes 786436
  89.3 17.8 %collective-permute-start.6 = (f32[4,128,128]{2,1,0:T(8,128)S(1)}, f32[4,128,128]{2,1,0:T(8,128)S(1)}, u32[]{:S(2)}, u32[]{:S(2)}) collective-permute-start(f32[4,128,128]{2,1,0:T(8,128)S(1)} %add.15.a_ref.refs_1_), channel_id=1, source_target_pairs={{0,2},{1,3},{2,0},{3,1},{4,6},{5,7},{6,4},{7,5},{8,10},{9,11},{10,... | collective-permute-start | bytes 786440 | tf_op jit(solution)/shard_map/ppermute | solution.py:416
  102.0 29.1 %collective-permute-start.10 = (f32[64,4096]{1,0:T(8,128)}, f32[64,4096]{1,0:T(8,128)S(1)}, u32[]{:S(2)}, u32[]{:S(2)}) collective-permute-start(f32[64,4096]{1,0:T(8,128)} %after.2.refs_3_), channel_id=1, source_target_pairs={{4,0},{8,4},{12,8},{16,12},{20,16},{24,20},{28,24},{32,28},{36,32}... | collective-permute-start | bytes 3145736 | tf_op jit(solution)/shard_map/ppermute | solution.py:395
  107.1 0.7 copy-start.8
  113.6 16.8 %collective-permute-start.7 = (f32[64,128]{1,0:T(8,128)}, f32[64,128]{1,0:T(8,128)S(1)}, u32[]{:S(2)}, u32[]{:S(2)}) collective-permute-start(f32[64,128]{1,0:T(8,128)} %get-tuple-element.48), channel_id=1, source_target_pairs={{0,4},{4,8},{8,12},{12,16},{16,20},{20,24},{24,28},{28,32},{32,36}... | collective-permute-start | bytes 98312 | tf_op jit(solution)/shard_map/ppermute | solution.py:390
  115.8 15.2 %collective-permute-start.8 = (f32[64,128]{1,0:T(8,128)}, f32[64,128]{1,0:T(8,128)S(1)}, u32[]{:S(2)}, u32[]{:S(2)}) collective-permute-start(f32[64,128]{1,0:T(8,128)} %get-tuple-element.49), channel_id=1, source_target_pairs={{4,0},{8,4},{12,8},{16,12},{20,16},{24,20},{28,24},{32,28},{36,32}... | collective-permute-start | bytes 98312 | tf_op jit(solution)/shard_map/ppermute | solution.py:395
  127.7 32.7 %collective-permute-start.15 = (f32[64,4096]{1,0:T(8,128)}, f32[64,4096]{1,0:T(8,128)S(1)}, u32[]{:S(2)}, u32[]{:S(2)}) collective-permute-start(f32[64,4096]{1,0:T(8,128)} %get-tuple-element.50.refs_12_.refs_6_), channel_id=1, source_target_pairs={{0,4},{4,8},{8,12},{12,16},{16,20},{20,24},{24,28},{28,32},{32,36}... | collective-permute-start | bytes 3145736 | tf_op jit(solution)/shard_map/ppermute | solution.py:390
  130.4 0.6 copy-start.12
  131.1 1.0 copy-start.6
  143.9 1.8 collective-permute-start.11
  146.8 13.6 %copy-start.3 = (f32[4,128,128]{2,1,0:T(8,128)}, f32[4,128,128]{2,1,0:T(8,128)S(1)}, u32[]{:S(2)}) copy-start(f32[4,128,128]{2,1,0:T(8,128)S(1)} %add.16.a_ref.refs_1_) | copy-start | bytes 786436
  146.8 16.5 %collective-permute-start.12 = (f32[4,128,128]{2,1,0:T(8,128)S(1)}, f32[4,128,128]{2,1,0:T(8,128)S(1)}, u32[]{:S(2)}, u32[]{:S(2)}) collective-permute-start(f32[4,128,128]{2,1,0:T(8,128)S(1)} %add.16.a_ref.refs_1_), channel_id=1, source_target_pairs={{0,2},{1,3},{2,0},{3,1},{4,6},{5,7},{6,4},{7,5},{8,10},{9,11},{10,... | collective-permute-start | bytes 786440 | tf_op jit(solution)/shard_map/ppermute | solution.py:416
  160.4 1.0 copy-start.5
  161.4 27.2 %collective-permute-start.16 = (f32[64,4096]{1,0:T(8,128)}, f32[64,4096]{1,0:T(8,128)S(1)}, u32[]{:S(2)}, u32[]{:S(2)}) collective-permute-start(f32[64,4096]{1,0:T(8,128)} %after.3.refs_1_), channel_id=1, source_target_pairs={{4,0},{8,4},{12,8},{16,12},{20,16},{24,20},{28,24},{32,28},{36,32}... | collective-permute-start | bytes 3145736 | tf_op jit(solution)/shard_map/ppermute | solution.py:395
  163.3 0.7 copy-start.9
  169.7 18.7 %collective-permute-start.13 = (f32[64,128]{1,0:T(8,128)}, f32[64,128]{1,0:T(8,128)S(1)}, u32[]{:S(2)}, u32[]{:S(2)}) collective-permute-start(f32[64,128]{1,0:T(8,128)} %get-tuple-element.53), channel_id=1, source_target_pairs={{0,4},{4,8},{8,12},{12,16},{16,20},{20,24},{24,28},{28,32},{32,36}... | collective-permute-start | bytes 98312 | tf_op jit(solution)/shard_map/ppermute | solution.py:390
  175.2 13.3 %collective-permute-start.14 = (f32[64,128]{1,0:T(8,128)}, f32[64,128]{1,0:T(8,128)S(1)}, u32[]{:S(2)}, u32[]{:S(2)}) collective-permute-start(f32[64,128]{1,0:T(8,128)} %get-tuple-element.54), channel_id=1, source_target_pairs={{4,0},{8,4},{12,8},{16,12},{20,16},{24,20},{28,24},{32,28},{36,32}... | collective-permute-start | bytes 98312 | tf_op jit(solution)/shard_map/ppermute | solution.py:395
  188.5 0.6 copy-start.14
  188.5 0.6 copy-start.15
  188.5 1.0 copy-start.7
  (1 other events, 0.6 us)

commit v4 on v3

--- a/solution.py
+++ b/solution.py
@@ -109,7 +109,7 @@
         out_specs=[pl.BlockSpec((n, W, W), lambda i: (0, 0, 0)) for n in counts],
         out_shape=[jax.ShapeDtypeStruct((n, W, W), F32) for n in counts],
         scratch_shapes=[pltpu.VMEM((PD, W, 2 * W), F32)],
-        compiler_params=params(),
+        compiler_params=params(56),
         cost_estimate=LONG,
         name=name,
     )(*operands)
@@ -184,7 +184,7 @@
         in_specs=[SMEM_SPEC, vmem, vmem],
         out_specs=[vmem] * (1 + edges),
         out_shape=[jax.ShapeDtypeStruct(a.shape, F32)] + [jax.ShapeDtypeStruct((B, W), F32)] * edges,
-        compiler_params=params(),
+        compiler_params=params(40),
         cost_estimate=LONG,
         name=name,
     )(flags, a, b)
@@ -227,7 +227,7 @@
         in_specs=[SMEM_SPEC] + [whole] * len(ys) + specs + [ANY_SPEC] * len(deps),
         out_specs=[pl.BlockSpec((B, chunk), lambda i: (0, i))] * count,
         out_shape=[jax.ShapeDtypeStruct((B, cols), F32)] * count,
-        compiler_params=params(),
+        compiler_params=params(56),
         cost_estimate=LONG,
         name=name,
     )(flags, *ys, *operands, *deps)

time: 198 us -> 195 us (0.985)
  Pallas kernels: 71.1 us -> 67.5 us
  local copies, waits for them, and re-layouts: 5.69 us -> 7.96 us
    pallas_call x3, Pallas kernels: 16.3 us -> 12.7 us  [factors(): pl.pallas_call(factors_kernel, in_specs=[SMEM_SPEC, vmem, vmem], out_spec...]
    unnamed x32 -> x42, local copies, waits for them, and re-layouts: 5.69 us -> 7.96 us
  transfers between devices with their start and end apart: 17 -> 17, of which waited for: 11 -> 11; matrix products, arithmetic and copies ran while one was open for 3% -> 2% of each run, Pallas kernels for 25% -> 24%
where the time goes in v4:
time: 195 us; the launch traced here: 194 us
  Pallas kernels  67.5 us (35%)
  waiting for transfers between devices  64.6 us (33%)
  starting transfers between devices  48.7 us (25%)
  local copies, waits for them, and re-layouts  7.96 us (4%)
  other arithmetic  5.19 us (3%)
    ppermute x5, waiting for transfers between devices, send_on(): return lax.ppermute(x, 'pair', [(i, i + 1) for i in range(peers - 1)])  43.2 us
    ppermute x5, starting transfers between devices, send_back(): return lax.ppermute(x, 'pair', [(i + 1, i) for i in range(peers - 1)])  28.7 us
    pallas_call x3, Pallas kernels, rotate_call(): pl.pallas_call(functools.partial(rotate_kernel, parts, by_rows, len(ys),...  15.3 us
    ppermute x5, starting transfers between devices, send_on(): return lax.ppermute(x, 'pair', [(i, i + 1) for i in range(peers - 1)])  15 us
    pallas_call x3, Pallas kernels, factors(): pl.pallas_call(factors_kernel, in_specs=[SMEM_SPEC, vmem, vmem], out_spec...  12.7 us
    pallas_call x1, Pallas kernels, round_2_rest(): pl.pallas_call(round_2_rest_kernel, grid=(cols // chunk,), in_specs=[SMEM...  11.9 us
    pallas_call x2, Pallas kernels, gram_call(): pl.pallas_call(kernel, grid=(steps,), in_specs=specs, out_specs=[pl.Block...  11.2 us
    ppermute x5, waiting for transfers between devices, send_back(): return lax.ppermute(x, 'pair', [(i + 1, i) for i in range(peers - 1)])  11 us
  transfers between devices with their start and end apart: 17, of which 11 were waited for; matrix products, arithmetic and copies ran while one was open for 2% of the time, Pallas kernels for 24%

profile of v4, /device:TPU:96, one launch (start us, length us, event | category | flops | bytes accessed | tf_op | source)
XLA Modules:
  0.0 194.2 jit_solution(11229516247187287079)
XLA Ops:
  0.0 5.1 %gram_1.1 = (f32[2,128,128]{2,1,0:T(8,128)}, f32[2,128,128]{2,1,0:T(8,128)}) custom-call(f32[4096,512]{1,0:T(8,128)} %refs_5_.1, f32[4096,512]{1,0:T(8,128)} %refs_5_.1, f32[4096,512]{1,0:T(8,128)} %refs_5_.1, f32[4096,512]{1,0:T(8,128)} %refs_5_.1), custom_call_target="tpu_custom_call" | custom-call | flops 10000000000 | bytes 400000000 | tf_op jit(solution)/shard_map/gram_1/pallas_call | solution.py:105
  7.6 1.6 collective-permute-start.1
  9.3 4.0 %collective-permute-done.1.b_ref = f32[2,128,128]{2,1,0:T(8,128)S(1)} collective-permute-done((f32[2,128,128]{2,1,0:T(8,128)S(1)}, f32[2,128,128]{2,1,0:T(8,128)S(1)}, u32[]{:S(2)}, u32[]{:S(2)}) %collective-permute-start.1) | collective-permute-done | bytes 131104 | tf_op jit(solution)/shard_map/ppermute | solution.py:416
  13.2 3.7 %factors_1.1.refs_0_ = f32[2,128,128]{2,1,0:T(8,128)S(1)} custom-call(s32[3]{0:T(128)S(1)} %pad_add_fusion.flags, f32[2,128,128]{2,1,0:T(8,128)S(1)} %add.14.a_ref, f32[2,128,128]{2,1,0:T(8,128)S(1)} %collective-permute-done.1.b_ref), custom_call_target="tpu_custom_call" | custom-call | flops 10000000000 | bytes 400000000 | tf_op jit(solution)/shard_map/factors_1/pallas_call | solution.py:182
  19.1 4.1 %rotate_1_ends.1 = (f32[64,4096]{1,0:T(8,128)}, f32[64,4096]{1,0:T(8,128)}) custom-call(s32[3]{0:T(128)} %copy-done.4, f32[2,128,128]{2,1,0:T(8,128)} %copy-done.7, f32[2,128,128]{2,1,0:T(8,128)} %copy-done.16, f32[4096,512]{1,0:T(8,128)} %refs_5_.1, f32[4096,512]{1,0:T(8,128)} %refs_5_.1), custom_call_target="tpu_custom_call" | custom-call | flops 10000000000 | bytes 400000000 | tf_op jit(solution)/shard_map/rotate_1_ends/pallas_call | solution.py:224
  23.2 7.2 %collective-permute-start.4 = (f32[64,4096]{1,0:T(8,128)}, f32[64,4096]{1,0:T(8,128)S(1)}, u32[]{:S(2)}, u32[]{:S(2)}) collective-permute-start(f32[64,4096]{1,0:T(8,128)} %get-tuple-element.39.refs_1_), channel_id=1, source_target_pairs={{4,0},{8,4},{12,8},{16,12},{20,16},{24,20},{28,24},{32,28},{36,32}... | collective-permute-start | bytes 3145736 | tf_op jit(solution)/shard_map/ppermute | solution.py:395
  30.4 2.1 %collective-permute-start.3 = (f32[64,4096]{1,0:T(8,128)}, f32[64,4096]{1,0:T(8,128)S(1)}, u32[]{:S(2)}, u32[]{:S(2)}) collective-permute-start(f32[64,4096]{1,0:T(8,128)} %get-tuple-element.40.refs_10_), channel_id=1, source_target_pairs={{0,4},{4,8},{8,12},{12,16},{16,20},{20,24},{24,28},{28,32},{32,36}... | collective-permute-start | bytes 3145736 | tf_op jit(solution)/shard_map/ppermute | solution.py:390
  32.5 7.4 %rotate_1_inner.1 = (f32[64,4096]{1,0:T(8,128)}, f32[64,4096]{1,0:T(8,128)}, f32[64,4096]{1,0:T(8,128)}, f32[64,4096]{1,0:T(8,128)}, f32[64,4096]{1,0:T(8,128)}, /*index=5*/f32[64,4096]{1,0:T(8,128)}) custom-call(s32[3]{0:T(128)} %copy-done.4, f32[2,128,128]{2,1,0:T(8,128)} %copy-done.7, f32[2,128,128]{2,1,0:T(8,128)} %copy-done.16, f32[4096,512]{1,0:T(8,128)} %refs_5_.1, ...), custom_call_target="tpu_custom_call" | custom-call | flops 10000000000 | bytes 400000000 | tf_op jit(solution)/shard_map/rotate_1_inner/pallas_call | solution.py:224
  39.9 4.0 %collective-permute-start.9 = (f32[64,4096]{1,0:T(8,128)}, f32[64,4096]{1,0:T(8,128)S(1)}, u32[]{:S(2)}, u32[]{:S(2)}) collective-permute-start(f32[64,4096]{1,0:T(8,128)} %get-tuple-element.46.refs_6_.refs_8_), channel_id=1, source_target_pairs={{0,4},{4,8},{8,12},{12,16},{16,20},{20,24},{24,28},{28,32},{32,36}... | collective-permute-start | bytes 3145736 | tf_op jit(solution)/shard_map/ppermute | solution.py:390
  43.9 10.3 %collective-permute-done.4 = f32[64,4096]{1,0:T(8,128)S(1)} collective-permute-done((f32[64,4096]{1,0:T(8,128)}, f32[64,4096]{1,0:T(8,128)S(1)}, u32[]{:S(2)}, u32[]{:S(2)}) %collective-permute-start.4) | collective-permute-done | bytes 1048608 | tf_op jit(solution)/shard_map/ppermute | solution.py:395
  55.3 22.2 %collective-permute-done.3 = f32[64,4096]{1,0:T(8,128)S(1)} collective-permute-done((f32[64,4096]{1,0:T(8,128)}, f32[64,4096]{1,0:T(8,128)S(1)}, u32[]{:S(2)}, u32[]{:S(2)}) %collective-permute-start.3) | collective-permute-done | bytes 1048608 | tf_op jit(solution)/shard_map/ppermute | solution.py:390
  78.7 6.1 %gram_2.1 = f32[4,128,128]{2,1,0:T(8,128)} custom-call(f32[64,4096]{1,0:T(8,128)} %broadcast_select_fusion.1.refs_0_.refs_2_, f32[64,4096]{1,0:T(8,128)} %get-tuple-element.41.refs_1_.refs_0_, f32[64,4096]{1,0:T(8,128)} %get-tuple-element.42.refs_2_.refs_3_.refs_4_, f32[64,4096]{1,0:T(8,128)} %get-tuple-element.43.refs_3_.refs_4_.refs_5_, ...), custom_call_target="tpu_custom_call" | custom-call | flops 10000000000 | bytes 400000000 | tf_op jit(solution)/shard_map/gram_2/pallas_call | solution.py:105
  84.7 1.7 collective-permute-done.5
  87.5 1.6 collective-permute-start.6
  89.0 11.0 %collective-permute-done.9.refs_2_.refs_0_ = f32[64,4096]{1,0:T(8,128)S(1)} collective-permute-done((f32[64,4096]{1,0:T(8,128)}, f32[64,4096]{1,0:T(8,128)S(1)}, u32[]{:S(2)}, u32[]{:S(2)}) %collective-permute-start.9) | collective-permute-done | bytes 1048608 | tf_op jit(solution)/shard_map/ppermute | solution.py:390
  101.0 5.1 %collective-permute-start.10 = (f32[64,4096]{1,0:T(8,128)}, f32[64,4096]{1,0:T(8,128)S(1)}, u32[]{:S(2)}, u32[]{:S(2)}) collective-permute-start(f32[64,4096]{1,0:T(8,128)} %after.2.refs_3_), channel_id=1, source_target_pairs={{4,0},{8,4},{12,8},{16,12},{20,16},{24,20},{28,24},{32,28},{36,32}... | collective-permute-start | bytes 3145736 | tf_op jit(solution)/shard_map/ppermute | solution.py:395
  107.1 4.5 %factors_2.1 = (f32[4,128,128]{2,1,0:T(8,128)S(1)}, f32[64,128]{1,0:T(8,128)S(1)}, f32[64,128]{1,0:T(8,128)S(1)}) custom-call(s32[3]{0:T(128)S(1)} %copy-done.5, f32[4,128,128]{2,1,0:T(8,128)S(1)} %copy-done.1, f32[4,128,128]{2,1,0:T(8,128)S(1)} %collective-permute-done.6.b_ref), custom_call_target="tpu_custom_call" | custom-call | flops 10000000000 | bytes 400000000 | tf_op jit(solution)/shard_map/factors_2/pallas_call | solution.py:182
  112.3 2.2 %collective-permute-start.7 = (f32[64,128]{1,0:T(8,128)S(1)}, f32[64,128]{1,0:T(8,128)S(1)}, u32[]{:S(2)}, u32[]{:S(2)}) collective-permute-start(f32[64,128]{1,0:T(8,128)S(1)} %get-tuple-element.48), channel_id=1, source_target_pairs={{0,4},{4,8},{8,12},{12,16},{16,20},{20,24},{24,28},{28,32},{32,36}... | collective-permute-start | bytes 98312 | tf_op jit(solution)/shard_map/ppermute | solution.py:390
  114.5 8.1 %collective-permute-start.8 = (f32[64,128]{1,0:T(8,128)S(1)}, f32[64,128]{1,0:T(8,128)S(1)}, u32[]{:S(2)}, u32[]{:S(2)}) collective-permute-start(f32[64,128]{1,0:T(8,128)S(1)} %get-tuple-element.49), channel_id=1, source_target_pairs={{4,0},{8,4},{12,8},{16,12},{20,16},{24,20},{28,24},{32,28},{36,32}... | collective-permute-start | bytes 98312 | tf_op jit(solution)/shard_map/ppermute | solution.py:395
  122.7 3.8 %rotate_2_ends.1 = (f32[64,4096]{1,0:T(8,128)}, f32[64,4096]{1,0:T(8,128)}) custom-call(s32[3]{0:T(128)} %copy-done.4, f32[4,128,128]{2,1,0:T(8,128)} %copy-done.8, f32[64,4096]{1,0:T(8,128)} %get-tuple-element.44.refs_4_.refs_1_.refs_6_, f32[64,4096]{1,0:T(8,128)} %get-tuple-element.45.refs_5_.refs_2_.refs_7_, ...), custom_call_target="tpu_custom_call" | custom-call | flops 10000000000 | bytes 400000000 | tf_op jit(solution)/shard_map/rotate_2_ends/pallas_call | solution.py:224
  126.4 1.9 collective-permute-start.15
  128.3 1.9 collective-permute-done.7.y_left
  131.9 11.9 %round_2_rest.1 = (f32[64,4096]{1,0:T(8,128)}, f32[64,4096]{1,0:T(8,128)}, f32[64,4096]{1,0:T(8,128)}, f32[64,4096]{1,0:T(8,128)}, f32[64,4096]{1,0:T(8,128)}, /...) custom-call(s32[3]{0:T(128)} %copy-done.4, f32[4,128,128]{2,1,0:T(8,128)} %copy-done.8, ...), custom_call_target="tpu_custom_call" | custom-call | flops 10000000000 | bytes 400000000 | tf_op jit(solution)/shard_map/round_2_rest/pallas_call | solution.py:290
  143.9 1.7 collective-permute-done.11
  146.7 1.7 collective-permute-start.12
  148.4 8.1 %collective-permute-done.15.refs_2_.lt = f32[64,4096]{1,0:T(8,128)S(1)} collective-permute-done((f32[64,4096]{1,0:T(8,128)}, f32[64,4096]{1,0:T(8,128)S(1)}, u32[]{:S(2)}, u32[]{:S(2)}) %collective-permute-start.15) | collective-permute-done | bytes 1048608 | tf_op jit(solution)/shard_map/ppermute | solution.py:390
  157.6 2.5 %collective-permute-start.16 = (f32[64,4096]{1,0:T(8,128)}, f32[64,4096]{1,0:T(8,128)S(1)}, u32[]{:S(2)}, u32[]{:S(2)}) collective-permute-start(f32[64,4096]{1,0:T(8,128)} %after.3.refs_1_), channel_id=1, source_target_pairs={{4,0},{8,4},{12,8},{16,12},{20,16},{24,20},{28,24},{32,28},{36,32}... | collective-permute-start | bytes 3145736 | tf_op jit(solution)/shard_map/ppermute | solution.py:395
  161.1 4.5 %factors_3.1 = (f32[4,128,128]{2,1,0:T(8,128)S(1)}, f32[64,128]{1,0:T(8,128)S(1)}, f32[64,128]{1,0:T(8,128)S(1)}) custom-call(s32[3]{0:T(128)S(1)} %copy-done.6, f32[4,128,128]{2,1,0:T(8,128)S(1)} %copy-done.3, f32[4,128,128]{2,1,0:T(8,128)S(1)} %collective-permute-done.12.b_ref), custom_call_target="tpu_custom_call" | custom-call | flops 10000000000 | bytes 400000000 | tf_op jit(solution)/shard_map/factors_3/pallas_call | solution.py:182
  166.3 4.8 %collective-permute-start.13 = (f32[64,128]{1,0:T(8,128)S(1)}, f32[64,128]{1,0:T(8,128)S(1)}, u32[]{:S(2)}, u32[]{:S(2)}) collective-permute-start(f32[64,128]{1,0:T(8,128)S(1)} %get-tuple-element.53), channel_id=1, source_target_pairs={{0,4},{4,8},{8,12},{12,16},{16,20},{20,24},{24,28},{28,32},{32,36}... | collective-permute-start | bytes 98312 | tf_op jit(solution)/shard_map/ppermute | solution.py:390
  171.1 5.7 %collective-permute-start.14 = (f32[64,128]{1,0:T(8,128)S(1)}, f32[64,128]{1,0:T(8,128)S(1)}, u32[]{:S(2)}, u32[]{:S(2)}) collective-permute-start(f32[64,128]{1,0:T(8,128)S(1)} %get-tuple-element.54), channel_id=1, source_target_pairs={{4,0},{8,4},{12,8},{16,12},{20,16},{24,20},{28,24},{32,28},{36,32}... | collective-permute-start | bytes 98312 | tf_op jit(solution)/shard_map/ppermute | solution.py:395
  176.9 8.1 %final_inner.1 = (f32[4096,256]{1,0:T(8,128)}, f32[64,4096]{1,0:T(8,128)}, f32[64,4096]{1,0:T(8,128)}, f32[64,4096]{1,0:T(8,128)}, f32[64,4096]{1,0:T(8,128)}) custom-call(s32[3]{0:T(128)} %copy-done.4, f32[4,128,128]{2,1,0:T(8,128)} %copy-done.9, f32[64,4096]{1,0:T(8,128)} %get-tuple-element.58.refs_0_, f32[64,4096]{1,0:T(8,128)} %after.3.refs_1_, ...), custom_call_target="tpu_custom_call" | custom-call | flops 10000000000 | bytes 400000000 | tf_op jit(solution)/shard_map/final_inner/pallas_call | solution.py:340
  186.0 8.2 %final.1 = f32[4096,512]{1,0:T(8,128)} custom-call(s32[3]{0:T(128)} %copy-done.4, f32[64,128]{1,0:T(8,128)} %copy-done.19, f32[64,128]{1,0:T(8,128)} %copy-done.20, f32[64,4096]{1,0:T(8,128)} %copy-done.12, f32[64,4096]{1,0:T(8,128)} %get-tuple-element.55.lb, f32[64,4096]{1,0:T(8,128)} %get-tuple-element.56.rt, f32[64,4096]{1,0:T(8,128)} %copy-done.15, ...), custom_call_target="tpu_custom_call" | custom-call | flops 10000000000 | bytes 400000000 | tf_op jit(solution)/shard_map/final/pallas_call | solution.py:370
  (63 shorter events, 16.9 us)
Async XLA Ops:
  5.1 1.6 collective-permute-start
  7.6 5.6 %collective-permute-start.1 = (f32[2,128,128]{2,1,0:T(8,128)S(1)}, f32[2,128,128]{2,1,0:T(8,128)S(1)}, u32[]{:S(2)}, u32[]{:S(2)}) collective-permute-start(f32[2,128,128]{2,1,0:T(8,128)S(1)} %add.14.a_ref), channel_id=1, source_target_pairs={{0,2},{1,3},{2,0},{3,1},{4,6},{5,7},{6,4},{7,5},{8,10},{9,11},{10,... | collective-permute-start | bytes 393224 | tf_op jit(solution)/shard_map/ppermute | solution.py:416
  9.3 7.7 %copy-start.4 = (s32[3]{0:T(128)}, s32[3]{0:T(128)S(1)}, u32[]{:S(2)}) copy-start(s32[3]{0:T(128)S(1)} %pad_add_fusion.flags) | copy-start | bytes 40
  17.0 1.4 copy-start.7
  17.0 1.4 collective-permute-start.2
  23.2 31.0 %collective-permute-start.4 = (f32[64,4096]{1,0:T(8,128)}, f32[64,4096]{1,0:T(8,128)S(1)}, u32[]{:S(2)}, u32[]{:S(2)}) collective-permute-start(f32[64,4096]{1,0:T(8,128)} %get-tuple-element.39.refs_1_), channel_id=1, source_target_pairs={{4,0},{8,4},{12,8},{16,12},{20,16},{24,20},{28,24},{32,28},{36,32}... | collective-permute-start | bytes 3145736 | tf_op jit(solution)/shard_map/ppermute | solution.py:395
  30.4 23.8 %copy-start.10 = (f32[64,4096]{1,0:T(8,128)S(1)}, f32[64,4096]{1,0:T(8,128)}, u32[]{:S(2)}) copy-start(f32[64,4096]{1,0:T(8,128)} %get-tuple-element.40.refs_10_) | copy-start | bytes 3145732
  30.4 47.1 %copy-start.11 = (f32[64,4096]{1,0:T(8,128)S(1)}, f32[64,4096]{1,0:T(8,128)}, u32[]{:S(2)}) copy-start(f32[64,4096]{1,0:T(8,128)} %get-tuple-element.39.refs_1_) | copy-start | bytes 3145732
  30.4 47.1 %collective-permute-start.3 = (f32[64,4096]{1,0:T(8,128)}, f32[64,4096]{1,0:T(8,128)S(1)}, u32[]{:S(2)}, u32[]{:S(2)}) collective-permute-start(f32[64,4096]{1,0:T(8,128)} %get-tuple-element.40.refs_10_), channel_id=1, source_target_pairs={{0,4},{4,8},{8,12},{12,16},{16,20},{20,24},{24,28},{28,32},{32,36}... | collective-permute-start | bytes 3145736 | tf_op jit(solution)/shard_map/ppermute | solution.py:390
  39.9 60.1 %collective-permute-start.9 = (f32[64,4096]{1,0:T(8,128)}, f32[64,4096]{1,0:T(8,128)S(1)}, u32[]{:S(2)}, u32[]{:S(2)}) collective-permute-start(f32[64,4096]{1,0:T(8,128)} %get-tuple-element.46.refs_6_.refs_8_), channel_id=1, source_target_pairs={{0,4},{4,8},{8,12},{12,16},{16,20},{20,24},{24,28},{28,32},{32,36}... | collective-permute-start | bytes 3145736 | tf_op jit(solution)/shard_map/ppermute | solution.py:390
  84.7 1.7 collective-permute-start.5
  87.5 12.6 %copy-start = (f32[4,128,128]{2,1,0:T(8,128)}, f32[4,128,128]{2,1,0:T(8,128)S(1)}, u32[]{:S(2)}) copy-start(f32[4,128,128]{2,1,0:T(8,128)S(1)} %add.15.a_ref.refs_1_) | copy-start | bytes 786436
  87.5 18.6 %copy-start.5 = (s32[3]{0:T(128)S(1)}, s32[3]{0:T(128)}, u32[]{:S(2)}) copy-start(s32[3]{0:T(128)} %copy-done.4) | copy-start | bytes 40
  87.5 18.6 %collective-permute-start.6 = (f32[4,128,128]{2,1,0:T(8,128)S(1)}, f32[4,128,128]{2,1,0:T(8,128)S(1)}, u32[]{:S(2)}, u32[]{:S(2)}) collective-permute-start(f32[4,128,128]{2,1,0:T(8,128)S(1)} %add.15.a_ref.refs_1_), channel_id=1, source_target_pairs={{0,2},{1,3},{2,0},{3,1},{4,6},{5,7},{6,4},{7,5},{8,10},{9,11},{10,... | collective-permute-start | bytes 786440 | tf_op jit(solution)/shard_map/ppermute | solution.py:416
  100.0 1.0 copy-start.13
  101.0 30.0 %collective-permute-start.10 = (f32[64,4096]{1,0:T(8,128)}, f32[64,4096]{1,0:T(8,128)S(1)}, u32[]{:S(2)}, u32[]{:S(2)}) collective-permute-start(f32[64,4096]{1,0:T(8,128)} %after.2.refs_3_), channel_id=1, source_target_pairs={{4,0},{8,4},{12,8},{16,12},{20,16},{24,20},{28,24},{32,28},{36,32}... | collective-permute-start | bytes 3145736 | tf_op jit(solution)/shard_map/ppermute | solution.py:395
  106.1 1.0 copy-start.1
  112.3 17.9 %collective-permute-start.7 = (f32[64,128]{1,0:T(8,128)S(1)}, f32[64,128]{1,0:T(8,128)S(1)}, u32[]{:S(2)}, u32[]{:S(2)}) collective-permute-start(f32[64,128]{1,0:T(8,128)S(1)} %get-tuple-element.48), channel_id=1, source_target_pairs={{0,4},{4,8},{8,12},{12,16},{16,20},{20,24},{24,28},{28,32},{32,36}... | collective-permute-start | bytes 98312 | tf_op jit(solution)/shard_map/ppermute | solution.py:390
  114.5 16.4 %collective-permute-start.8 = (f32[64,128]{1,0:T(8,128)S(1)}, f32[64,128]{1,0:T(8,128)S(1)}, u32[]{:S(2)}, u32[]{:S(2)}) collective-permute-start(f32[64,128]{1,0:T(8,128)S(1)} %get-tuple-element.49), channel_id=1, source_target_pairs={{4,0},{8,4},{12,8},{16,12},{20,16},{24,20},{28,24},{32,28},{36,32}... | collective-permute-start | bytes 98312 | tf_op jit(solution)/shard_map/ppermute | solution.py:395
  126.4 30.1 %collective-permute-start.15 = (f32[64,4096]{1,0:T(8,128)}, f32[64,4096]{1,0:T(8,128)S(1)}, u32[]{:S(2)}, u32[]{:S(2)}) collective-permute-start(f32[64,4096]{1,0:T(8,128)} %get-tuple-element.50.refs_12_.refs_6_), channel_id=1, source_target_pairs={{0,4},{4,8},{8,12},{12,16},{16,20},{20,24},{24,28},{28,32},{32,36}... | collective-permute-start | bytes 3145736 | tf_op jit(solution)/shard_map/ppermute | solution.py:390
  130.2 0.7 copy-start.17
  130.9 1.0 copy-start.14
  143.9 1.8 collective-permute-start.11
  146.7 9.9 %copy-start.2 = (f32[4,128,128]{2,1,0:T(8,128)}, f32[4,128,128]{2,1,0:T(8,128)S(1)}, u32[]{:S(2)}) copy-start(f32[4,128,128]{2,1,0:T(8,128)S(1)} %add.16.a_ref.refs_1_) | copy-start | bytes 786436
  146.7 13.5 %copy-start.6 = (s32[3]{0:T(128)S(1)}, s32[3]{0:T(128)}, u32[]{:S(2)}) copy-start(s32[3]{0:T(128)} %copy-done.4) | copy-start | bytes 40
  146.7 13.4 %collective-permute-start.12 = (f32[4,128,128]{2,1,0:T(8,128)S(1)}, f32[4,128,128]{2,1,0:T(8,128)S(1)}, u32[]{:S(2)}, u32[]{:S(2)}) collective-permute-start(f32[4,128,128]{2,1,0:T(8,128)S(1)} %add.16.a_ref.refs_1_), channel_id=1, source_target_pairs={{0,2},{1,3},{2,0},{3,1},{4,6},{5,7},{6,4},{7,5},{8,10},{9,11},{10,... | collective-permute-start | bytes 786440 | tf_op jit(solution)/shard_map/ppermute | solution.py:416
  156.5 1.1 copy-start.12
  157.6 27.5 %collective-permute-start.16 = (f32[64,4096]{1,0:T(8,128)}, f32[64,4096]{1,0:T(8,128)S(1)}, u32[]{:S(2)}, u32[]{:S(2)}) collective-permute-start(f32[64,4096]{1,0:T(8,128)} %after.3.refs_1_), channel_id=1, source_target_pairs={{4,0},{8,4},{12,8},{16,12},{20,16},{24,20},{28,24},{32,28},{36,32}... | collective-permute-start | bytes 3145736 | tf_op jit(solution)/shard_map/ppermute | solution.py:395
  160.1 1.0 copy-start.3
  166.3 18.7 %collective-permute-start.13 = (f32[64,128]{1,0:T(8,128)S(1)}, f32[64,128]{1,0:T(8,128)S(1)}, u32[]{:S(2)}, u32[]{:S(2)}) collective-permute-start(f32[64,128]{1,0:T(8,128)S(1)} %get-tuple-element.53), channel_id=1, source_target_pairs={{0,4},{4,8},{8,12},{12,16},{16,20},{20,24},{24,28},{28,32},{32,36}... | collective-permute-start | bytes 98312 | tf_op jit(solution)/shard_map/ppermute | solution.py:390
  171.1 13.9 %collective-permute-start.14 = (f32[64,128]{1,0:T(8,128)S(1)}, f32[64,128]{1,0:T(8,128)S(1)}, u32[]{:S(2)}, u32[]{:S(2)}) collective-permute-start(f32[64,128]{1,0:T(8,128)S(1)} %get-tuple-element.54), channel_id=1, source_target_pairs={{4,0},{8,4},{12,8},{16,12},{20,16},{24,20},{28,24},{32,28},{36,32}... | collective-permute-start | bytes 98312 | tf_op jit(solution)/shard_map/ppermute | solution.py:395
  185.1 1.0 copy-start.15
  (6 other events, 3.9 us)

commit v5 on v4

--- a/solution.py
+++ b/solution.py
@@ -109,7 +109,7 @@
         out_specs=[pl.BlockSpec((n, W, W), lambda i: (0, 0, 0)) for n in counts],
         out_shape=[jax.ShapeDtypeStruct((n, W, W), F32) for n in counts],
         scratch_shapes=[pltpu.VMEM((PD, W, 2 * W), F32)],
-        compiler_params=params(56),
+        compiler_params=params(52),
         cost_estimate=LONG,
         name=name,
     )(*operands)

time: 195 us -> 194 us (level)
  waiting for transfers between devices: 64.6 us -> 68.4 us
  other arithmetic: 5.19 us -> 2.33 us
    ppermute x5, waiting for transfers between devices: 43.2 us -> 47.4 us  [send_on(): return lax.ppermute(x, 'pair', [(i, i + 1) for i in range(peers - 1)])]
  transfers between devices with their start and end apart: 17 -> 17, of which waited for: 11 -> 11; matrix products, arithmetic and copies ran while one was open for 2% -> 1% of each run, Pallas kernels for 24% -> 24%
where the time goes in v5:
time: 194 us; the launch traced here: 193 us
  waiting for transfers between devices  68.4 us (35%)
  Pallas kernels  66.3 us (34%)
  starting transfers between devices  49 us (25%)
  local copies, waits for them, and re-layouts  6.95 us (4%)
  other arithmetic  2.33 us (1%)
    ppermute x5, waiting for transfers between devices, send_on(): return lax.ppermute(x, 'pair', [(i, i + 1) for i in range(peers - 1)])  47.4 us
    ppermute x5, starting transfers between devices, send_back(): return lax.ppermute(x, 'pair', [(i + 1, i) for i in range(peers - 1)])  27.4 us
    ppermute x5, starting transfers between devices, send_on(): return lax.ppermute(x, 'pair', [(i, i + 1) for i in range(peers - 1)])  15.7 us
    pallas_call x3, Pallas kernels, rotate_call(): pl.pallas_call(functools.partial(rotate_kernel, parts, by_rows, len(ys),...  15.2 us
    pallas_call x3, Pallas kernels, factors(): pl.pallas_call(factors_kernel, in_specs=[SMEM_SPEC, vmem, vmem], out_spec...  12.7 us
    pallas_call x1, Pallas kernels, round_2_rest(): pl.pallas_call(round_2_rest_kernel, grid=(cols // chunk,), in_specs=[SMEM...  11.9 us
    ppermute x5, waiting for transfers between devices, send_back(): return lax.ppermute(x, 'pair', [(i + 1, i) for i in range(peers - 1)])  11 us
    pallas_call x2, Pallas kernels, gram_call(): pl.pallas_call(kernel, grid=(steps,), in_specs=specs, out_specs=[pl.Block...  10.1 us
  transfers between devices with their start and end apart: 17, of which 11 were waited for; matrix products, arithmetic and copies ran while one was open for 1% of the time, Pallas kernels for 24%

profile of v5, /device:TPU:96, one launch (start us, length us, event | category | flops | bytes accessed | tf_op | source)
XLA Modules:
  0.0 193.4 jit_solution(11096013900561456399)
XLA Ops:
  0.0 4.5 %gram_1.1 = (f32[2,128,128]{2,1,0:T(8,128)S(1)}, f32[2,128,128]{2,1,0:T(8,128)S(1)}) custom-call(f32[4096,512]{1,0:T(8,128)} %refs_5_.1, f32[4096,512]{1,0:T(8,128)} %refs_5_.1, f32[4096,512]{1,0:T(8,128)} %refs_5_.1, f32[4096,512]{1,0:T(8,128)} %refs_5_.1), custom_call_target="tpu_custom_call" | custom-call | flops 10000000000 | bytes 400000000 | tf_op jit(solution)/shard_map/gram_1/pallas_call | solution.py:105
  4.6 1.3 collective-permute-done
  5.9 1.6 collective-permute-start.1
  7.6 4.0 %collective-permute-done.1.b_ref = f32[2,128,128]{2,1,0:T(8,128)S(1)} collective-permute-done((f32[2,128,128]{2,1,0:T(8,128)S(1)}, f32[2,128,128]{2,1,0:T(8,128)S(1)}, u32[]{:S(2)}, u32[]{:S(2)}) %collective-permute-start.1) | collective-permute-done | bytes 131104 | tf_op jit(solution)/shard_map/ppermute | solution.py:416
  11.6 3.7 %factors_1.1.refs_0_ = f32[2,128,128]{2,1,0:T(8,128)S(1)} custom-call(s32[3]{0:T(128)S(1)} %pad_add_fusion.flags, f32[2,128,128]{2,1,0:T(8,128)S(1)} %add.14.a_ref, f32[2,128,128]{2,1,0:T(8,128)S(1)} %collective-permute-done.1.b_ref), custom_call_target="tpu_custom_call" | custom-call | flops 10000000000 | bytes 400000000 | tf_op jit(solution)/shard_map/factors_1/pallas_call | solution.py:182
  17.4 4.1 %rotate_1_ends.1 = (f32[64,4096]{1,0:T(8,128)}, f32[64,4096]{1,0:T(8,128)}) custom-call(s32[3]{0:T(128)} %copy-done.5, f32[2,128,128]{2,1,0:T(8,128)} %copy-done.8, f32[2,128,128]{2,1,0:T(8,128)} %copy-done.16, f32[4096,512]{1,0:T(8,128)} %refs_5_.1, f32[4096,512]{1,0:T(8,128)} %refs_5_.1), custom_call_target="tpu_custom_call" | custom-call | flops 10000000000 | bytes 400000000 | tf_op jit(solution)/shard_map/rotate_1_ends/pallas_call | solution.py:224
  21.5 7.2 %collective-permute-start.4 = (f32[64,4096]{1,0:T(8,128)}, f32[64,4096]{1,0:T(8,128)S(1)}, u32[]{:S(2)}, u32[]{:S(2)}) collective-permute-start(f32[64,4096]{1,0:T(8,128)} %get-tuple-element.39.refs_1_), channel_id=1, source_target_pairs={{4,0},{8,4},{12,8},{16,12},{20,16},{24,20},{28,24},{32,28},{36,32}... | collective-permute-start | bytes 3145736 | tf_op jit(solution)/shard_map/ppermute | solution.py:395
  28.7 2.1 %collective-permute-start.3 = (f32[64,4096]{1,0:T(8,128)}, f32[64,4096]{1,0:T(8,128)S(1)}, u32[]{:S(2)}, u32[]{:S(2)}) collective-permute-start(f32[64,4096]{1,0:T(8,128)} %get-tuple-element.40.refs_10_), channel_id=1, source_target_pairs={{0,4},{4,8},{8,12},{12,16},{16,20},{20,24},{24,28},{28,32},{32,36}... | collective-permute-start | bytes 3145736 | tf_op jit(solution)/shard_map/ppermute | solution.py:390
  30.8 7.4 %rotate_1_inner.1 = (f32[64,4096]{1,0:T(8,128)}, f32[64,4096]{1,0:T(8,128)}, f32[64,4096]{1,0:T(8,128)}, f32[64,4096]{1,0:T(8,128)}, f32[64,4096]{1,0:T(8,128)}, /*index=5*/f32[64,4096]{1,0:T(8,128)}) custom-call(s32[3]{0:T(128)} %copy-done.5, f32[2,128,128]{2,1,0:T(8,128)} %copy-done.8, f32[2,128,128]{2,1,0:T(8,128)} %copy-done.16, f32[4096,512]{1,0:T(8,128)} %refs_5_.1, ...), custom_call_target="tpu_custom_call" | custom-call | flops 10000000000 | bytes 400000000 | tf_op jit(solution)/shard_map/rotate_1_inner/pallas_call | solution.py:224
  38.2 4.0 %collective-permute-start.9 = (f32[64,4096]{1,0:T(8,128)}, f32[64,4096]{1,0:T(8,128)}, u32[]{:S(2)}, u32[]{:S(2)}) collective-permute-start(f32[64,4096]{1,0:T(8,128)} %get-tuple-element.46.refs_6_.refs_8_), channel_id=1, source_target_pairs={{0,4},{4,8},{8,12},{12,16},{16,20},{20,24},{24,28},{28,32},{32,36}... | collective-permute-start | bytes 3145736 | tf_op jit(solution)/shard_map/ppermute | solution.py:390
  42.2 10.3 %collective-permute-done.4 = f32[64,4096]{1,0:T(8,128)S(1)} collective-permute-done((f32[64,4096]{1,0:T(8,128)}, f32[64,4096]{1,0:T(8,128)S(1)}, u32[]{:S(2)}, u32[]{:S(2)}) %collective-permute-start.4) | collective-permute-done | bytes 1048608 | tf_op jit(solution)/shard_map/ppermute | solution.py:395
  53.6 22.2 %collective-permute-done.3 = f32[64,4096]{1,0:T(8,128)S(1)} collective-permute-done((f32[64,4096]{1,0:T(8,128)}, f32[64,4096]{1,0:T(8,128)S(1)}, u32[]{:S(2)}, u32[]{:S(2)}) %collective-permute-start.3) | collective-permute-done | bytes 1048608 | tf_op jit(solution)/shard_map/ppermute | solution.py:390
  76.0 5.6 %gram_2.1 = f32[4,128,128]{2,1,0:T(8,128)S(1)} custom-call(f32[64,4096]{1,0:T(8,128)S(1)} %broadcast_select_fusion.1.refs_0_.refs_2_, f32[64,4096]{1,0:T(8,128)} %get-tuple-element.41.refs_1_.refs_0_, f32[64,4096]{1,0:T(8,128)} %get-tuple-element.42.refs_2_.refs_3_.refs_4_, f32[64,4096]{1,0:T(8,128)} %get-tuple-element.43.refs_3_.refs_4_.refs_5_, ...), custom_call_target="tpu_custom_call" | custom-call | flops 10000000000 | bytes 400000000 | tf_op jit(solution)/shard_map/gram_2/pallas_call | solution.py:105
  81.7 1.5 collective-permute-done.5
  83.3 1.6 collective-permute-start.6
  84.8 13.6 %collective-permute-done.9.refs_2_.refs_0_ = f32[64,4096]{1,0:T(8,128)} collective-permute-done((f32[64,4096]{1,0:T(8,128)}, f32[64,4096]{1,0:T(8,128)}, u32[]{:S(2)}, u32[]{:S(2)}) %collective-permute-start.9) | collective-permute-done | bytes 1048608 | tf_op jit(solution)/shard_map/ppermute | solution.py:390
  98.4 5.1 %collective-permute-start.10 = (f32[64,4096]{1,0:T(8,128)}, f32[64,4096]{1,0:T(8,128)S(1)}, u32[]{:S(2)}, u32[]{:S(2)}) collective-permute-start(f32[64,4096]{1,0:T(8,128)} %after.2.refs_3_), channel_id=1, source_target_pairs={{4,0},{8,4},{12,8},{16,12},{20,16},{24,20},{28,24},{32,28},{36,32}... | collective-permute-start | bytes 3145736 | tf_op jit(solution)/shard_map/ppermute | solution.py:395
  104.5 4.5 %factors_2.1 = (f32[4,128,128]{2,1,0:T(8,128)S(1)}, f32[64,128]{1,0:T(8,128)S(1)}, f32[64,128]{1,0:T(8,128)S(1)}) custom-call(s32[3]{0:T(128)S(1)} %copy-done.6, f32[4,128,128]{2,1,0:T(8,128)S(1)} %copy-done.2, f32[4,128,128]{2,1,0:T(8,128)S(1)} %collective-permute-done.6.b_ref), custom_call_target="tpu_custom_call" | custom-call | flops 10000000000 | bytes 400000000 | tf_op jit(solution)/shard_map/factors_2/pallas_call | solution.py:182
  109.7 2.2 %collective-permute-start.7 = (f32[64,128]{1,0:T(8,128)S(1)}, f32[64,128]{1,0:T(8,128)S(1)}, u32[]{:S(2)}, u32[]{:S(2)}) collective-permute-start(f32[64,128]{1,0:T(8,128)S(1)} %get-tuple-element.48), channel_id=1, source_target_pairs={{0,4},{4,8},{8,12},{12,16},{16,20},{20,24},{24,28},{28,32},{32,36}... | collective-permute-start | bytes 98312 | tf_op jit(solution)/shard_map/ppermute | solution.py:390
  112.0 8.1 %collective-permute-start.8 = (f32[64,128]{1,0:T(8,128)S(1)}, f32[64,128]{1,0:T(8,128)S(1)}, u32[]{:S(2)}, u32[]{:S(2)}) collective-permute-start(f32[64,128]{1,0:T(8,128)S(1)} %get-tuple-element.49), channel_id=1, source_target_pairs={{4,0},{8,4},{12,8},{16,12},{20,16},{24,20},{28,24},{32,28},{36,32}... | collective-permute-start | bytes 98312 | tf_op jit(solution)/shard_map/ppermute | solution.py:395
  120.1 3.8 %rotate_2_ends.1 = (f32[64,4096]{1,0:T(8,128)}, f32[64,4096]{1,0:T(8,128)}) custom-call(s32[3]{0:T(128)} %copy-done.5, f32[4,128,128]{2,1,0:T(8,128)} %copy-done.9, f32[64,4096]{1,0:T(8,128)} %get-tuple-element.44.refs_4_.refs_1_.refs_6_, f32[64,4096]{1,0:T(8,128)} %get-tuple-element.45.refs_5_.refs_2_.refs_7_, ...), custom_call_target="tpu_custom_call" | custom-call | flops 10000000000 | bytes 400000000 | tf_op jit(solution)/shard_map/rotate_2_ends/pallas_call | solution.py:224
  123.9 1.9 collective-permute-start.15
  128.6 11.9 %round_2_rest.1 = (f32[64,4096]{1,0:T(8,128)}, f32[64,4096]{1,0:T(8,128)}, f32[64,4096]{1,0:T(8,128)}, f32[64,4096]{1,0:T(8,128)}, f32[64,4096]{1,0:T(8,128)}, /...) custom-call(s32[3]{0:T(128)} %copy-done.5, f32[4,128,128]{2,1,0:T(8,128)} %copy-done.9, ...), custom_call_target="tpu_custom_call" | custom-call | flops 10000000000 | bytes 400000000 | tf_op jit(solution)/shard_map/round_2_rest/pallas_call | solution.py:290
  140.7 1.7 collective-permute-done.11
  143.4 2.5 %collective-permute-start.12 = (f32[4,128,128]{2,1,0:T(8,128)S(1)}, f32[4,128,128]{2,1,0:T(8,128)S(1)}, u32[]{:S(2)}, u32[]{:S(2)}) collective-permute-start(f32[4,128,128]{2,1,0:T(8,128)S(1)} %add.16.a_ref.refs_1_), channel_id=1, source_target_pairs={{0,2},{1,3},{2,0},{3,1},{4,6},{5,7},{6,4},{7,5},{8,10},{9,11},{10,... | collective-permute-start | bytes 786440 | tf_op jit(solution)/shard_map/ppermute | solution.py:416
  145.9 10.5 %collective-permute-done.15.refs_2_.lt = f32[64,4096]{1,0:T(8,128)S(1)} collective-permute-done((f32[64,4096]{1,0:T(8,128)}, f32[64,4096]{1,0:T(8,128)S(1)}, u32[]{:S(2)}, u32[]{:S(2)}) %collective-permute-start.15) | collective-permute-done | bytes 1048608 | tf_op jit(solution)/shard_map/ppermute | solution.py:390
  157.4 1.9 collective-permute-start.16
  160.2 4.5 %factors_3.1 = (f32[4,128,128]{2,1,0:T(8,128)S(1)}, f32[64,128]{1,0:T(8,128)S(1)}, f32[64,128]{1,0:T(8,128)S(1)}) custom-call(s32[3]{0:T(128)S(1)} %copy-done.7, f32[4,128,128]{2,1,0:T(8,128)S(1)} %copy-done.4, f32[4,128,128]{2,1,0:T(8,128)S(1)} %collective-permute-done.12.b_ref), custom_call_target="tpu_custom_call" | custom-call | flops 10000000000 | bytes 400000000 | tf_op jit(solution)/shard_map/factors_3/pallas_call | solution.py:182
  165.5 5.4 %collective-permute-start.13 = (f32[64,128]{1,0:T(8,128)S(1)}, f32[64,128]{1,0:T(8,128)S(1)}, u32[]{:S(2)}, u32[]{:S(2)}) collective-permute-start(f32[64,128]{1,0:T(8,128)S(1)} %get-tuple-element.53), channel_id=1, source_target_pairs={{0,4},{4,8},{8,12},{12,16},{16,20},{20,24},{24,28},{28,32},{32,36}... | collective-permute-start | bytes 98312 | tf_op jit(solution)/shard_map/ppermute | solution.py:390
  170.9 5.1 %collective-permute-start.14 = (f32[64,128]{1,0:T(8,128)S(1)}, f32[64,128]{1,0:T(8,128)S(1)}, u32[]{:S(2)}, u32[]{:S(2)}) collective-permute-start(f32[64,128]{1,0:T(8,128)S(1)} %get-tuple-element.54), channel_id=1, source_target_pairs={{4,0},{8,4},{12,8},{16,12},{20,16},{24,20},{28,24},{32,28},{36,32}... | collective-permute-start | bytes 98312 | tf_op jit(solution)/shard_map/ppermute | solution.py:395
  176.0 8.1 %final_inner.1 = (f32[4096,256]{1,0:T(8,128)}, f32[64,4096]{1,0:T(8,128)}, f32[64,4096]{1,0:T(8,128)}, f32[64,4096]{1,0:T(8,128)}, f32[64,4096]{1,0:T(8,128)}) custom-call(s32[3]{0:T(128)} %copy-done.5, f32[4,128,128]{2,1,0:T(8,128)} %copy-done.10, f32[64,4096]{1,0:T(8,128)} %get-tuple-element.58.refs_0_, f32[64,4096]{1,0:T(8,128)} %after.3.refs_1_, ...), custom_call_target="tpu_custom_call" | custom-call | flops 10000000000 | bytes 400000000 | tf_op jit(solution)/shard_map/final_inner/pallas_call | solution.py:340
  185.2 8.2 %final.1 = f32[4096,512]{1,0:T(8,128)} custom-call(s32[3]{0:T(128)} %copy-done.5, f32[64,128]{1,0:T(8,128)} %copy-done.19, f32[64,128]{1,0:T(8,128)} %copy-done.20, f32[64,4096]{1,0:T(8,128)} %copy-done.13, f32[64,4096]{1,0:T(8,128)} %get-tuple-element.55.lb, f32[64,4096]{1,0:T(8,128)} %get-tuple-element.56.rt, f32[64,4096]{1,0:T(8,128)} %copy-done.15, ...), custom_call_target="tpu_custom_call" | custom-call | flops 10000000000 | bytes 400000000 | tf_op jit(solution)/shard_map/final/pallas_call | solution.py:370
  (63 shorter events, 12.8 us)
Async XLA Ops:
  4.5 1.4 collective-permute-start
  5.9 5.6 %collective-permute-start.1 = (f32[2,128,128]{2,1,0:T(8,128)S(1)}, f32[2,128,128]{2,1,0:T(8,128)S(1)}, u32[]{:S(2)}, u32[]{:S(2)}) collective-permute-start(f32[2,128,128]{2,1,0:T(8,128)S(1)} %add.14.a_ref), channel_id=1, source_target_pairs={{0,2},{1,3},{2,0},{3,1},{4,6},{5,7},{6,4},{7,5},{8,10},{9,11},{10,... | collective-permute-start | bytes 393224 | tf_op jit(solution)/shard_map/ppermute | solution.py:416
  7.6 7.7 %copy-start.5 = (s32[3]{0:T(128)}, s32[3]{0:T(128)S(1)}, u32[]{:S(2)}) copy-start(s32[3]{0:T(128)S(1)} %pad_add_fusion.flags) | copy-start | bytes 40
  15.3 1.4 copy-start.8
  15.3 1.4 collective-permute-start.2
  21.5 31.0 %collective-permute-start.4 = (f32[64,4096]{1,0:T(8,128)}, f32[64,4096]{1,0:T(8,128)S(1)}, u32[]{:S(2)}, u32[]{:S(2)}) collective-permute-start(f32[64,4096]{1,0:T(8,128)} %get-tuple-element.39.refs_1_), channel_id=1, source_target_pairs={{4,0},{8,4},{12,8},{16,12},{20,16},{24,20},{28,24},{32,28},{36,32}... | collective-permute-start | bytes 3145736 | tf_op jit(solution)/shard_map/ppermute | solution.py:395
  28.7 23.8 %copy-start.11 = (f32[64,4096]{1,0:T(8,128)S(1)}, f32[64,4096]{1,0:T(8,128)}, u32[]{:S(2)}) copy-start(f32[64,4096]{1,0:T(8,128)} %get-tuple-element.40.refs_10_) | copy-start | bytes 3145732
  28.7 47.1 %copy-start.12 = (f32[64,4096]{1,0:T(8,128)S(1)}, f32[64,4096]{1,0:T(8,128)}, u32[]{:S(2)}) copy-start(f32[64,4096]{1,0:T(8,128)} %get-tuple-element.39.refs_1_) | copy-start | bytes 3145732
  28.7 47.1 %collective-permute-start.3 = (f32[64,4096]{1,0:T(8,128)}, f32[64,4096]{1,0:T(8,128)S(1)}, u32[]{:S(2)}, u32[]{:S(2)}) collective-permute-start(f32[64,4096]{1,0:T(8,128)} %get-tuple-element.40.refs_10_), channel_id=1, source_target_pairs={{0,4},{4,8},{8,12},{12,16},{16,20},{20,24},{24,28},{28,32},{32,36}... | collective-permute-start | bytes 3145736 | tf_op jit(solution)/shard_map/ppermute | solution.py:390
  38.2 60.3 %collective-permute-start.9 = (f32[64,4096]{1,0:T(8,128)}, f32[64,4096]{1,0:T(8,128)}, u32[]{:S(2)}, u32[]{:S(2)}) collective-permute-start(f32[64,4096]{1,0:T(8,128)} %get-tuple-element.46.refs_6_.refs_8_), channel_id=1, source_target_pairs={{0,4},{4,8},{8,12},{12,16},{16,20},{20,24},{24,28},{28,32},{32,36}... | collective-permute-start | bytes 3145736 | tf_op jit(solution)/shard_map/ppermute | solution.py:390
  76.0 5.6 %copy-start = (f32[64,4096]{1,0:T(8,128)}, f32[64,4096]{1,0:T(8,128)S(1)}, u32[]{:S(2)}) copy-start(f32[64,4096]{1,0:T(8,128)S(1)} %broadcast_select_fusion.1.refs_0_.refs_2_) | copy-start | bytes 3145732
  81.6 1.6 collective-permute-start.5
  83.3 15.2 %copy-start.1 = (f32[4,128,128]{2,1,0:T(8,128)}, f32[4,128,128]{2,1,0:T(8,128)S(1)}, u32[]{:S(2)}) copy-start(f32[4,128,128]{2,1,0:T(8,128)S(1)} %add.15.a_ref.refs_1_) | copy-start | bytes 786436
  83.3 20.3 %copy-start.6 = (s32[3]{0:T(128)S(1)}, s32[3]{0:T(128)}, u32[]{:S(2)}) copy-start(s32[3]{0:T(128)} %copy-done.5) | copy-start | bytes 40
  83.3 20.3 %collective-permute-start.6 = (f32[4,128,128]{2,1,0:T(8,128)S(1)}, f32[4,128,128]{2,1,0:T(8,128)S(1)}, u32[]{:S(2)}, u32[]{:S(2)}) collective-permute-start(f32[4,128,128]{2,1,0:T(8,128)S(1)} %add.15.a_ref.refs_1_), channel_id=1, source_target_pairs={{0,2},{1,3},{2,0},{3,1},{4,6},{5,7},{6,4},{7,5},{8,10},{9,11},{10,... | collective-permute-start | bytes 786440 | tf_op jit(solution)/shard_map/ppermute | solution.py:416
  98.4 29.2 %collective-permute-start.10 = (f32[64,4096]{1,0:T(8,128)}, f32[64,4096]{1,0:T(8,128)S(1)}, u32[]{:S(2)}, u32[]{:S(2)}) collective-permute-start(f32[64,4096]{1,0:T(8,128)} %after.2.refs_3_), channel_id=1, source_target_pairs={{4,0},{8,4},{12,8},{16,12},{20,16},{24,20},{28,24},{32,28},{36,32}... | collective-permute-start | bytes 3145736 | tf_op jit(solution)/shard_map/ppermute | solution.py:395
  103.6 1.0 copy-start.2
  109.7 17.2 %collective-permute-start.7 = (f32[64,128]{1,0:T(8,128)S(1)}, f32[64,128]{1,0:T(8,128)S(1)}, u32[]{:S(2)}, u32[]{:S(2)}) collective-permute-start(f32[64,128]{1,0:T(8,128)S(1)} %get-tuple-element.48), channel_id=1, source_target_pairs={{0,4},{4,8},{8,12},{12,16},{16,20},{20,24},{24,28},{28,32},{32,36}... | collective-permute-start | bytes 98312 | tf_op jit(solution)/shard_map/ppermute | solution.py:390
  112.0 15.7 %collective-permute-start.8 = (f32[64,128]{1,0:T(8,128)S(1)}, f32[64,128]{1,0:T(8,128)S(1)}, u32[]{:S(2)}, u32[]{:S(2)}) collective-permute-start(f32[64,128]{1,0:T(8,128)S(1)} %get-tuple-element.49), channel_id=1, source_target_pairs={{4,0},{8,4},{12,8},{16,12},{20,16},{24,20},{28,24},{32,28},{36,32}... | collective-permute-start | bytes 98312 | tf_op jit(solution)/shard_map/ppermute | solution.py:395
  123.9 32.5 %collective-permute-start.15 = (f32[64,4096]{1,0:T(8,128)}, f32[64,4096]{1,0:T(8,128)S(1)}, u32[]{:S(2)}, u32[]{:S(2)}) collective-permute-start(f32[64,4096]{1,0:T(8,128)} %get-tuple-element.50.refs_12_.refs_6_), channel_id=1, source_target_pairs={{0,4},{4,8},{8,12},{12,16},{16,20},{20,24},{24,28},{28,32},{32,36}... | collective-permute-start | bytes 3145736 | tf_op jit(solution)/shard_map/ppermute | solution.py:390
  126.9 0.7 copy-start.17
  127.7 1.0 copy-start.14
  140.6 1.8 collective-permute-start.11
  143.4 12.9 %copy-start.3 = (f32[4,128,128]{2,1,0:T(8,128)}, f32[4,128,128]{2,1,0:T(8,128)S(1)}, u32[]{:S(2)}) copy-start(f32[4,128,128]{2,1,0:T(8,128)S(1)} %add.16.a_ref.refs_1_) | copy-start | bytes 786436
  143.4 15.9 %copy-start.7 = (s32[3]{0:T(128)S(1)}, s32[3]{0:T(128)}, u32[]{:S(2)}) copy-start(s32[3]{0:T(128)} %copy-done.5) | copy-start | bytes 40
  143.4 15.9 %collective-permute-start.12 = (f32[4,128,128]{2,1,0:T(8,128)S(1)}, f32[4,128,128]{2,1,0:T(8,128)S(1)}, u32[]{:S(2)}, u32[]{:S(2)}) collective-permute-start(f32[4,128,128]{2,1,0:T(8,128)S(1)} %add.16.a_ref.refs_1_), channel_id=1, source_target_pairs={{0,2},{1,3},{2,0},{3,1},{4,6},{5,7},{6,4},{7,5},{8,10},{9,11},{10,... | collective-permute-start | bytes 786440 | tf_op jit(solution)/shard_map/ppermute | solution.py:416
  156.3 1.0 copy-start.13
  157.4 26.8 %collective-permute-start.16 = (f32[64,4096]{1,0:T(8,128)}, f32[64,4096]{1,0:T(8,128)S(1)}, u32[]{:S(2)}, u32[]{:S(2)}) collective-permute-start(f32[64,4096]{1,0:T(8,128)} %after.3.refs_1_), channel_id=1, source_target_pairs={{4,0},{8,4},{12,8},{16,12},{20,16},{24,20},{28,24},{32,28},{36,32}... | collective-permute-start | bytes 3145736 | tf_op jit(solution)/shard_map/ppermute | solution.py:395
  159.3 1.0 copy-start.4
  165.5 18.7 %collective-permute-start.13 = (f32[64,128]{1,0:T(8,128)S(1)}, f32[64,128]{1,0:T(8,128)S(1)}, u32[]{:S(2)}, u32[]{:S(2)}) collective-permute-start(f32[64,128]{1,0:T(8,128)S(1)} %get-tuple-element.53), channel_id=1, source_target_pairs={{0,4},{4,8},{8,12},{12,16},{16,20},{20,24},{24,28},{28,32},{32,36}... | collective-permute-start | bytes 98312 | tf_op jit(solution)/shard_map/ppermute | solution.py:390
  170.9 13.3 %collective-permute-start.14 = (f32[64,128]{1,0:T(8,128)S(1)}, f32[64,128]{1,0:T(8,128)S(1)}, u32[]{:S(2)}, u32[]{:S(2)}) collective-permute-start(f32[64,128]{1,0:T(8,128)S(1)} %get-tuple-element.54), channel_id=1, source_target_pairs={{4,0},{8,4},{12,8},{16,12},{20,16},{24,20},{28,24},{32,28},{36,32}... | collective-permute-start | bytes 98312 | tf_op jit(solution)/shard_map/ppermute | solution.py:395
  184.2 1.0 copy-start.15
  (6 other events, 3.9 us)
